TPU v7x, 32 devices: a whole 2x2x4 slice. The times are simulated.
32 devices in a mesh: dp: 8 (over y, x, core), tensor: 4 (over z).
Axes of the slice: x: 2, y: 2, z: 4, core: 2. Of those that a mesh axis runs over, the one named last changes fastest.
Arguments:
- streams: bfloat16 [8192, 4, 2048], P(('dp', 'tensor')), may hold values from -6 to 6
- cotangent: bfloat16 [8192, 4, 2048], P(('dp', 'tensor')), may hold values from -6 to 6
- lengths: int32 [24], replicated, may hold values from 1 to 1021, as said below
- permutation: int32 [24], replicated, may hold values from 0 to 23, as said below
- query_weight: bfloat16 [2048, 2048], P('dp', 'tensor'), may hold values from -0.125 to 0.125
- key_weight: bfloat16 [2048, 2048], P('dp', 'tensor'), may hold values from -0.125 to 0.125
- value_weight: bfloat16 [2048, 2048], P('dp', 'tensor'), may hold values from -0.125 to 0.125
- out_weight: bfloat16 [2048, 2048], P('dp', 'tensor'), may hold values from -3 to 3
- gate_weight: bfloat16 [2048, 8192], P('dp', 'tensor'), may hold values from -0.125 to 0.125
- up_weight: bfloat16 [2048, 8192], P('dp', 'tensor'), may hold values from -0.125 to 0.125
- down_weight: bfloat16 [2048, 8192], P('dp', 'tensor'), may hold values from -0.0625 to 0.0625
- mix_static: float32 [2, 4, 6], replicated, may hold values from -1 to 1
- mix_weight: float32 [2, 2048, 6], replicated, may hold values from -0.125 to 0.125
- mix_scale: float32 [2, 6], replicated, may hold values from 0.3 to 1
Outputs:
- out_streams: bfloat16 [8192, 4, 2048], P(('dp', 'tensor'))
- stream_grads: bfloat16 [8192, 4, 2048], P(('dp', 'tensor'))
- query_weight_grad: float32 [2048, 2048], P(None, 'tensor')
- key_weight_grad: float32 [2048, 2048], P(None, 'tensor')
- value_weight_grad: float32 [2048, 2048], P(None, 'tensor')
- out_weight_grad: float32 [2048, 2048], P(None, 'tensor')
- gate_weight_grad: float32 [2048, 8192], P(None, 'tensor')
- up_weight_grad: float32 [2048, 8192], P(None, 'tensor')
- down_weight_grad: float32 [2048, 8192], P(None, 'tensor')
- mix_static_grad: float32 [2, 4, 6], replicated
- mix_weight_grad: float32 [2, 2048, 6], replicated
- mix_scale_grad: float32 [2, 6], replicated
Inputs may be any that keep to these rules, and one draw needn't show every extreme that they name: The lengths of the 3 sequences that the permutation deals to one data group add up to 1023 or less. `permutation`: each number appears once.
All inputs are finite; a program needn't handle non-finite values.
Results may differ from a plain program's by a relative error of at most 0.014.
The roundings to bfloat16 on the way count: a program that leaves them out, or rounds other values in their place, can miss the bound.
Values may be sent and summed in bfloat16 or wider, within the bound.
A program may use at most 384 MiB of HBM per device.

v0:
```python
import jax
import jax.numpy as jnp
from jax import lax
from jax.sharding import PartitionSpec as P

HEAD_DIM = 128


EPSILON = 1e-05
THETA = 10000.0
HIGHEST = lax.Precision.HIGHEST
MASKED = -1e30


def matmul(left, right):
    return jnp.dot(left, right, preferred_element_type=jnp.float32)


def times_transposed(left, right):
    return lax.dot_general(
        left, right, (((1,), (1,)), ((), ())), preferred_element_type=jnp.float32
    )


def transposed_times(left, right):
    return lax.dot_general(
        left, right, (((0,), (0,)), ((), ())), preferred_element_type=jnp.float32
    )


def layer_norm(values):
    centre = values - jnp.mean(values, axis=-1, keepdims=True)
    spread = jnp.mean(centre * centre, axis=-1, keepdims=True)
    return centre * lax.rsqrt(spread + EPSILON)


def mix_streams(streams, static, mix_weight, mix_scale):
    stream_count = static.shape[0]
    normed = layer_norm(streams)
    dynamic = jnp.tanh(jnp.einsum("rjd,dc->rjc", normed, mix_weight, precision=HIGHEST))
    coeffs = static[None] + mix_scale[None, None, :] * dynamic
    entering = jnp.einsum("rj,rjd->rd", coeffs[:, :, 0], streams, precision=HIGHEST)
    carried = jnp.einsum(
        "rji,rjd->rid", coeffs[:, :, 1 : stream_count + 1], streams, precision=HIGHEST
    )
    return (layer_norm(entering), carried, coeffs[:, :, stream_count + 1])


def rope_tables(position, head_dim):
    halfway = head_dim // 2
    frequency = THETA ** (-(2.0 * jnp.arange(halfway, dtype=jnp.float32)) / head_dim)
    angles = position.astype(jnp.float32)[:, None] * frequency[None, :]
    angles = jnp.concatenate([angles, angles], axis=1)
    return (jnp.cos(angles), jnp.sin(angles))


def rotate(heads_in, cosine_table, sine_table):
    halfway = heads_in.shape[-1] // 2
    turned = jnp.concatenate([-heads_in[..., halfway:], heads_in[..., :halfway]], axis=-1)
    return heads_in * cosine_table[:, None, :] + turned * sine_table[:, None, :]


def rotate_back(gradient, cosine_table, sine_table):
    halfway = gradient.shape[-1] // 2
    scaled = gradient * sine_table[:, None, :]
    turned = jnp.concatenate([scaled[..., halfway:], -scaled[..., :halfway]], axis=-1)
    return gradient * cosine_table[:, None, :] + turned


def segments_from(slot_lengths, group_rows):
    bounds = jnp.cumsum(slot_lengths)
    row_ids = jnp.arange(group_rows, dtype=jnp.int32)
    segment = jnp.sum((row_ids[:, None] >= bounds[None, :]).astype(jnp.int32), axis=1)
    starting = jnp.concatenate([jnp.zeros((1,), jnp.int32), bounds])
    labels = jnp.arange(starting.shape[0], dtype=jnp.int32)
    begins = jnp.sum(jnp.where(segment[:, None] == labels[None, :], starting[None, :], 0), axis=1)
    return (segment, row_ids - begins)


def group_layout(lengths, permutation, group_rows, seq_count):
    group_index = lax.axis_index("dp")
    chosen = lax.dynamic_slice_in_dim(permutation, group_index * seq_count, seq_count)
    matches = chosen[:, None] == jnp.arange(permutation.shape[0], dtype=jnp.int32)[None, :]
    slot_lengths = jnp.sum(jnp.where(matches, lengths[None, :], 0), axis=1)
    return segments_from(slot_lengths, group_rows)


def block_mask(segment, first_row, block_rows):
    row_ids = jnp.arange(segment.shape[0], dtype=jnp.int32)
    block_segment = lax.dynamic_slice_in_dim(segment, first_row, block_rows)
    block_ids = first_row + jnp.arange(block_rows, dtype=jnp.int32)
    return (block_segment[:, None] == segment[None, :]) & (row_ids[None, :] <= block_ids[:, None])


def attend(query_heads, key_heads, value_heads, segment):
    group_rows, heads_here, head_dim = query_heads.shape
    block_rows = min(512, group_rows)
    score_scale = head_dim ** (-0.5)

    def one_block(block_index):
        first_row = block_index * block_rows
        query_block = lax.dynamic_slice_in_dim(query_heads, first_row, block_rows, 0)
        allowed = block_mask(segment, first_row, block_rows)
        scores = (
            jnp.einsum("qhd,khd->hqk", query_block, key_heads, preferred_element_type=jnp.float32)
            * score_scale
        )
        scores = jnp.where(allowed[None], scores, MASKED)
        highest = jnp.max(scores, axis=-1, keepdims=True)
        exponent = jnp.exp(scores - highest)
        row_total = jnp.sum(exponent, axis=-1, keepdims=True)
        probabilities = (exponent / row_total).astype(jnp.bfloat16)
        attended = jnp.einsum(
            "hqk,khd->qhd", probabilities, value_heads, preferred_element_type=jnp.float32
        ).astype(jnp.bfloat16)
        return (attended, (highest + jnp.log(row_total))[:, :, 0])

    attended, log_totals = lax.map(one_block, jnp.arange(group_rows // block_rows, dtype=jnp.int32))
    return (attended.reshape(group_rows, heads_here, head_dim), log_totals)


def attend_back(query_heads, key_heads, value_heads, attended_grad, log_totals, segment):
    group_rows, heads_here, head_dim = query_heads.shape
    block_rows = min(512, group_rows)
    score_scale = head_dim ** (-0.5)

    def one_block(accumulated, block_index):
        key_total, value_total = accumulated
        first_row = block_index * block_rows
        query_block = lax.dynamic_slice_in_dim(query_heads, first_row, block_rows, 0)
        grad_block = lax.dynamic_slice_in_dim(attended_grad, first_row, block_rows, 0)
        allowed = block_mask(segment, first_row, block_rows)
        scores = (
            jnp.einsum("qhd,khd->hqk", query_block, key_heads, preferred_element_type=jnp.float32)
            * score_scale
        )
        scores = jnp.where(allowed[None], scores, MASKED)
        probabilities = jnp.where(
            allowed[None], jnp.exp(scores - log_totals[block_index][:, :, None]), 0.0
        )
        probs_low = probabilities.astype(jnp.bfloat16)
        prob_grad = jnp.einsum(
            "qhd,khd->hqk", grad_block, value_heads, preferred_element_type=jnp.float32
        )
        centre = jnp.sum(probabilities * prob_grad, axis=-1, keepdims=True)
        score_grad = (probabilities * (prob_grad - centre)).astype(jnp.bfloat16)
        query_part = (
            jnp.einsum("hqk,khd->qhd", score_grad, key_heads, preferred_element_type=jnp.float32)
            * score_scale
        )
        key_total = (
            key_total
            + jnp.einsum(
                "hqk,qhd->khd", score_grad, query_block, preferred_element_type=jnp.float32
            )
            * score_scale
        )
        value_total = value_total + jnp.einsum(
            "hqk,qhd->khd", probs_low, grad_block, preferred_element_type=jnp.float32
        )
        return ((key_total, value_total), query_part)

    empty_grad = jnp.zeros(key_heads.shape, jnp.float32)
    totals, query_parts = lax.scan(
        one_block, (empty_grad, empty_grad), jnp.arange(group_rows // block_rows, dtype=jnp.int32)
    )
    return (query_parts.reshape(group_rows, heads_here, head_dim), totals[0], totals[1])


def forward_pass(inputs, weights, mixing, segment, cosine_table, sine_table):
    query_full, key_full, value_full, out_full, gate_full, up_full, down_full = weights
    mix_static, mix_weight, mix_scale = mixing
    head_dim = cosine_table.shape[1]
    heads_here = query_full.shape[1] // head_dim
    (normed_attention, carried_attention, branch_attention), pull_attention = jax.vjp(
        mix_streams, inputs, mix_static[0], mix_weight[0], mix_scale[0]
    )
    attention_input = lax.all_gather(
        normed_attention.astype(jnp.bfloat16), "tensor", axis=0, tiled=True
    )
    group_rows = attention_input.shape[0]
    query_heads = rotate(
        matmul(attention_input, query_full).reshape(group_rows, heads_here, head_dim),
        cosine_table,
        sine_table,
    ).astype(jnp.bfloat16)
    key_heads = rotate(
        matmul(attention_input, key_full).reshape(group_rows, heads_here, head_dim),
        cosine_table,
        sine_table,
    ).astype(jnp.bfloat16)
    value_heads = (
        matmul(attention_input, value_full)
        .astype(jnp.bfloat16)
        .reshape(group_rows, heads_here, head_dim)
    )
    attended, log_totals = attend(query_heads, key_heads, value_heads, segment)
    attended_flat = attended.reshape(group_rows, heads_here * head_dim)
    attention_output = lax.psum_scatter(
        times_transposed(attended_flat, out_full), "tensor", scatter_dimension=0, tiled=True
    )
    middle = carried_attention + branch_attention[:, :, None] * attention_output[:, None, :]
    (normed_feedforward, carried_feedforward, branch_feedforward), pull_feedforward = jax.vjp(
        mix_streams, middle, mix_static[1], mix_weight[1], mix_scale[1]
    )
    feedforward_input = lax.all_gather(
        normed_feedforward.astype(jnp.bfloat16), "tensor", axis=0, tiled=True
    )
    gate_value = matmul(feedforward_input, gate_full)
    up_value = matmul(feedforward_input, up_full)
    hidden = (gate_value / (1.0 + jnp.exp(-gate_value)) * up_value).astype(jnp.bfloat16)
    feedforward_output = lax.psum_scatter(
        times_transposed(hidden, down_full), "tensor", scatter_dimension=0, tiled=True
    )
    final_streams = (
        carried_feedforward + branch_feedforward[:, :, None] * feedforward_output[:, None, :]
    )
    return dict(
        attention_input=attention_input,
        query_heads=query_heads,
        key_heads=key_heads,
        value_heads=value_heads,
        attended_flat=attended_flat,
        log_totals=log_totals,
        attention_output=attention_output,
        branch_attention=branch_attention,
        pull_attention=pull_attention,
        feedforward_input=feedforward_input,
        gate_value=gate_value,
        up_value=up_value,
        hidden=hidden,
        feedforward_output=feedforward_output,
        branch_feedforward=branch_feedforward,
        pull_feedforward=pull_feedforward,
        final_streams=final_streams,
    )


def per_device(
    streams,
    cotangent,
    lengths,
    permutation,
    query_weight,
    key_weight,
    value_weight,
    out_weight,
    gate_weight,
    up_weight,
    down_weight,
    mix_static,
    mix_weight,
    mix_scale,
):
    weights = (
        lax.all_gather(query_weight, "dp", axis=0, tiled=True),
        lax.all_gather(key_weight, "dp", axis=0, tiled=True),
        lax.all_gather(value_weight, "dp", axis=0, tiled=True),
        lax.all_gather(out_weight, "dp", axis=0, tiled=True),
        lax.all_gather(gate_weight, "dp", axis=0, tiled=True),
        lax.all_gather(up_weight, "dp", axis=0, tiled=True),
        lax.all_gather(down_weight, "dp", axis=0, tiled=True),
    )
    query_full, key_full, value_full, out_full, gate_full, up_full, down_full = weights
    local_rows = streams.shape[0]
    group_rows = local_rows * lax.axis_size("tensor")
    seq_count = permutation.shape[0] // lax.axis_size("dp")
    segment, position = group_layout(lengths, permutation, group_rows, seq_count)
    cosine_table, sine_table = rope_tables(position, HEAD_DIM)
    head_dim = cosine_table.shape[1]
    heads_here = query_full.shape[1] // head_dim
    mixing = (mix_static, mix_weight, mix_scale)
    inputs = streams.astype(jnp.float32)
    kept_values = forward_pass(inputs, weights, mixing, segment, cosine_table, sine_table)
    out_streams = kept_values["final_streams"].astype(jnp.bfloat16)
    barrier = lax.optimization_barrier((inputs, cotangent))
    kept_values = forward_pass(barrier[0], weights, mixing, segment, cosine_table, sine_table)
    local_segment = lax.dynamic_slice_in_dim(
        segment, lax.axis_index("tensor") * local_rows, local_rows
    )
    valid_rows = (local_segment < seq_count).astype(jnp.float32)
    grad_final = cotangent.astype(jnp.float32) * valid_rows[:, None, None]
    feedforward_branch_grad = jnp.sum(
        grad_final * kept_values["feedforward_output"][:, None, :], axis=2
    )
    feedforward_output_grad = jnp.sum(
        kept_values["branch_feedforward"][:, :, None] * grad_final, axis=1
    ).astype(jnp.bfloat16)
    feedforward_grad_rows = lax.all_gather(feedforward_output_grad, "tensor", axis=0, tiled=True)
    hidden_grad = matmul(feedforward_grad_rows, down_full)
    down_weight_grad = transposed_times(feedforward_grad_rows, kept_values["hidden"])
    gate_value = kept_values["gate_value"]
    sigmoid = 1.0 / (1.0 + jnp.exp(-gate_value))
    gate_grad = (
        hidden_grad * kept_values["up_value"] * (sigmoid + gate_value * sigmoid * (1.0 - sigmoid))
    ).astype(jnp.bfloat16)
    up_grad = (hidden_grad * gate_value * sigmoid).astype(jnp.bfloat16)
    gate_weight_grad = transposed_times(kept_values["feedforward_input"], gate_grad)
    up_weight_grad = transposed_times(kept_values["feedforward_input"], up_grad)
    gate_rows = lax.slice_in_dim(gate_grad, 0, lax.axis_size("tensor") * local_rows, axis=0)
    up_rows = lax.slice_in_dim(up_grad, 0, lax.axis_size("tensor") * local_rows, axis=0)
    feedforward_normed_grad = lax.psum_scatter(
        times_transposed(gate_rows, gate_full) + times_transposed(up_rows, up_full),
        "tensor",
        scatter_dimension=0,
        tiled=True,
    )
    middle_grad, static_feedforward, weight_feedforward, scale_feedforward = kept_values[
        "pull_feedforward"
    ]((feedforward_normed_grad, grad_final, feedforward_branch_grad))
    attention_branch_grad = jnp.sum(
        middle_grad * kept_values["attention_output"][:, None, :], axis=2
    )
    attention_output_grad = jnp.sum(
        kept_values["branch_attention"][:, :, None] * middle_grad, axis=1
    ).astype(jnp.bfloat16)
    attention_grad_rows = lax.all_gather(attention_output_grad, "tensor", axis=0, tiled=True)
    attended_grad = (
        matmul(attention_grad_rows, out_full)
        .astype(jnp.bfloat16)
        .reshape(group_rows, heads_here, head_dim)
    )
    out_weight_grad = transposed_times(attention_grad_rows, kept_values["attended_flat"])
    query_grad, key_grad, value_grad = attend_back(
        kept_values["query_heads"],
        kept_values["key_heads"],
        kept_values["value_heads"],
        attended_grad,
        kept_values["log_totals"],
        segment,
    )
    query_pre = (
        rotate_back(query_grad, cosine_table, sine_table)
        .reshape(group_rows, heads_here * head_dim)
        .astype(jnp.bfloat16)
    )
    key_pre = (
        rotate_back(key_grad, cosine_table, sine_table)
        .reshape(group_rows, heads_here * head_dim)
        .astype(jnp.bfloat16)
    )
    value_pre = value_grad.reshape(group_rows, heads_here * head_dim).astype(jnp.bfloat16)
    query_weight_grad = transposed_times(kept_values["attention_input"], query_pre)
    key_weight_grad = transposed_times(kept_values["attention_input"], key_pre)
    value_weight_grad = transposed_times(kept_values["attention_input"], value_pre)
    attention_normed_grad = lax.psum_scatter(
        times_transposed(query_pre, query_full)
        + times_transposed(key_pre, key_full)
        + times_transposed(value_pre, value_full),
        "tensor",
        scatter_dimension=0,
        tiled=True,
    )
    input_grad, static_attention, weight_attention, scale_attention = kept_values["pull_attention"](
        (attention_normed_grad, middle_grad, attention_branch_grad)
    )
    (
        query_weight_grad,
        key_weight_grad,
        value_weight_grad,
        out_weight_grad,
        gate_weight_grad,
        up_weight_grad,
        down_weight_grad,
    ) = lax.psum(
        (
            query_weight_grad,
            key_weight_grad,
            value_weight_grad,
            out_weight_grad,
            gate_weight_grad,
            up_weight_grad,
            down_weight_grad,
        ),
        "dp",
    )
    static_grad = jnp.stack([static_attention, static_feedforward])
    weight_mix_grad = jnp.stack([weight_attention, weight_feedforward])
    scale_grad = jnp.stack([scale_attention, scale_feedforward])
    static_grad, weight_mix_grad, scale_grad = lax.psum(
        (static_grad, weight_mix_grad, scale_grad), ("dp", "tensor")
    )
    return (
        out_streams,
        input_grad.astype(jnp.bfloat16),
        query_weight_grad,
        key_weight_grad,
        value_weight_grad,
        out_weight_grad,
        gate_weight_grad,
        up_weight_grad,
        down_weight_grad,
        static_grad,
        weight_mix_grad,
        scale_grad,
    )


def solution(mesh):
    placed = (
        P(("dp", "tensor"), None, None),
        P(("dp", "tensor"), None, None),
        P(),
        P(),
        P("dp", "tensor"),
        P("dp", "tensor"),
        P("dp", "tensor"),
        P("dp", "tensor"),
        P("dp", "tensor"),
        P("dp", "tensor"),
        P("dp", "tensor"),
        P(),
        P(),
        P(),
    )
    return jax.shard_map(
        per_device,
        mesh=mesh,
        in_specs=placed,
        out_specs=(
            P(("dp", "tensor"), None, None),
            P(("dp", "tensor"), None, None),
            P(None, "tensor"),
            P(None, "tensor"),
            P(None, "tensor"),
            P(None, "tensor"),
            P(None, "tensor"),
            P(None, "tensor"),
            P(None, "tensor"),
            P(),
            P(),
            P(),
        ),
        check_vma=False,
    )
```

profile of v0, /device:TPU:0, one launch (start us, length us, event | category | flops | bytes accessed | tf_op | source)
XLA Modules:
  0.0 2762.1 jit_solution(13410584705428408640)
XLA Ops:
  96.0 17.4 fusion.158
  143.0 19.8 all-gather.18.cloned.1.call-done
  192.4 82.8 %all-gather.32.cloned.1.call-done = bf16[1024,2048]{1,0:T(8,128)(2,1)} async-done(((bf16[256,2048]{1,0:T(8,128)(2,1)}), bf16[1024,2048]{1,0:T(8,128)(2,1)}) %all-gather.32.cloned.1.call-update) | async-done | bytes 4194320 | tf_op jit(solution)/shard_map/all_gather | solution.py:178
  315.8 21.5 while.38
  347.5 141.7 %reduce-scatter.11.cloned.1.call-done = f32[256,2048]{1,0:T(8,128)} async-done(((f32[1024,2048]{1,0:T(8,128)}), f32[256,2048]{1,0:T(8,128)}) %reduce-scatter.11.cloned.1.call-update) | async-done | bytes 2097168 | tf_op jit(solution)/shard_map/reduce_scatter | solution.py:199
  489.2 22.3 fusion.152
  543.9 17.9 fusion.161
  566.8 80.2 %all-gather.36.cloned.1.call-done = bf16[1024,2048]{1,0:T(8,128)(2,1)} async-done(((bf16[256,2048]{1,0:T(8,128)(2,1)}), bf16[1024,2048]{1,0:T(8,128)(2,1)}) %all-gather.36.cloned.1.call-update) | async-done | bytes 4194320 | tf_op jit(solution)/shard_map/all_gather | solution.py:206
  661.5 40.2 %all-gather.28.cloned.1.call-done = bf16[2048,2048]{1,0:T(8,128)(2,1)} async-done(((bf16[256,2048]{1,0:T(8,128)(2,1)}), bf16[2048,2048]{1,0:T(8,128)(2,1)}) %all-gather.28.cloned.1.call-update) | async-done | bytes 8388624 | tf_op jit(solution)/shard_map/all_gather | solution.py:261
  701.7 16.9 multiply_convert_fusion.1
  718.6 39.4 %all-gather.30.cloned.1.call-done = bf16[2048,2048]{1,0:T(8,128)(2,1)} async-done(((bf16[256,2048]{1,0:T(8,128)(2,1)}), bf16[2048,2048]{1,0:T(8,128)(2,1)}) %all-gather.30.cloned.1.call-update) | async-done | bytes 8388624 | tf_op jit(solution)/shard_map/all_gather | solution.py:262
  772.9 144.4 %reduce-scatter.15.cloned.1.call-done = f32[256,2048]{1,0:T(8,128)} async-done(((f32[1024,2048]{1,0:T(8,128)}), f32[256,2048]{1,0:T(8,128)}) %reduce-scatter.15.cloned.1.call-update) | async-done | bytes 2097168 | tf_op jit(solution)/shard_map/reduce_scatter | solution.py:212
  928.8 81.6 %all-gather.34.cloned.1.call-done = bf16[1024,2048]{1,0:T(8,128)(2,1)} async-done(((bf16[256,2048]{1,0:T(8,128)(2,1)}), bf16[1024,2048]{1,0:T(8,128)(2,1)}) %all-gather.34.cloned.1.call-update) | async-done | bytes 4194320 | tf_op jit(solution)/shard_map/all_gather | solution.py:289
  1010.4 18.2 multiply_convert_fusion.2
  1063.7 30.0 %while.37 = (s32[]{:T(128)}, bf16[2,512,4,128]{3,2,1,0:T(4,128)(2,1)S(1)}, s32[2]{0:T(128)S(1)}, s32[1024]{0:T(1024)S(1)}, bf16[1024,4,128]{2,0,1:T(8,128)(2,1)}...) while((s32[]{:T(128)}, ...), condition=%wide.region_11.12_spmd, body=%wide.region_8.11_spmd.sunk | while | flops 1088161280 | bytes 22051008 | solution.py:118
  1101.8 36.4 %fusion.56 = f32[256,4,4]{2,1,0:T(4,128)S(1)} fusion(f32[256,4,2048]{2,1,0:T(4,128)} %copy-done, bf16[256,4,2048]{2,1,0:T(4,128)(2,1)} %param.21, f32[256]{0:T(256)S(1)} %compare_convert_fusion), kind=kOutput, calls=%fused_computation.85 | convolution fusion | flops 104857600 | bytes 12600320 | tf_op jit(solution)/shard_map/transpose(jvp(rji,rjd->rid))/dot_general | solution.py:43
  1138.8 61.0 %reduce-scatter.13.cloned.1.call-done = f32[256,2048]{1,0:T(8,128)} async-done(((f32[1024,2048]{1,0:T(8,128)}), f32[256,2048]{1,0:T(8,128)}) %reduce-scatter.13.cloned.1.call-update) | async-done | bytes 2097168 | tf_op jit(solution)/shard_map/reduce_scatter | solution.py:302
  1204.8 35.1 %fusion.89 = f32[256,1,4]{2,1,0:T(1,128)S(1)} fusion(f32[256,4,2048]{2,1,0:T(4,128)} %copy-done, f32[256,2048,1]{1,0,2:T(8,128)S(1)} %fusion.259), kind=kOutput, calls=%fused_computation.152 | convolution fusion | flops 25165824 | bytes 10489856 | tf_op jit(solution)/shard_map/transpose(jvp(rj,rjd->rd))/dot_general | solution.py:42
  1273.0 34.2 %multiply_reduce_fusion.2 = (f32[256,4]{1,0:T(8,128)}, bf16[256,2048]{1,0:T(8,128)(2,1)}, f32[256,4,2048]{2,1,0:T(4,128)}) fusion(f32[256,2048]{1,0:T(8,128)S(1)} %copy-done.41, f32[256,4]{1,0:T(8,128)S(1)} %bitcast.308, f32[256,4]{1,0:T(8,128)S(1)} %negate_multiply_fusion.1, f32[256,4]{1,0:T(8,128)S(1)} %copy.400, f32[256,4,2048]{2,1,0:T(4,128)} %copy-done, ...), kind=kOutput, calls=%fused_computation.72 | convolution fusion | flops 131595264 | bytes 34649088 | tf_op jit(solution)/shard_map/transpose(jvp(rji,rjd->rid))/dot_general | solution.py:43
  1307.8 40.0 %reduce-scatter.7.cloned.1.call-done = f32[256,2048]{1,0:T(8,128)} async-done(((f32[1024,2048]{1,0:T(8,128)}), f32[256,2048]{1,0:T(8,128)}) %reduce-scatter.7.cloned.1.call-update) | async-done | bytes 2097168 | tf_op jit(solution)/shard_map/reduce_scatter | solution.py:199
  1386.4 17.5 fusion.156
  1407.0 24.3 all-gather.38.cloned.1.call-done
  1437.5 37.5 %while.39 = (s32[]{:T(128)}, f32[1024,4,128]{0,2,1:T(8,128)S(1)}, f32[1024,4,128]{0,2,1:T(8,128)}, f32[2,512,4,128]{3,1,2,0:T(8,128)}, s32[2]{0:T(128)S(1)}, /*i...) while((s32[]{:T(128)}, f32[1024,4,128]{0,2,1:T(8,128)S(1)}, ...), condition=%wide.region_42.43_spmd.clone, body=%wide.region_40.42_spmd.clone.sunk | while | flops 2709780992 | bytes 124836336 | solution.py:164
  1527.3 27.3 fusion.66
  1594.1 18.1 fusion.167
  1638.7 19.1 reduce-scatter.17.cloned.1.call-done
  1662.8 34.9 %fusion.87 = f32[256,1,4]{2,1,0:T(1,128)S(1)} fusion(f32[256,4,2048]{2,1,0:T(4,128)} %convert_element_type.115, f32[256,2048,1]{1,0,2:T(8,128)S(1)} %fusion.258), kind=kOutput, calls=%fused_computation.150 | convolution fusion | flops 25165824 | bytes 10489856 | tf_op jit(solution)/shard_map/transpose(jvp(rj,rjd->rd))/dot_general | solution.py:42
  1718.8 86.6 %reduce-scatter.9.cloned.1.call-done = f32[256,2048]{1,0:T(8,128)} async-done(((f32[1024,2048]{1,0:T(8,128)}), f32[256,2048]{1,0:T(8,128)}) %reduce-scatter.9.cloned.1.call-update) | async-done | bytes 2097168 | tf_op jit(solution)/shard_map/reduce_scatter | solution.py:212
  1805.4 20.3 add_convert_fusion.1
  1844.0 41.3 %all-reduce.6 = (f32[2,4,6]{2,1,0:T(4,128)}, f32[2,6]{1,0:T(2,128)}) all-reduce(f32[2,4,6]{2,1,0:T(4,128)S(1)} %pad_maximum_fusion.2, f32[2,6]{1,0:T(2,128)S(1)} %pad_maximum_fusion.3), channel_id=1, replica_groups=mesh['dp'=8,'tensor'=4] {'dp','tensor'}, use_global_device_ids=true, to_apply=%region_58.59 | all-reduce | flops 60 | bytes 480 | tf_op jit(solution)/shard_map/psum | solution.py:380
  1898.1 29.0 %add_convert_fusion = bf16[256,4,2048]{2,1,0:T(4,128)(2,1)} fusion(f32[256,4,4]{2,1,0:T(4,128)S(1)} %copy-done.49, f32[256,4,2048]{2,1,0:T(4,128)} %get-tuple-element.586, f32[256,4]{1,0:T(8,128)S(1)} %negate_multiply_fusion, f32[256,2048]{1,0:T(8,128)S(1)} %broadcast_add_fusion, f32[256,4]{1,0:T(8,128)S(1)} %bitcast.303, f32[256,4]{1,0:T(8,128)S(1)} %copy.419, ...), kind=kOutput, calls=%fused_computation.70 | convolution fusion | flops 121634816 | bytes 31494144 | tf_op jit(solution)/shard_map/transpose(jvp(rji,rjd->rid))/dot_general | solution.py:43
  1935.7 771.6 %all-reduce.13.cloned.1.call-done = (f32[2048,512]{1,0:T(8,128)}, f32[2048,512]{1,0:T(8,128)}, f32[2048,512]{1,0:T(8,128)}, f32[2048,512]{1,0:T(8,128)}, f32[204...) async-done(((f32[2048,512]{1,0:T(8,128)}, f32[2048,512]{1,0:T(8,128)}, f32[2048,512]{1,0:T(8,128)}, f32[2048,512]{1,0:T(8,128)}, f32[2048,2048]{1,0:T(8,128)}, ...) | async-done | bytes 67108880 | tf_op jit(solution)/shard_map/psum | solution.py:365
  (596 shorter events, 717.6 us)
Async XLA Ops:
  7.2 115.1 %all-gather.16.cloned.1.call-start = ((), (), s32[]{:S(2)}) async-start(), calls=%async_computation.7 | async-start | bytes 2359296 | tf_op jit(solution)/shard_map/all_gather | solution.py:256
  7.9 126.5 %all-gather.14.cloned.1.call-start = ((), (), s32[]{:S(2)}) async-start(), calls=%async_computation.6 | async-start | bytes 5242880 | tf_op jit(solution)/shard_map/all_gather | solution.py:178
  9.4 70.1 %copy-start.108 = (f32[6]{0:T(128)}, f32[6]{0:T(128)S(1)}, u32[]{:S(2)}) copy-start(f32[6]{0:T(128)S(1)} %get-tuple-element.575) | copy-start | bytes 76
  18.2 61.3 %copy-start.56 = (f32[1,2048,6]{1,0,2:T(1,128)}, f32[1,2048,6]{1,0,2:T(1,128)S(1)}, u32[]{:S(2)}) copy-start(f32[1,2048,6]{1,0,2:T(1,128)S(1)} %get-tuple-element.563) | copy-start | bytes 147460
  50.8 111.9 %all-gather.18.cloned.1.call-start = ((), (), s32[]{:S(2)}) async-start(), calls=%async_computation.8 | async-start | bytes 2359296 | tf_op jit(solution)/shard_map/all_gather | solution.py:257
  51.6 140.9 %all-gather.20.cloned.1.call-start = ((), (), s32[]{:S(2)}) async-start(), calls=%async_computation.9 | async-start | bytes 2359296 | tf_op jit(solution)/shard_map/all_gather | solution.py:258
  52.1 223.1 %all-gather.32.cloned.1.call-start = ((), (), s32[]{:S(2)}) async-start(), calls=%async_computation.17 | async-start | bytes 5242880 | tf_op jit(solution)/shard_map/all_gather | solution.py:178
  117.6 219.8 %all-gather.22.cloned.1.call-start = ((), (), s32[]{:S(2)}) async-start(), calls=%async_computation.10 | async-start | bytes 2359296 | tf_op jit(solution)/shard_map/all_gather | solution.py:259
  118.2 371.0 %reduce-scatter.11.cloned.1.call-start = ((), (), s32[]{:S(2)}) async-start(), calls=%async_computation.18 | async-start | bytes 10485760 | tf_op jit(solution)/shard_map/reduce_scatter | solution.py:199
  346.2 220.6 %all-gather.26.cloned.1.call-start = ((), (), s32[]{:S(2)}) async-start(), calls=%async_computation.13 | async-start | bytes 9437184 | tf_op jit(solution)/shard_map/all_gather | solution.py:260
  347.0 300.0 %all-gather.36.cloned.1.call-start = ((), (), s32[]{:S(2)}) async-start(), calls=%async_computation.20 | async-start | bytes 5242880 | tf_op jit(solution)/shard_map/all_gather | solution.py:206
  347.2 164.3 %copy-start.74 = (f32[256,4,1]{1,0,2:T(8,128)}, f32[256,4,1]{1,0,2:T(8,128)S(1)}, u32[]{:S(2)}) copy-start(f32[256,4,1]{1,0,2:T(8,128)S(1)} %copy.443) | copy-start | bytes 12292
  347.5 164.0 %copy-start.48 = (f32[256,4,4]{2,1,0:T(4,128)}, f32[256,4,4]{2,1,0:T(4,128)S(1)}, u32[]{:S(2)}) copy-start(f32[256,4,4]{2,1,0:T(4,128)S(1)} %copy.403) | copy-start | bytes 49156
  563.7 97.7 %copy-start.122 = (f32[256]{0:T(256)}, f32[256]{0:T(256)S(1)}, u32[]{:S(2)}) copy-start(f32[256]{0:T(256)S(1)} %fusion.133) | copy-start | bytes 3076
  565.4 136.2 %all-gather.28.cloned.1.call-start = ((), (), s32[]{:S(2)}) async-start(), calls=%async_computation.14 | async-start | bytes 9437184 | tf_op jit(solution)/shard_map/all_gather | solution.py:261
  566.0 192.0 %all-gather.30.cloned.1.call-start = ((), (), s32[]{:S(2)}) async-start(), calls=%async_computation.15 | async-start | bytes 9437184 | tf_op jit(solution)/shard_map/all_gather | solution.py:262
  566.8 350.5 %reduce-scatter.15.cloned.1.call-start = ((), (), s32[]{:S(2)}) async-start(), calls=%async_computation.22 | async-start | bytes 10485760 | tf_op jit(solution)/shard_map/reduce_scatter | solution.py:212
  772.7 237.8 %all-gather.34.cloned.1.call-start = ((), (), s32[]{:S(2)}) async-start(), calls=%async_computation.19 | async-start | bytes 5242880 | tf_op jit(solution)/shard_map/all_gather | solution.py:289
  928.8 271.0 %reduce-scatter.13.cloned.1.call-start = ((), (), s32[]{:S(2)}) async-start(), calls=%async_computation.21 | async-start | bytes 10485760 | tf_op jit(solution)/shard_map/reduce_scatter | solution.py:302
  1056.6 291.2 %reduce-scatter.7.cloned.1.call-start = ((), (), s32[]{:S(2)}) async-start(), calls=%async_computation.11 | async-start | bytes 10485760 | tf_op jit(solution)/shard_map/reduce_scatter | solution.py:199
  1101.1 330.2 %all-gather.38.cloned.1.call-start = ((), (), s32[]{:S(2)}) async-start(), calls=%async_computation.23 | async-start | bytes 5242880 | tf_op jit(solution)/shard_map/all_gather | solution.py:317
  1101.8 97.9 %copy-start.5 = (f32[256,1,2048]{2,1,0:T(1,128)S(1)}, f32[256,1,2048]{2,1,0:T(1,128)}, u32[]{:S(2)}) copy-start(f32[256,1,2048]{2,1,0:T(1,128)} %copy-done.4) | copy-start | bytes 6291460
  1101.8 97.9 %copy-start.107 = (f32[256]{0:T(256)S(1)}, f32[256]{0:T(256)}, u32[]{:S(2)}) copy-start(f32[256]{0:T(256)} %copy-done.106) | copy-start | bytes 3076
  1138.2 64.0 %copy-start.119 = (f32[256]{0:T(256)S(1)}, f32[256]{0:T(256)}, u32[]{:S(2)}) copy-start(f32[256]{0:T(256)} %copy-done.118) | copy-start | bytes 3076
  1138.2 64.0 %copy-start.123 = (f32[256]{0:T(256)S(1)}, f32[256]{0:T(256)}, u32[]{:S(2)}) copy-start(f32[256]{0:T(256)} %copy-done.122) | copy-start | bytes 3076
  1138.4 101.5 %copy-start.80 = (f32[256,4,4]{0,2,1:T(4,128)}, f32[256,4,4]{0,2,1:T(4,128)S(1)}, u32[]{:S(2)}) copy-start(f32[256,4,4]{0,2,1:T(4,128)S(1)} %copy.396) | copy-start | bytes 49156
  1138.8 101.2 %copy-start.96 = (f32[256,4,1]{0,2,1:T(1,128)}, f32[256,4,1]{0,2,1:T(1,128)S(1)}, u32[]{:S(2)}) copy-start(f32[256,4,1]{0,2,1:T(1,128)S(1)} %copy.447) | copy-start | bytes 12292
  1307.3 205.4 %all-gather.24.cloned.1.call-start = ((), (), s32[]{:S(2)}) async-start(), calls=%async_computation.12 | async-start | bytes 5242880 | tf_op jit(solution)/shard_map/all_gather | solution.py:206
  1406.9 250.9 %reduce-scatter.17.cloned.1.call-start = ((), (), s32[]{:S(2)}) async-start(), calls=%async_computation.24 | async-start | bytes 10485760 | tf_op jit(solution)/shard_map/reduce_scatter | solution.py:346
  1509.9 295.6 %reduce-scatter.9.cloned.1.call-start = ((), (), s32[]{:S(2)}) async-start(), calls=%async_computation.16 | async-start | bytes 10485760 | tf_op jit(solution)/shard_map/reduce_scatter | solution.py:212
  1554.6 379.5 %all-reduce.11.cloned.1.call-start = ((), (), s32[]{:S(2)}) async-start(), calls=%async_computation.25 | async-start | bytes 262144 | tf_op jit(solution)/shard_map/psum | solution.py:380
  1711.0 996.4 %all-reduce.13.cloned.1.call-start = ((), (), s32[]{:S(2)}) async-start(), calls=%async_computation.26 | async-start | bytes 134217728 | tf_op jit(solution)/shard_map/psum | solution.py:365
  (141 other events, 1362.0 us)
Sparse Core Ops, SparseCore 0:
  9.9 30.5 all-gather.15
  51.0 83.4 all-gather.13
  136.3 26.4 all-gather.17
  164.5 27.8 all-gather.19
  194.4 80.7 all-gather.31
  277.0 26.4 all-gather.21
  346.4 142.8 reduce-scatter.10
  491.1 55.0 all-gather.25
  565.6 81.3 all-gather.35
  648.7 52.9 all-gather.27
  703.6 54.3 all-gather.29
  772.8 144.4 reduce-scatter.14
  928.9 81.4 all-gather.33
  1056.7 142.9 reduce-scatter.12
  1202.5 145.1 reduce-scatter.6
  1349.7 81.4 all-gather.37
  1433.3 79.3 all-gather.23
  1514.8 142.9 reduce-scatter.16
  1660.2 145.1 reduce-scatter.8
  1810.8 123.2 all-reduce.10
  1940.3 766.9 all-reduce.12
where the time goes:
time: 2770 us; the launch traced here: 2760 us
  waiting for transfers between devices  1670 us (60%)
  matrix products  722 us (26%)
  other arithmetic  181 us (7%)
  local copies, waits for them, and re-layouts  119 us (4%)
  blocking collectives  41.3 us (1%)
    psum x1, waiting for transfers between devices, per_device(): lax.psum((query_weight_grad, key_weight_grad, value_weight_grad, out_weig...  772 us
    reduce_scatter x2, waiting for transfers between devices, forward_pass(): lax.psum_scatter(times_transposed(hidden, down_full), 'tensor', scatter_d...  231 us
    reduce_scatter x2, waiting for transfers between devices, forward_pass(): lax.psum_scatter(times_transposed(attended_flat, out_full), 'tensor', sca...  182 us
    dot_general x7, matrix products, mix_streams(): jnp.einsum('rji,rjd->rid', coeffs[:, :, 1:stream_count + 1], streams, pre...  171 us
    dot_general x6, matrix products, mix_streams(): jnp.einsum('rj,rjd->rd', coeffs[:, :, 0], streams, precision=HIGHEST)  131 us
    dot_general x11, matrix products, matmul(): return jnp.dot(left, right, preferred_element_type=jnp.float32)  107 us
    dot_general x8, matrix products, mix_streams(): jnp.einsum('rjd,dc->rjc', normed, mix_weight, precision=HIGHEST)  100 us
    dot_general x9, matrix products, times_transposed(): lax.dot_general(left, right, (((1,), (1,)), ((), ())), preferred_element_...  96.6 us
  transfers between devices with their start and end apart: 21, of which 18 were waited for; matrix products, arithmetic and copies ran while one was open for 31% of the time, Pallas kernels for 0%

commit v1 on v0

v1 whole, which is shorter than its diff:
```python
import functools
import jax
import jax.numpy as jnp
from jax import lax
from jax.experimental import pallas as pl
from jax.experimental.pallas import tpu as pltpu
from jax.sharding import PartitionSpec as P

HEAD_DIM = 128
EPSILON = 1e-05
THETA = 10000.0
MASKED = -1e30
LANES = 128
GROUP = 16
CHUNK = 512
PARAMS = pltpu.CompilerParams(vmem_limit_bytes=50 * 1024 * 1024)


def matmul(left, right):
    return jnp.dot(left, right, preferred_element_type=jnp.float32)


def times_transposed(left, right):
    return lax.dot_general(
        left, right, (((1,), (1,)), ((), ())), preferred_element_type=jnp.float32
    )


def transposed_times(left, right):
    return lax.dot_general(
        left, right, (((0,), (0,)), ((), ())), preferred_element_type=jnp.float32
    )


def lanes_of(rows):
    return lax.broadcasted_iota(jnp.int32, (rows, LANES), 1)


def column(values, lane):
    return values[:, lane : lane + 1]


def place(values, columns, first):
    lane = lanes_of(values.shape[0])
    for offset, one in enumerate(columns):
        values = jnp.where(lane == first + offset, one, values)
    return values


def fold(values):
    total = values[:, :LANES]
    for start in range(LANES, values.shape[1], LANES):
        total = total + values[:, start : start + LANES]
    return total


def row_sum(values):
    return jnp.sum(values, axis=1, keepdims=True)


def rolled(values, shift):
    shift = shift % LANES
    return values if shift == 0 else pltpu.roll(values, shift, 1)


def coefficients(projected, means, rsqrts, param_ref, streams, uses, parts, centred):
    rows = projected[0].shape[0]
    lane = lanes_of(rows)
    gathered = jnp.zeros((rows, LANES), jnp.float32)
    for j in range(streams):
        total = projected[j]
        for part in range(1, parts):
            total = total + rolled(projected[j], -part * uses)
        if not centred:
            total = total - means[j] * param_ref[2:3, :]
        total = total * rsqrts[j]
        inside = (lane >= j * uses) & (lane < (j + 1) * uses)
        gathered = jnp.where(inside, rolled(total, j * uses), gathered)
    bent = jnp.tanh(gathered)
    return gathered, bent, param_ref[0:1, :] + param_ref[1:2, :] * bent


def pack_saved(coeffs, bent, gathered, means, rsqrts, mean_e, rsqrt_e, streams, uses):
    lane = lanes_of(coeffs.shape[0])
    count = streams * uses
    saved = jnp.where(lane < count, coeffs, 0.0)
    saved = jnp.where((lane >= count) & (lane < 2 * count), rolled(bent, count), saved)
    saved = jnp.where((lane >= 2 * count) & (lane < 3 * count), rolled(gathered, 2 * count), saved)
    return place(saved, [*means, *rsqrts, mean_e, rsqrt_e], 3 * count)


def centre_stats(total, values_of, width):
    mean = row_sum(total) * (1.0 / width)
    spread = None
    for start in range(0, width, CHUNK):
        centred = values_of(start) - mean
        square = fold(centred * centred)
        spread = square if spread is None else spread + square
    return mean, lax.rsqrt(row_sum(spread) * (1.0 / width) + EPSILON)


def entering_norm(read, coeffs, streams, uses, width, entering_ref, rows):
    total = None
    for start in range(0, width, CHUNK):
        entering = column(coeffs, 0) * read(0, start)
        for j in range(1, streams):
            entering = entering + column(coeffs, j * uses) * read(j, start)
        entering_ref[rows, start : start + CHUNK] = entering
        part = fold(entering)
        total = part if total is None else total + part
    return centre_stats(total, lambda start: entering_ref[rows, start : start + CHUNK], width)


def open_attention_kernel(streams, uses, width, x_ref, w_ref, param_ref, normed_ref, saved_ref, raw_ref, entering_ref):
    block = x_ref.shape[0]
    stacked = jnp.concatenate([x_ref[:, j * width : (j + 1) * width] for j in range(streams)], axis=0)
    raw_ref[...] = jnp.dot(stacked, w_ref[...], preferred_element_type=jnp.float32)

    def body(index, carry):
        first = pl.multiple_of(index * GROUP, GROUP)
        rows = pl.ds(first, GROUP)

        def read(j, start):
            return x_ref[rows, j * width + start : j * width + start + CHUNK].astype(jnp.float32)

        means, rsqrts, projected = [], [], []
        for j in range(streams):
            total = None
            for start in range(0, width, CHUNK):
                part = fold(read(j, start))
                total = part if total is None else total + part
            mean, rsqrt = centre_stats(total, functools.partial(read, j), width)
            means.append(mean)
            rsqrts.append(rsqrt)
            projected.append(raw_ref[pl.ds(pl.multiple_of(j * block + first, GROUP), GROUP), :])
        gathered, bent, coeffs = coefficients(projected, means, rsqrts, param_ref, streams, uses, 3, False)
        mean_e, rsqrt_e = entering_norm(read, coeffs, streams, uses, width, entering_ref, rows)
        for start in range(0, width, CHUNK):
            normed_ref[rows, start : start + CHUNK] = (
                (entering_ref[rows, start : start + CHUNK] - mean_e) * rsqrt_e
            ).astype(jnp.bfloat16)
        saved_ref[rows, :] = pack_saved(coeffs, bent, gathered, means, rsqrts, mean_e, rsqrt_e, streams, uses)
        return carry

    lax.fori_loop(0, block // GROUP, body, 0)


def open_feedforward_kernel(
    streams, uses, width,
    x_ref, saved_a_ref, arrived_ref, partial_ref, g_ref, valid_ref, w_ref, param_ref,
    normed_ref, grad_ref, saved_ref, h_ref, out_ref,
    high_ref, low_ref, raw_ref, entering_ref, stats_ref,
):
    block = x_ref.shape[0]
    count = streams * uses

    def first_pass(index, carry):
        first = pl.multiple_of(index * GROUP, GROUP)
        rows = pl.ds(first, GROUP)
        coeffs = saved_a_ref[rows, :]
        totals = [None] * streams
        for start in range(0, width, CHUNK):
            out = arrived_ref[rows, start : start + CHUNK].astype(jnp.float32) + partial_ref[rows, start : start + CHUNK]
            out_ref[rows, start : start + CHUNK] = out
            values = [
                x_ref[rows, j * width + start : j * width + start + CHUNK].astype(jnp.float32)
                for j in range(streams)
            ]
            for i in range(streams):
                mixed = column(coeffs, i * uses + streams + 1) * out
                for j in range(streams):
                    mixed = mixed + column(coeffs, j * uses + 1 + i) * values[j]
                h_ref[rows, i * width + start : i * width + start + CHUNK] = mixed
                part = fold(mixed)
                totals[i] = part if totals[i] is None else totals[i] + part
        stats = jnp.zeros((GROUP, LANES), jnp.float32)
        means, rsqrts = [], []
        for i in range(streams):
            mean = row_sum(totals[i]) * (1.0 / width)
            spread = None
            for start in range(0, width, CHUNK):
                centred = h_ref[rows, i * width + start : i * width + start + CHUNK] - mean
                high = centred.astype(jnp.bfloat16)
                target = pl.ds(pl.multiple_of(i * block + first, GROUP), GROUP)
                high_ref[target, start : start + CHUNK] = high
                low_ref[target, start : start + CHUNK] = (centred - high.astype(jnp.float32)).astype(jnp.bfloat16)
                square = fold(centred * centred)
                spread = square if spread is None else spread + square
            means.append(mean)
            rsqrts.append(lax.rsqrt(row_sum(spread) * (1.0 / width) + EPSILON))
        stats_ref[rows, :] = place(stats, [*means, *rsqrts], 0)
        return carry

    lax.fori_loop(0, block // GROUP, first_pass, 0)
    raw_ref[...] = jnp.dot(high_ref[...], w_ref[...], preferred_element_type=jnp.float32) + jnp.dot(
        low_ref[...], w_ref[...], preferred_element_type=jnp.float32
    )

    def second_pass(index, carry):
        first = pl.multiple_of(index * GROUP, GROUP)
        rows = pl.ds(first, GROUP)
        stats = stats_ref[rows, :]
        means = [column(stats, j) for j in range(streams)]
        rsqrts = [column(stats, streams + j) for j in range(streams)]
        projected = [raw_ref[pl.ds(pl.multiple_of(j * block + first, GROUP), GROUP), :] for j in range(streams)]
        gathered, bent, coeffs = coefficients(projected, means, rsqrts, param_ref, streams, uses, 2, True)

        def read(j, start):
            return h_ref[rows, j * width + start : j * width + start + CHUNK]

        mean_e, rsqrt_e = entering_norm(read, coeffs, streams, uses, width, entering_ref, rows)
        branch = [column(coeffs, i * uses + streams + 1) * valid_ref[rows, 0:1] for i in range(streams)]
        for start in range(0, width, CHUNK):
            normed_ref[rows, start : start + CHUNK] = (
                (entering_ref[rows, start : start + CHUNK] - mean_e) * rsqrt_e
            ).astype(jnp.bfloat16)
            grad = None
            for i in range(streams):
                term = branch[i] * g_ref[rows, i * width + start : i * width + start + CHUNK].astype(jnp.float32)
                grad = term if grad is None else grad + term
            grad_ref[rows, start : start + CHUNK] = grad.astype(jnp.bfloat16)
        saved_ref[rows, :] = pack_saved(coeffs, bent, gathered, means, rsqrts, mean_e, rsqrt_e, streams, uses)
        return carry

    lax.fori_loop(0, block // GROUP, second_pass, 0)


def finish_kernel(streams, uses, width, h_ref, saved_ref, arrived_ref, partial_ref, y_ref):
    def body(index, carry):
        rows = pl.ds(pl.multiple_of(index * GROUP, GROUP), GROUP)
        coeffs = saved_ref[rows, :]
        for start in range(0, width, CHUNK):
            out = arrived_ref[rows, start : start + CHUNK].astype(jnp.float32) + partial_ref[rows, start : start + CHUNK]
            values = [h_ref[rows, j * width + start : j * width + start + CHUNK] for j in range(streams)]
            for i in range(streams):
                mixed = column(coeffs, i * uses + streams + 1) * out
                for j in range(streams):
                    mixed = mixed + column(coeffs, j * uses + 1 + i) * values[j]
                y_ref[rows, i * width + start : i * width + start + CHUNK] = mixed.astype(jnp.bfloat16)
        return carry

    lax.fori_loop(0, h_ref.shape[0] // GROUP, body, 0)


def close_kernel(streams, uses, width, inner, *refs):
    if inner:
        (h_ref, saved_ref, g_ref, arrived_ref, partial_ref, arrived_f_ref, partial_f_ref, valid_ref, saved_a_ref,
         out_a_ref, wt_ref, param_ref, grad_ref, below_ref, branch_ref, weight_ref, small_ref,
         centre_ref, du_ref, left_ref, dl_ref, cols_ref, sums_ref) = refs
    else:
        (h_ref, saved_ref, g_ref, arrived_ref, partial_ref, branch_in_ref, wt_ref, param_ref,
         grad_ref, weight_ref, small_ref, centre_ref, du_ref, left_ref, dl_ref, cols_ref, sums_ref) = refs
    block = h_ref.shape[0]
    count = streams * uses
    step = pl.program_id(0)
    base = pl.multiple_of(step * block, GROUP)
    all_rows = centre_ref.shape[0] // streams

    @pl.when(step == 0)
    def _():
        sums_ref[...] = jnp.zeros_like(sums_ref)

    def read_h(rows, j, start):
        return h_ref[rows, j * width + start : j * width + start + CHUNK].astype(jnp.float32)

    def read_g(rows, i, start):
        values = g_ref[rows, i * width + start : i * width + start + CHUNK].astype(jnp.float32)
        return values * valid_ref[rows, 0:1] if inner else values

    def read_dn(rows, start):
        return arrived_ref[rows, start : start + CHUNK].astype(jnp.float32) + partial_ref[rows, start : start + CHUNK]

    def first_pass(index, carry):
        first = pl.multiple_of(index * GROUP, GROUP)
        rows = pl.ds(first, GROUP)
        saved = saved_ref[rows, :]
        means = [column(saved, 3 * count + j) for j in range(streams)]
        rsqrts = [column(saved, 3 * count + streams + j) for j in range(streams)]
        mean_e = column(saved, 3 * count + 2 * streams)
        rsqrt_e = column(saved, 3 * count + 2 * streams + 1)
        sums = {}

        def add(key, values):
            part = fold(values)
            sums[key] = part if key not in sums else sums[key] + part

        for start in range(0, width, CHUNK):
            dn = read_dn(rows, start)
            values = [read_h(rows, j, start) for j in range(streams)]
            for j in range(streams):
                target = pl.ds(pl.multiple_of(j * all_rows + base + first, GROUP), GROUP)
                centre_ref[target, start : start + CHUNK] = (values[j] - means[j]).astype(jnp.bfloat16)
            entering = column(saved, 0) * values[0]
            for j in range(1, streams):
                entering = entering + column(saved, j * uses) * values[j]
            normed = (entering - mean_e) * rsqrt_e
            add("dn", dn)
            add("dnn", dn * normed)
            for j in range(streams):
                add(("dnh", j), dn * values[j])
                add(("nh", j), normed * values[j])
            if inner:
                out = (
                    arrived_f_ref[rows, start : start + CHUNK].astype(jnp.float32)
                    + partial_f_ref[rows, start : start + CHUNK]
                )
            for i in range(streams):
                g = read_g(rows, i, start)
                for j in range(streams):
                    add(("gh", j, i), g * values[j])
                if inner:
                    add(("go", i), g * out)
        total = {key: row_sum(value) for key, value in sums.items()}
        mean_dn = total["dn"] * (1.0 / width)
        mean_dnn = total["dnn"] * (1.0 / width)
        columns = []
        for j in range(streams):
            columns.append(
                rsqrt_e * (total["dnh", j] - total["dn"] * means[j] - mean_dnn * total["nh", j])
            )
            columns.extend(total["gh", j, i] for i in range(streams))
            columns.append(total["go", j] if inner else branch_in_ref[rows, j : j + 1])
        d_coeffs = place(jnp.zeros((GROUP, LANES), jnp.float32), columns, 0)
        lane = lanes_of(GROUP)
        bent = jnp.where(lane < count, rolled(saved, -count), 0.0)
        projected = jnp.where(lane < count, rolled(saved, -2 * count), 0.0)
        sums_ref[0] += d_coeffs
        sums_ref[1] += d_coeffs * bent
        du = d_coeffs * param_ref[1:2, :] * (1.0 - bent * bent)
        with_mean = du * param_ref[3:4, :] * (1.0 / width)
        with_value = du * projected * (1.0 / width)
        shifts, slopes = [], []
        scaled = jnp.zeros((GROUP, LANES), jnp.float32)
        for j in range(streams):
            inside = (lane >= j * uses) & (lane < (j + 1) * uses)
            slope = rsqrts[j] * rsqrts[j] * row_sum(jnp.where(inside, with_value, 0.0))
            shifts.append(means[j] * slope - rsqrts[j] * row_sum(jnp.where(inside, with_mean, 0.0)))
            slopes.append(slope)
            scaled = jnp.where(inside, du * rsqrts[j], scaled)
        high = scaled.astype(jnp.bfloat16).astype(jnp.float32)
        low = (scaled - high).astype(jnp.bfloat16).astype(jnp.float32)
        spread = jnp.where(lane < count, high, 0.0)
        spread = jnp.where((lane >= count) & (lane < 2 * count), rolled(low, count), spread)
        spread = jnp.where((lane >= 2 * count) & (lane < 3 * count), rolled(high, 2 * count), spread)
        for j in range(streams):
            mine = lane < 0
            for part in range(3):
                begin = part * count + j * uses
                mine = mine | ((lane >= begin) & (lane < begin + uses))
            left_ref[pl.ds(pl.multiple_of(j * block + first, GROUP), GROUP), :] = jnp.where(
                mine, spread, 0.0
            ).astype(jnp.bfloat16)
            pair = jnp.where(lane < uses, rolled(high, -j * uses), 0.0)
            pair = jnp.where((lane >= uses) & (lane < 2 * uses), rolled(low, uses - j * uses), pair)
            du_ref[pl.ds(pl.multiple_of(j * all_rows + base + first, GROUP), GROUP), :] = pair.astype(jnp.bfloat16)
        cols_ref[rows, :] = place(
            jnp.zeros((GROUP, LANES), jnp.float32), [mean_dn, mean_dnn, *shifts, *slopes], 0
        )
        return carry

    lax.fori_loop(0, block // GROUP, first_pass, 0)
    dl_ref[...] = jnp.dot(left_ref[...], wt_ref[...], preferred_element_type=jnp.float32)

    def second_pass(index, carry):
        first = pl.multiple_of(index * GROUP, GROUP)
        rows = pl.ds(first, GROUP)
        saved = saved_ref[rows, :]
        cols = cols_ref[rows, :]
        mean_e = column(saved, 3 * count + 2 * streams)
        rsqrt_e = column(saved, 3 * count + 2 * streams + 1)
        scaled_mean = column(cols, 0) * rsqrt_e
        scaled_slope = column(cols, 1) * rsqrt_e
        branch_sums = [None] * streams
        for start in range(0, width, CHUNK):
            values = [read_h(rows, j, start) for j in range(streams)]
            entering = column(saved, 0) * values[0]
            for j in range(1, streams):
                entering = entering + column(saved, j * uses) * values[j]
            normed = (entering - mean_e) * rsqrt_e
            de = rsqrt_e * read_dn(rows, start) - scaled_mean - normed * scaled_slope
            gs = [read_g(rows, i, start) for i in range(streams)]
            below = None
            for j in range(streams):
                grad = column(saved, j * uses) * de + column(cols, 2 + j)
                grad = grad - values[j] * column(cols, 2 + streams + j)
                grad = grad + dl_ref[pl.ds(pl.multiple_of(j * block + first, GROUP), GROUP), start : start + CHUNK]
                for i in range(streams):
                    grad = grad + column(saved, j * uses + 1 + i) * gs[i]
                grad_ref[rows, j * width + start : j * width + start + CHUNK] = grad.astype(grad_ref.dtype)
                if inner:
                    part = fold(grad * out_a_ref[rows, start : start + CHUNK])
                    branch_sums[j] = part if branch_sums[j] is None else branch_sums[j] + part
                    term = saved_a_ref[rows, j * uses + streams + 1 : j * uses + streams + 2] * grad
                    below = term if below is None else below + term
            if inner:
                below_ref[rows, start : start + CHUNK] = below.astype(jnp.bfloat16)
        if inner:
            branch_ref[rows, :] = place(
                jnp.zeros((GROUP, LANES), jnp.float32), [row_sum(one) for one in branch_sums], 0
            )
        return carry

    lax.fori_loop(0, block // GROUP, second_pass, 0)

    @pl.when(step == pl.num_programs(0) - 1)
    def _():
        product = lax.dot_general(
            du_ref[...], centre_ref[...], (((0,), (0,)), ((), ())), preferred_element_type=jnp.float32
        )
        weight_ref[...] = product[: weight_ref.shape[0]]
        small_ref[0:1, :] = jnp.sum(sums_ref[0], axis=0, keepdims=True)
        small_ref[1:2, :] = jnp.sum(sums_ref[1], axis=0, keepdims=True)


def rows_block(rows):
    return min(64, rows)


def specs_for(arrays, block, whole):
    return [
        pl.BlockSpec(a.shape, lambda i: (0, 0)) if k in whole else pl.BlockSpec((block, a.shape[1]), lambda i: (i, 0))
        for k, a in enumerate(arrays)
    ]


def rounded(values):
    return lax.reduce_precision(values, 8, 7)


def mix_tables(static, weight, scale):
    streams, uses = static.shape
    width = weight.shape[0]
    high = rounded(weight)
    middle = rounded(weight - high)
    low = rounded(weight - high - middle)
    forward = jnp.pad(jnp.concatenate([high, middle, low], axis=1), ((0, 0), (0, LANES - 3 * uses))).astype(jnp.bfloat16)
    tall = [jnp.tile(part.T, (streams, 1)) for part in (high, high, middle)]
    backward = jnp.pad(jnp.concatenate(tall, axis=0), ((0, LANES - 3 * streams * uses), (0, 0))).astype(jnp.bfloat16)
    total = jnp.sum(weight, axis=0)
    count = streams * uses

    def row(values):
        return jnp.pad(values, (0, LANES - values.shape[0]))[None]

    params = jnp.concatenate(
        [row(static.reshape(count)), row(jnp.tile(scale, streams)), row(total), row(jnp.tile(total, streams)), jnp.zeros((4, LANES), jnp.float32)]
    )
    return forward, backward, params


def open_attention(x, tables, streams, uses):
    rows, width = x.shape[0], x.shape[1] // streams
    block = rows_block(rows)
    arrays = [x, tables[0], tables[2]]
    return pl.pallas_call(
        functools.partial(open_attention_kernel, streams, uses, width),
        grid=(rows // block,),
        in_specs=specs_for(arrays, block, {1, 2}),
        out_specs=[pl.BlockSpec((block, width), lambda i: (i, 0)), pl.BlockSpec((block, LANES), lambda i: (i, 0))],
        out_shape=[jax.ShapeDtypeStruct((rows, width), jnp.bfloat16), jax.ShapeDtypeStruct((rows, LANES), jnp.float32)],
        scratch_shapes=[pltpu.VMEM((streams * block, LANES), jnp.float32), pltpu.VMEM((block, width), jnp.float32)],
        compiler_params=PARAMS,
        name="open_attention",
    )(*arrays)


def open_feedforward(x, saved_a, arrived, partial, g, valid, tables, streams, uses):
    rows, width = x.shape[0], x.shape[1] // streams
    block = rows_block(rows)
    arrays = [x, saved_a, arrived, partial, g, valid, tables[0], tables[2]]

    def by_rows(columns):
        return pl.BlockSpec((block, columns), lambda i: (i, 0))

    return pl.pallas_call(
        functools.partial(open_feedforward_kernel, streams, uses, width),
        grid=(rows // block,),
        in_specs=specs_for(arrays, block, {6, 7}),
        out_specs=[by_rows(width), by_rows(width), by_rows(LANES), by_rows(streams * width), by_rows(width)],
        out_shape=[
            jax.ShapeDtypeStruct((rows, width), jnp.bfloat16),
            jax.ShapeDtypeStruct((rows, width), jnp.bfloat16),
            jax.ShapeDtypeStruct((rows, LANES), jnp.float32),
            jax.ShapeDtypeStruct((rows, streams * width), jnp.float32),
            jax.ShapeDtypeStruct((rows, width), jnp.float32),
        ],
        scratch_shapes=[
            pltpu.VMEM((streams * block, width), jnp.bfloat16),
            pltpu.VMEM((streams * block, width), jnp.bfloat16),
            pltpu.VMEM((streams * block, LANES), jnp.float32),
            pltpu.VMEM((block, width), jnp.float32),
            pltpu.VMEM((block, LANES), jnp.float32),
        ],
        compiler_params=PARAMS,
        name="open_feedforward",
    )(*arrays)


def finish(h, saved, arrived, partial, streams, uses):
    rows, width = h.shape[0], h.shape[1] // streams
    block = rows_block(rows)
    arrays = [h, saved, arrived, partial]
    return pl.pallas_call(
        functools.partial(finish_kernel, streams, uses, width),
        grid=(rows // block,),
        in_specs=specs_for(arrays, block, set()),
        out_specs=pl.BlockSpec((block, streams * width), lambda i: (i, 0)),
        out_shape=jax.ShapeDtypeStruct((rows, streams * width), jnp.bfloat16),
        compiler_params=PARAMS,
        name="finish",
    )(*arrays)


def close_mix(inner, arrays, tables, streams, uses):
    h = arrays[0]
    rows, width = h.shape[0], h.shape[1] // streams
    block = rows_block(rows)
    arrays = [*arrays, tables[1], tables[2]]
    last = len(arrays)

    def by_rows(columns):
        return pl.BlockSpec((block, columns), lambda i: (i, 0))

    def fixed(height, columns):
        return pl.BlockSpec((height, columns), lambda i: (0, 0))

    out_specs = [by_rows(streams * width)]
    out_shape = [jax.ShapeDtypeStruct((rows, streams * width), jnp.float32 if inner else jnp.bfloat16)]
    if inner:
        out_specs += [by_rows(width), by_rows(LANES)]
        out_shape += [
            jax.ShapeDtypeStruct((rows, width), jnp.bfloat16),
            jax.ShapeDtypeStruct((rows, LANES), jnp.float32),
        ]
    out_specs += [fixed(16, width), fixed(8, LANES)]
    out_shape += [jax.ShapeDtypeStruct((16, width), jnp.float32), jax.ShapeDtypeStruct((8, LANES), jnp.float32)]
    return pl.pallas_call(
        functools.partial(close_kernel, streams, uses, width, inner),
        grid=(rows // block,),
        in_specs=specs_for(arrays, block, {last - 2, last - 1}),
        out_specs=out_specs,
        out_shape=out_shape,
        scratch_shapes=[
            pltpu.VMEM((streams * rows, width), jnp.bfloat16),
            pltpu.VMEM((streams * rows, LANES), jnp.bfloat16),
            pltpu.VMEM((streams * block, LANES), jnp.bfloat16),
            pltpu.VMEM((streams * block, width), jnp.float32),
            pltpu.VMEM((block, LANES), jnp.float32),
            pltpu.VMEM((2, GROUP, LANES), jnp.float32),
        ],
        compiler_params=PARAMS,
        name="close_feedforward" if inner else "close_attention",
    )(*arrays)


def mix_grads(weight_sum, small, streams, uses):
    count = streams * uses
    return (
        small[0, :count].reshape(streams, uses),
        (weight_sum[:uses] + weight_sum[uses : 2 * uses]).T,
        jnp.sum(small[1, :count].reshape(streams, uses), axis=0),
    )


QUERY_ROWS = 256


def turn(values, cosine, sine):
    return values * cosine + pltpu.roll(values, HEAD_DIM // 2, 1) * sine


def turn_back(values, cosine, sine):
    return values * cosine - pltpu.roll(values, HEAD_DIM // 2, 1) * sine


def block_offset(mine, step, size, rows):
    return pl.multiple_of(lax.rem(mine + size - step, size) * rows, rows)


def allowed_keys(start_ref, first, rows, keys):
    row = first + lax.broadcasted_iota(jnp.int32, (rows, keys), 0)
    key = lax.broadcasted_iota(jnp.int32, (rows, keys), 1)
    return (key <= row) & (key >= start_ref[first : first + rows, 0:1])


def attend_kernel(size, *refs):
    mine_ref, start_ref, cosine_ref, sine_ref = refs[:4]
    raw = [refs[4 + 3 * s : 7 + 3 * s] for s in range(size)]
    q_ref, k_ref, v_ref, out_ref, log_ref, attended_ref = refs[4 + 3 * size :]
    mine = mine_ref[0]
    block = raw[0][0].shape[0]
    total = size * block
    for step in range(size):
        rows = pl.ds(block_offset(mine, step, size, block), block)
        cosine, sine = cosine_ref[rows, :], sine_ref[rows, :]
        q_ref[rows, :] = turn(raw[step][0][...], cosine, sine).astype(jnp.bfloat16)
        k_ref[rows, :] = turn(raw[step][1][...], cosine, sine).astype(jnp.bfloat16)
        v_ref[rows, :] = raw[step][2][...].astype(jnp.bfloat16)
    height = min(QUERY_ROWS, total)
    for first in range(0, total, height):
        keys = first + height
        scores = times_transposed(q_ref[first:keys, :], k_ref[:keys, :]) * HEAD_DIM**-0.5
        scores = jnp.where(allowed_keys(start_ref, first, height, keys), scores, MASKED)
        highest = jnp.max(scores, axis=1, keepdims=True)
        exponent = jnp.exp(scores - highest)
        row_total = jnp.sum(exponent, axis=1, keepdims=True)
        probs = (exponent * (1.0 / row_total)).astype(jnp.bfloat16)
        attended_ref[first:keys, :] = jnp.dot(
            probs, v_ref[:keys, :], preferred_element_type=jnp.float32
        ).astype(jnp.bfloat16)
        log_ref[first:keys, :] = jnp.broadcast_to(highest + jnp.log(row_total), (height, LANES))
    for step in range(size):
        rows = pl.ds(block_offset(mine, step, size, block), block)
        out_ref[step * block : (step + 1) * block, :] = attended_ref[rows, :]


def attend_back_kernel(size, *refs):
    mine_ref, start_ref, cosine_ref, sine_ref, q_ref, k_ref, v_ref, log_ref = refs[:8]
    grads = refs[8 : 8 + size]
    dqkv_ref, d_out_ref, dq_ref, dk_ref, dv_ref = refs[8 + size :]
    mine = mine_ref[0]
    head, heads = pl.program_id(0), pl.num_programs(0)
    block = grads[0].shape[0]
    total = size * block
    for step in range(size):
        d_out_ref[pl.ds(block_offset(mine, step, size, block), block), :] = grads[step][...]
    height = min(QUERY_ROWS, total)
    dk_ref[...] = jnp.zeros_like(dk_ref)
    dv_ref[...] = jnp.zeros_like(dv_ref)
    for first in range(0, total, height):
        keys = first + height
        q, d_out = q_ref[first:keys, :], d_out_ref[first:keys, :]
        k, v = k_ref[:keys, :], v_ref[:keys, :]
        scores = times_transposed(q, k) * HEAD_DIM**-0.5
        probs = jnp.where(
            allowed_keys(start_ref, first, height, keys), jnp.exp(scores - log_ref[first:keys, 0:1]), 0.0
        )
        d_probs = times_transposed(d_out, v)
        centre = jnp.sum(probs * d_probs, axis=1, keepdims=True)
        d_scores = (probs * (d_probs - centre)).astype(jnp.bfloat16)
        dv_ref[:keys, :] += transposed_times(probs.astype(jnp.bfloat16), d_out)
        dk_ref[:keys, :] += transposed_times(d_scores, q)
        dq_ref[first:keys, :] = jnp.dot(d_scores, k, preferred_element_type=jnp.float32)
    for step in range(size):
        rows = pl.ds(block_offset(mine, step, size, block), block)
        cosine, sine = cosine_ref[rows, :], sine_ref[rows, :]
        target = slice(step * block, (step + 1) * block)
        for part, values in enumerate(
            (
                turn_back(dq_ref[rows, :] * HEAD_DIM**-0.5, cosine, sine),
                turn_back(dk_ref[rows, :] * HEAD_DIM**-0.5, cosine, sine),
                dv_ref[rows, :],
            )
        ):
            columns = pl.ds(pl.multiple_of((part * heads + head) * HEAD_DIM, HEAD_DIM), HEAD_DIM)
            dqkv_ref[target, columns] = values.astype(jnp.bfloat16)


def whole_spec(shape):
    return pl.BlockSpec(shape, lambda h: (0,) * len(shape))


def head_spec(rows, first=0):
    return pl.BlockSpec((rows, HEAD_DIM), lambda h: (0, first + h))


def attend(raw_blocks, mine, starts, cosine, sine):
    size, block = len(raw_blocks), raw_blocks[0].shape[0]
    heads = raw_blocks[0].shape[1] // (3 * HEAD_DIM)
    total = size * block
    flat = jax.ShapeDtypeStruct((total, heads * HEAD_DIM), jnp.bfloat16)
    return pl.pallas_call(
        functools.partial(attend_kernel, size),
        grid=(heads,),
        in_specs=[pl.BlockSpec(memory_space=pltpu.SMEM)]
        + [whole_spec(a.shape) for a in (starts, cosine, sine)]
        + [head_spec(block, part * heads) for _ in range(size) for part in range(3)],
        out_specs=[head_spec(total)] * 5,
        out_shape=[flat] * 4 + [jax.ShapeDtypeStruct(flat.shape, jnp.float32)],
        scratch_shapes=[pltpu.VMEM((total, HEAD_DIM), jnp.bfloat16)],
        compiler_params=PARAMS,
        name="attend",
    )(mine, starts, cosine, sine, *[raw for raw in raw_blocks for _ in range(3)])


def attend_back(heads_kept, grad_blocks, mine, starts, cosine, sine):
    size, block = len(grad_blocks), grad_blocks[0].shape[0]
    total, columns = heads_kept[0].shape
    heads = columns // HEAD_DIM
    return pl.pallas_call(
        functools.partial(attend_back_kernel, size),
        grid=(heads,),
        in_specs=[pl.BlockSpec(memory_space=pltpu.SMEM)]
        + [whole_spec(a.shape) for a in (starts, cosine, sine)]
        + [head_spec(total)] * 4
        + [head_spec(block)] * size,
        out_specs=whole_spec((total, 3 * columns)),
        out_shape=jax.ShapeDtypeStruct((total, 3 * columns), jnp.bfloat16),
        scratch_shapes=[pltpu.VMEM((total, HEAD_DIM), jnp.bfloat16)] + [pltpu.VMEM((total, HEAD_DIM), jnp.float32)] * 3,
        compiler_params=PARAMS,
        name="attend_back",
    )(mine, starts, cosine, sine, *heads_kept, *grad_blocks)


def ring_shift(block):
    size = lax.axis_size("tensor")
    return lax.ppermute(block, "tensor", [(i, (i + 1) % size) for i in range(size)])


def ring_gather(block):
    blocks = [block]
    for _ in range(lax.axis_size("tensor") - 1):
        blocks.append(ring_shift(blocks[-1]))
    return blocks


def ring_scatter(partials):
    total = partials[1]
    for step in range(2, len(partials) + 1):
        arrived = ring_shift(total.astype(jnp.bfloat16))
        own = partials[step % len(partials)]
        total = arrived.astype(jnp.float32) + own
    return arrived, own


def swap(values, axis, bit):
    return lax.ppermute(values, axis, [(i, i ^ (1 << bit)) for i in range(lax.axis_size(axis))])


def bit_of(axis, bit):
    return (lax.axis_index(axis) >> bit) & 1


def halves_by(bit_value, mine, other):
    return jnp.where(
        bit_value == 0, jnp.concatenate([mine, other], axis=0), jnp.concatenate([other, mine], axis=0)
    )


def product_sum(left, right):
    bits = (lax.axis_size("dp") - 1).bit_length()
    half = left.shape[1] // 2
    core = bit_of("dp", 0)
    away = transposed_times(lax.dynamic_slice_in_dim(left, (1 - core) * half, half, 1), right)
    arrived = swap(away.astype(jnp.bfloat16), "dp", 0)
    total = transposed_times(lax.dynamic_slice_in_dim(left, core * half, half, 1), right)
    total = total + arrived.astype(jnp.float32)
    gathered = []
    for part, order in zip(jnp.split(total, 2), (list(range(1, bits)), list(range(bits - 1, 0, -1)))):
        for bit in order:
            rows, which = part.shape[0] // 2, bit_of("dp", bit)
            away = lax.dynamic_slice_in_dim(part, (1 - which) * rows, rows).astype(jnp.bfloat16)
            arrived = swap(away, "dp", bit)
            part = lax.dynamic_slice_in_dim(part, which * rows, rows) + arrived.astype(jnp.float32)
        part = part.astype(jnp.bfloat16)
        for bit in reversed(order):
            part = halves_by(bit_of("dp", bit), part, swap(part, "dp", bit))
        gathered.append(part)
    mine = jnp.concatenate(gathered)
    return mine, swap(mine, "dp", 0)


def sum_everywhere(values):
    for axis in ("dp", "tensor"):
        for bit in range((lax.axis_size(axis) - 1).bit_length()):
            values = values + swap(values, axis, bit)
    return values


def in_order(halves):
    return halves_by(bit_of("dp", 0), *halves).astype(jnp.float32)


def segments_from(slot_lengths, group_rows):
    bounds = jnp.cumsum(slot_lengths)
    row_ids = jnp.arange(group_rows, dtype=jnp.int32)
    segment = jnp.sum((row_ids[:, None] >= bounds[None, :]).astype(jnp.int32), axis=1)
    starting = jnp.concatenate([jnp.zeros((1,), jnp.int32), bounds])
    labels = jnp.arange(starting.shape[0], dtype=jnp.int32)
    begins = jnp.sum(jnp.where(segment[:, None] == labels[None, :], starting[None, :], 0), axis=1)
    return (segment, begins)


def group_layout(lengths, permutation, group_rows, seq_count):
    group_index = lax.axis_index("dp")
    chosen = lax.dynamic_slice_in_dim(permutation, group_index * seq_count, seq_count)
    matches = chosen[:, None] == jnp.arange(permutation.shape[0], dtype=jnp.int32)[None, :]
    slot_lengths = jnp.sum(jnp.where(matches, lengths[None, :], 0), axis=1)
    return segments_from(slot_lengths, group_rows)


def rope_tables(position):
    halfway = HEAD_DIM // 2
    frequency = THETA ** (-(2.0 * jnp.arange(halfway, dtype=jnp.float32)) / HEAD_DIM)
    angles = position.astype(jnp.float32)[:, None] * frequency[None, :]
    cosine, sine = jnp.cos(angles), jnp.sin(angles)
    return jnp.concatenate([cosine, cosine], axis=1), jnp.concatenate([-sine, sine], axis=1)


def gather_rows(*weights):
    return lax.all_gather(jnp.concatenate(weights, axis=1), "dp", axis=0, tiled=True)


def per_device(
    streams,
    cotangent,
    lengths,
    permutation,
    query_weight,
    key_weight,
    value_weight,
    out_weight,
    gate_weight,
    up_weight,
    down_weight,
    mix_static,
    mix_weight,
    mix_scale,
):
    qkv_full = gather_rows(query_weight, key_weight, value_weight)
    out_full = gather_rows(out_weight)
    gate_up_full = gather_rows(gate_weight, up_weight)
    down_full = gather_rows(down_weight)
    local_rows, count, width = streams.shape
    uses = mix_static.shape[2]
    sizes = (count, uses)
    size = lax.axis_size("tensor")
    group_rows = local_rows * size
    mine = lax.axis_index("tensor")
    place_index = jnp.full((1,), mine, jnp.int32)
    units = gate_weight.shape[1]
    seq_count = permutation.shape[0] // lax.axis_size("dp")

    inputs = streams.reshape(local_rows, count * width)
    cotangents = cotangent.reshape(local_rows, count * width)
    tables_a = mix_tables(mix_static[0], mix_weight[0], mix_scale[0])
    tables_f = mix_tables(mix_static[1], mix_weight[1], mix_scale[1])
    segment, begins = group_layout(lengths, permutation, group_rows, seq_count)
    cosine, sine = rope_tables(jnp.arange(group_rows, dtype=jnp.int32) - begins)
    starts = jnp.broadcast_to(begins[:, None], (group_rows, LANES))
    local_segment = lax.dynamic_slice_in_dim(segment, mine * local_rows, local_rows)
    valid = jnp.broadcast_to((local_segment < seq_count).astype(jnp.float32)[:, None], (local_rows, LANES))

    normed_a, saved_a = open_attention(inputs, tables_a, *sizes)
    input_blocks = ring_gather(normed_a)
    query, key, value, attended, log_totals = attend(
        [matmul(block, qkv_full) for block in input_blocks], place_index, starts, cosine, sine
    )
    arrived_a, own_a = ring_scatter([times_transposed(block, out_full) for block in jnp.split(attended, size)])
    normed_f, d_out_f, saved_f, middle, out_a = open_feedforward(
        inputs, saved_a, arrived_a, own_a, cotangents, valid, tables_f, *sizes
    )
    feedforward_blocks = ring_gather(normed_f)
    grad_blocks = ring_gather(d_out_f)
    hidden_blocks, unit_grads = [], []
    for block, grad in zip(feedforward_blocks, grad_blocks):
        gate_up = matmul(block, gate_up_full)
        gate, up = gate_up[:, :units], gate_up[:, units:]
        hidden_blocks.append((gate / (1.0 + jnp.exp(-gate)) * up).astype(jnp.bfloat16))
        d_hidden = matmul(grad, down_full)
        sigmoid = 1.0 / (1.0 + jnp.exp(-gate))
        d_gate = (d_hidden * up * (sigmoid + gate * sigmoid * (1.0 - sigmoid))).astype(jnp.bfloat16)
        d_up = (d_hidden * gate * sigmoid).astype(jnp.bfloat16)
        unit_grads.append(jnp.concatenate([d_gate, d_up], axis=1))
    arrived_f, own_f = ring_scatter([times_transposed(hidden, down_full) for hidden in hidden_blocks])
    out_streams = finish(middle, saved_f, arrived_f, own_f, *sizes)
    arrived_n, own_n = ring_scatter([times_transposed(grads, gate_up_full) for grads in unit_grads])
    down_grad = product_sum(jnp.concatenate(grad_blocks), jnp.concatenate(hidden_blocks))
    gate_up_grad = product_sum(jnp.concatenate(feedforward_blocks), jnp.concatenate(unit_grads))

    middle_grad, d_out_a, d_branch_a, weight_sum_f, small_f = close_mix(
        True,
        [middle, saved_f, cotangents, arrived_n, own_n, arrived_f, own_f, valid, saved_a, out_a],
        tables_f,
        *sizes,
    )
    output_grads = ring_gather(d_out_a)
    attended_grads = [matmul(block, out_full).astype(jnp.bfloat16) for block in output_grads]
    d_qkv = attend_back([query, key, value, log_totals], attended_grads, place_index, starts, cosine, sine)
    arrived_i, own_i = ring_scatter([times_transposed(block, qkv_full) for block in jnp.split(d_qkv, size)])
    out_grad = product_sum(jnp.concatenate(output_grads), attended)
    qkv_grad = product_sum(jnp.concatenate(input_blocks), d_qkv)
    input_grad, weight_sum_a, small_a = close_mix(
        False, [inputs, saved_a, middle_grad, arrived_i, own_i, d_branch_a], tables_a, *sizes
    )

    def summed(weight_sum, small):
        height = width // LANES
        flat = sum_everywhere(
            jnp.concatenate([weight_sum.reshape(weight_sum.shape[0] * height, LANES)[: 2 * uses * height], small])
        )
        return mix_grads(flat[: 2 * uses * height].reshape(2 * uses, width), flat[2 * uses * height :], *sizes)

    static_f, weight_f, scale_f = summed(weight_sum_f, small_f)
    static_a, weight_a, scale_a = summed(weight_sum_a, small_a)
    query_grad, key_grad, value_grad = (
        in_order([part[:, i * query_weight.shape[1] : (i + 1) * query_weight.shape[1]] for part in qkv_grad])
        for i in range(3)
    )
    gate_grad, up_grad = (
        in_order([part[:, i * units : (i + 1) * units] for part in gate_up_grad]) for i in range(2)
    )
    shape = streams.shape
    return (
        out_streams.reshape(shape),
        input_grad.reshape(shape),
        query_grad,
        key_grad,
        value_grad,
        in_order(out_grad),
        gate_grad,
        up_grad,
        in_order(down_grad),
        jnp.stack([static_a, static_f]),
        jnp.stack([weight_a, weight_f]),
        jnp.stack([scale_a, scale_f]),
    )


def solution(mesh):
    placed = (
        P(("dp", "tensor"), None, None),
        P(("dp", "tensor"), None, None),
        P(),
        P(),
        P("dp", "tensor"),
        P("dp", "tensor"),
        P("dp", "tensor"),
        P("dp", "tensor"),
        P("dp", "tensor"),
        P("dp", "tensor"),
        P("dp", "tensor"),
        P(),
        P(),
        P(),
    )
    return jax.shard_map(
        per_device,
        mesh=mesh,
        in_specs=placed,
        out_specs=(
            P(("dp", "tensor"), None, None),
            P(("dp", "tensor"), None, None),
            P(None, "tensor"),
            P(None, "tensor"),
            P(None, "tensor"),
            P(None, "tensor"),
            P(None, "tensor"),
            P(None, "tensor"),
            P(None, "tensor"),
            P(),
            P(),
            P(),
        ),
        check_vma=False,
    )
```

time: 2770 us -> 1180 us (0.43)
  waiting for transfers between devices: 1670 us -> 494 us
  matrix products: 722 us -> 259 us
  Pallas kernels: 0 us -> 128 us
  other arithmetic: 181 us -> 109 us
  starting transfers between devices: 1.65 us -> 69.1 us
  blocking collectives: 41.3 us -> 0 us
    psum x2 -> x0, waiting for transfers between devices: 779 us -> none  [the longest x1 772 us: per_device(): lax.psum((query_weight_grad, key_weight_grad, value_weight_grad, out_weig...]
    reduce_scatter x6 -> x0, waiting for transfers between devices: 493 us -> none  [the longest x2 231 us: forward_pass(): lax.psum_scatter(times_transposed(hidden, down_full), 'tensor', scatter_d...]
    ppermute x0 -> x74, waiting for transfers between devices: none -> 492 us  [the longest x24 280 us: ring_shift(): lax.ppermute(block, 'tensor', [(i, (i + 1) % size) for i in range(size)])]
    dot_general x37 -> x0, matrix products: 443 us -> none  [the longest x7 171 us: mix_streams(): jnp.einsum('rji,rjd->rid', coeffs[:, :, 1:stream_count + 1], streams, pre...]
    all_gather x13 -> x4, waiting for transfers between devices: 396 us -> 0.03 us  [gather_rows(): lax.all_gather(jnp.concatenate(weights, axis=1), 'dp', axis=0, tiled=True)]
    pallas_call x0 -> x7, Pallas kernels: none -> 128 us  [the longest x2 55.3 us: close_mix(): pl.pallas_call(functools.partial(close_kernel, streams, uses, width, inne...]
    reduce_sum x27 -> x3, other arithmetic: 90.5 us -> 0.26 us  [the longest x1 0.21 us: mix_tables(): total = jnp.sum(weight, axis=0)]
    ppermute x0 -> x74, starting transfers between devices: none -> 69 us  [the longest x50 55.7 us: swap(): lax.ppermute(values, axis, [(i, i ^ 1 << bit) for i in range(lax.axis_siz...]
  transfers between devices with their start and end apart: 21 -> 78, of which waited for: 18 -> 36; matrix products, arithmetic and copies ran while one was open for 31% -> 37% of each run, Pallas kernels for 0% -> 11%
where the time goes in v1:
time: 1180 us; the launch traced here: 1170 us
  waiting for transfers between devices  494 us (42%)
  matrix products  259 us (22%)
  Pallas kernels  128 us (11%)
  other arithmetic  109 us (9%)
  local copies, waits for them, and re-layouts  97.3 us (8%)
  starting transfers between devices  69.1 us (6%)
  between operations  15.9 us (1%)
    ppermute x24, waiting for transfers between devices, ring_shift(): lax.ppermute(block, 'tensor', [(i, (i + 1) % size) for i in range(size)])  280 us
    ppermute x50, waiting for transfers between devices, swap(): lax.ppermute(values, axis, [(i, i ^ 1 << bit) for i in range(lax.axis_siz...  213 us
    dot_general x16, matrix products, times_transposed(): lax.dot_general(left, right, (((1,), (1,)), ((), ())), preferred_element_...  96.9 us
    dot_general x16, matrix products, matmul(): return jnp.dot(left, right, preferred_element_type=jnp.float32)  95.5 us
    dot_general x8, matrix products, transposed_times(): lax.dot_general(left, right, (((0,), (0,)), ((), ())), preferred_element_...  66.2 us
    ppermute x50, starting transfers between devices, swap(): lax.ppermute(values, axis, [(i, i ^ 1 << bit) for i in range(lax.axis_siz...  55.7 us
    pallas_call x2, Pallas kernels, close_mix(): pl.pallas_call(functools.partial(close_kernel, streams, uses, width, inne...  55.3 us
    unnamed x181, local copies, waits for them, and re-layouts  44 us
  transfers between devices with their start and end apart: 78, of which 36 were waited for; matrix products, arithmetic and copies ran while one was open for 37% of the time, Pallas kernels for 11%

profile of v1, /device:TPU:0, one launch (start us, length us, event | category | flops | bytes accessed | tf_op | source)
XLA Modules:
  0.0 1171.4 jit_solution(3113753043010082608)
XLA Ops:
  24.1 12.4 %open_attention.1 = (bf16[256,2048]{1,0:T(8,128)(2,1)S(1)}, f32[256,128]{1,0:T(8,128)S(1)}) custom-call(bf16[256,8192]{1,0:T(8,128)(2,1)} %bitcast.119, bf16[2048,128]{1,0:T(8,128)(2,1)S(1)} %pad.44.w_ref, f32[8,128]{1,0:T(8,128)S(1)} %concatenate.228.param_ref.refs_7_), custom_call_target="tpu_custom_call" | custom-call | tf_op jit(solution)/shard_map/open_attention/pallas_call | solution.py:455
  40.0 24.8 %collective-permute-done = bf16[256,2048]{1,0:T(8,128)(2,1)} collective-permute-done((bf16[256,2048]{1,0:T(8,128)(2,1)S(1)}, bf16[256,2048]{1,0:T(8,128)(2,1)}, u32[]{:S(2)}, u32[]{:S(2)}) %collective-permute-start) | collective-permute-done | bytes 1048608 | tf_op jit(solution)/shard_map/ppermute | solution.py:707
  67.4 23.9 %collective-permute-done.1 = bf16[256,2048]{1,0:T(8,128)(2,1)} collective-permute-done((bf16[256,2048]{1,0:T(8,128)(2,1)}, bf16[256,2048]{1,0:T(8,128)(2,1)}, u32[]{:S(2)}, u32[]{:S(2)}) %collective-permute-start.1) | collective-permute-done | bytes 1048608 | tf_op jit(solution)/shard_map/ppermute | solution.py:707
  121.3 14.4 %attend.1 = (bf16[1024,512]{1,0:T(8,128)(2,1)S(1)}, bf16[1024,512]{1,0:T(8,128)(2,1)S(1)}, bf16[1024,512]{1,0:T(8,128)(2,1)}, bf16[1024,512]{1,0:T(8,128)(2,1)}, f32[1024,512]{1,0:T(8,128)}) custom-call(s32[1]{0:T(128)} %bitcast.6.refs_0_, s32[1024,128]{1,0:T(8,128)S(1)} %broadcast_in_dim.82.refs_1_, f32[1024,128]{1,0:T(8,128)S(1)} %get-tuple-element.146.refs_2_, ...), custom_call_target="tpu_custom_call" | custom-call | tf_op jit(solution)/shard_map/attend/pallas_call | solution.py:672
  141.2 24.3 %collective-permute-done.3 = bf16[256,2048]{1,0:T(8,128)(2,1)S(1)} collective-permute-done((bf16[256,2048]{1,0:T(8,128)(2,1)S(1)}, bf16[256,2048]{1,0:T(8,128)(2,1)S(1)}, u32[]{:S(2)}, u32[]{:S(2)}) %collective-permute-start.3) | collective-permute-done | bytes 1048608 | tf_op jit(solution)/shard_map/ppermute | solution.py:707
  169.9 21.5 %collective-permute-done.4 = bf16[256,2048]{1,0:T(8,128)(2,1)S(1)} collective-permute-done((bf16[256,2048]{1,0:T(8,128)(2,1)S(1)}, bf16[256,2048]{1,0:T(8,128)(2,1)S(1)}, u32[]{:S(2)}, u32[]{:S(2)}) %collective-permute-start.4) | collective-permute-done | bytes 1048608 | tf_op jit(solution)/shard_map/ppermute | solution.py:707
  215.8 20.8 %open_feedforward.1 = (bf16[256,2048]{1,0:T(8,128)(2,1)S(1)}, bf16[256,2048]{1,0:T(8,128)(2,1)}, f32[256,128]{1,0:T(8,128)S(1)}, f32[256,8192]{1,0:T(8,128)}, f32[256,2048]{1,0:T(8,128)}) custom-call(bf16[256,8192]{1,0:T(8,128)(2,1)} %bitcast.120, f32[256,128]{1,0:T(8,128)S(1)} %get-tuple-element.32.saved_a_ref.refs_8_.refs_1_, ...), custom_call_target="tpu_custom_call" | custom-call | tf_op jit(solution)/shard_map/open_feedforward/pallas_call | solution.py:475
  240.7 25.1 %collective-permute-done.12 = bf16[256,2048]{1,0:T(8,128)(2,1)} collective-permute-done((bf16[256,2048]{1,0:T(8,128)(2,1)}, bf16[256,2048]{1,0:T(8,128)(2,1)}, u32[]{:S(2)}, u32[]{:S(2)}) %collective-permute-start.12) | collective-permute-done | bytes 1048608 | tf_op jit(solution)/shard_map/ppermute | solution.py:707
  269.6 18.6 %collective-permute-done.6 = bf16[256,2048]{1,0:T(8,128)(2,1)} collective-permute-done((bf16[256,2048]{1,0:T(8,128)(2,1)}, bf16[256,2048]{1,0:T(8,128)(2,1)}, u32[]{:S(2)}, u32[]{:S(2)}) %collective-permute-start.6) | collective-permute-done | bytes 1048608 | tf_op jit(solution)/shard_map/ppermute | solution.py:707
  289.5 21.2 %collective-permute-done.14 = bf16[256,2048]{1,0:T(8,128)(2,1)} collective-permute-done((bf16[256,2048]{1,0:T(8,128)(2,1)}, bf16[256,2048]{1,0:T(8,128)(2,1)}, u32[]{:S(2)}, u32[]{:S(2)}) %collective-permute-start.14) | collective-permute-done | bytes 1048608 | tf_op jit(solution)/shard_map/ppermute | solution.py:707
  317.5 15.7 %collective-permute-done.8 = bf16[256,2048]{1,0:T(8,128)(2,1)} collective-permute-done((bf16[256,2048]{1,0:T(8,128)(2,1)}, bf16[256,2048]{1,0:T(8,128)(2,1)}, u32[]{:S(2)}, u32[]{:S(2)}) %collective-permute-start.8) | collective-permute-done | bytes 1048608 | tf_op jit(solution)/shard_map/ppermute | solution.py:707
  335.7 19.8 %collective-permute-done.16 = bf16[256,2048]{1,0:T(8,128)(2,1)S(1)} collective-permute-done((bf16[256,2048]{1,0:T(8,128)(2,1)}, bf16[256,2048]{1,0:T(8,128)(2,1)S(1)}, u32[]{:S(2)}, u32[]{:S(2)}) %collective-permute-start.16) | collective-permute-done | bytes 1048608 | tf_op jit(solution)/shard_map/ppermute | solution.py:707
  356.7 12.6 %fusion.106 = f32[256,4096]{1,0:T(8,128)} fusion(bf16[256,2048]{1,0:T(8,128)(2,1)} %collective-permute-done.6, bf16[2048,4096]{1,0:T(8,128)(2,1)} %all-gather.9.cloned.1.call-done), kind=kOutput, calls=%fused_computation.276 | convolution fusion | flops 4294967296 | bytes 22020096 | tf_op jit(solution)/shard_map/dot_general | solution.py:20
  394.3 12.7 %fusion.107 = f32[256,4096]{1,0:T(8,128)} fusion(bf16[256,2048]{1,0:T(8,128)(2,1)} %collective-permute-done.8, bf16[2048,4096]{1,0:T(8,128)(2,1)} %all-gather.9.cloned.1.call-done), kind=kOutput, calls=%fused_computation.277 | convolution fusion | flops 4294967296 | bytes 22020096 | tf_op jit(solution)/shard_map/dot_general | solution.py:20
  452.7 12.3 %fusion.12 = f32[256,2048]{1,0:T(8,128)} fusion(bf16[2048,4096]{1,0:T(8,128)(2,1)} %all-gather.9.cloned.1.call-done, bf16[256,2048]{1,0:T(8,128)(2,1)} %get-tuple-element.111, bf16[256,2048]{1,0:T(8,128)(2,1)} %get-tuple-element.110), kind=kOutput, calls=%fused_computation.47 | convolution fusion | flops 4299161600 | bytes 20971520 | tf_op jit(solution)/shard_map/dot_general | solution.py:24
  480.3 12.2 %add_convert_fusion.5 = bf16[256,2048]{1,0:T(8,128)(2,1)} fusion(bf16[256,2048]{1,0:T(8,128)(2,1)} %collective-permute-done.13, bf16[2048,4096]{1,0:T(8,128)(2,1)} %all-gather.9.cloned.1.call-done, bf16[256,2048]{1,0:T(8,128)(2,1)} %get-tuple-element.107, bf16[256,2048]{1,0:T(8,128)(2,1)} %get-tuple-element.106), kind=kOutput, calls=%fused_computation.93 | convolution fusion | flops 4300734464 | bytes 20971520 | tf_op jit(solution)/shard_map/dot_general | solution.py:24
  509.5 20.5 %collective-permute-done.15 = bf16[256,2048]{1,0:T(8,128)(2,1)S(1)} collective-permute-done((bf16[256,2048]{1,0:T(8,128)(2,1)}, bf16[256,2048]{1,0:T(8,128)(2,1)S(1)}, u32[]{:S(2)}, u32[]{:S(2)}) %collective-permute-start.15) | collective-permute-done | bytes 1048608 | tf_op jit(solution)/shard_map/ppermute | solution.py:707
  532.2 12.3 %fusion.16.refs_4_ = f32[256,2048]{1,0:T(8,128)} fusion(bf16[2048,4096]{1,0:T(8,128)(2,1)} %all-gather.9.cloned.1.call-done, bf16[256,2048]{1,0:T(8,128)(2,1)} %get-tuple-element.105, bf16[256,2048]{1,0:T(8,128)(2,1)} %get-tuple-element.104), kind=kOutput, calls=%fused_computation.51 | convolution fusion | flops 4299161600 | bytes 20971520 | tf_op jit(solution)/shard_map/dot_general | solution.py:24
  552.5 22.4 %collective-permute-done.17.refs_3_ = bf16[256,2048]{1,0:T(8,128)(2,1)} collective-permute-done((bf16[256,2048]{1,0:T(8,128)(2,1)}, bf16[256,2048]{1,0:T(8,128)(2,1)}, u32[]{:S(2)}, u32[]{:S(2)}) %collective-permute-start.17) | collective-permute-done | bytes 1048608 | tf_op jit(solution)/shard_map/ppermute | solution.py:707
  574.9 29.8 %close_feedforward.1 = (f32[256,8192]{1,0:T(8,128)}, bf16[256,2048]{1,0:T(8,128)(2,1)S(1)}, f32[256,128]{1,0:T(8,128)S(1)}, f32[16,2048]{1,0:T(8,128)S(1)}, f32[8,128]{1,0:T(8,128)S(1)}) custom-call(f32[256,8192]{1,0:T(8,128)} %get-tuple-element.35.h_ref.refs_0_, f32[256,128]{1,0:T(8,128)S(1)} %get-tuple-element.36.saved_ref.refs_1_, ...), custom_call_target="tpu_custom_call" | custom-call | tf_op jit(solution)/shard_map/close_feedforward/pallas_call | solution.py:537
  616.0 17.9 %convolution_convert_fusion = bf16[1024,4096]{1,0:T(8,128)(2,1)} fusion(bf16[1024,2048]{1,0:T(8,128)(2,1)} %constant_dynamic-update-slice_fusion.8, s32[]{:T(128)S(6)} %select_n.230, bf16[256,2048]{1,0:T(8,128)(2,1)} %get-tuple-element.111, bf16[256,2048]{1,0:T(8,128)(2,1)} %get-tuple-element.110, bf16[256,2048]{1,0:T(8,128)(2,1)} %get-tuple-element.107, ...), kind=kOutput, calls=%fused_computation.14 | convolution fusion | flops 8661237760 | bytes 18874372 | tf_op jit(solution)/shard_map/dot_general | solution.py:30
  650.6 12.1 %collective-permute-done.72 = f32[200,128]{1,0:T(8,128)S(1)} collective-permute-done((f32[200,128]{1,0:T(8,128)S(1)}, f32[200,128]{1,0:T(8,128)S(1)}, u32[]{:S(2)}, u32[]{:S(2)}) %collective-permute-start.72) | collective-permute-done | bytes 102432 | tf_op jit(solution)/shard_map/ppermute | solution.py:727
  689.8 19.2 %collective-permute-done.55 = bf16[256,2048]{1,0:T(8,128)(2,1)S(1)} collective-permute-done((bf16[256,2048]{1,0:T(8,128)(2,1)S(1)}, bf16[256,2048]{1,0:T(8,128)(2,1)S(1)}, u32[]{:S(2)}, u32[]{:S(2)}) %collective-permute-start.55) | collective-permute-done | bytes 1048608 | tf_op jit(solution)/shard_map/ppermute | solution.py:727
  737.9 17.2 %attend_back.1 = bf16[1024,1536]{1,0:T(8,128)(2,1)} custom-call(s32[1]{0:T(128)} %bitcast.6.refs_0_, s32[1024,128]{1,0:T(8,128)S(1)} %copy-done.2, f32[1024,128]{1,0:T(8,128)S(1)} %get-tuple-element.146.refs_2_, f32[1024,128]{1,0:T(8,128)S(1)} %get-tuple-element.147.refs_3_, bf16[1024,512]{1,0:T(8,128)(2,1)S(1)} %copy-done.11, bf16[1024,512]{1,0:T(8,128)(2,1)} %copy-done.12, ...), custom_call_target="tpu_custom_call" | custom-call | tf_op jit(solution)/shard_map/attend_back/pallas_call | solution.py:690
  790.9 19.4 %convert_add_fusion = f32[1024,4096]{1,0:T(8,128)} fusion(bf16[1024,4096]{1,0:T(8,128)(2,1)} %collective-permute-done.44, bf16[1024,2048]{1,0:T(8,128)(2,1)} %constant_dynamic-update-slice_fusion.8, s32[]{:T(128)S(6)} %select_n.229, bf16[256,2048]{1,0:T(8,128)(2,1)} %get-tuple-element.111, bf16[256,2048]{1,0:T(8,128)(2,1)} %get-tuple-element.110, ...), kind=kOutput, calls=%fused_computation | convolution fusion | flops 8665432064 | bytes 35651588 | tf_op jit(solution)/shard_map/dot_general | solution.py:30
  825.3 38.8 %collective-permute-done.36 = bf16[128,512]{1,0:T(8,128)(2,1)S(1)} collective-permute-done((bf16[128,512]{1,0:T(8,128)(2,1)S(1)}, bf16[128,512]{1,0:T(8,128)(2,1)S(1)}, u32[]{:S(2)}, u32[]{:S(2)}) %collective-permute-start.36) | collective-permute-done | bytes 131104 | tf_op jit(solution)/shard_map/ppermute | solution.py:727
  872.4 37.4 %collective-permute-done.45 = bf16[256,4096]{1,0:T(8,128)(2,1)S(1)} collective-permute-done((bf16[256,4096]{1,0:T(8,128)(2,1)S(1)}, bf16[256,4096]{1,0:T(8,128)(2,1)S(1)}, u32[]{:S(2)}, u32[]{:S(2)}) %collective-permute-start.45) | collective-permute-done | bytes 2097184 | tf_op jit(solution)/shard_map/ppermute | solution.py:727
  919.1 12.5 %collective-permute-done.50 = bf16[128,4096]{1,0:T(8,128)(2,1)} collective-permute-done((bf16[128,4096]{1,0:T(8,128)(2,1)S(1)}, bf16[128,4096]{1,0:T(8,128)(2,1)}, u32[]{:S(2)}, u32[]{:S(2)}) %collective-permute-start.50) | collective-permute-done | bytes 1048608 | tf_op jit(solution)/shard_map/ppermute | solution.py:727
  962.6 25.5 %close_attention.1 = (bf16[256,8192]{1,0:T(8,128)(2,1)}, f32[16,2048]{1,0:T(8,128)S(1)}, f32[8,128]{1,0:T(8,128)S(1)}) custom-call(bf16[256,8192]{1,0:T(8,128)(2,1)} %bitcast.121, f32[256,128]{1,0:T(8,128)S(1)} %get-tuple-element.32.saved_a_ref.refs_8_.refs_1_, f32[256,8192]{1,0:T(8,128)} %get-tuple-element.40.refs_2_, ...), custom_call_target="tpu_custom_call" | custom-call | tf_op jit(solution)/shard_map/close_attention/pallas_call | solution.py:537
  989.6 24.2 %collective-permute-done.29 = bf16[256,1536]{1,0:T(8,128)(2,1)} collective-permute-done((bf16[256,1536]{1,0:T(8,128)(2,1)}, bf16[256,1536]{1,0:T(8,128)(2,1)}, u32[]{:S(2)}, u32[]{:S(2)}) %collective-permute-start.29) | collective-permute-done | bytes 786464 | tf_op jit(solution)/shard_map/ppermute | solution.py:727
  1068.2 16.7 %collective-permute-done.65 = f32[200,128]{1,0:T(8,128)S(1)} collective-permute-done((f32[200,128]{1,0:T(8,128)S(1)}, f32[200,128]{1,0:T(8,128)S(1)}, u32[]{:S(2)}, u32[]{:S(2)}) %collective-permute-start.65) | collective-permute-done | bytes 102432 | tf_op jit(solution)/shard_map/ppermute | solution.py:727
  1117.8 13.0 %fusion.2 = f32[2048,2048]{1,0:T(8,128)} fusion(bf16[1024,2048]{1,0:T(8,128)(2,1)} %collective-permute-done.63, bf16[512,2048]{1,0:T(8,128)(2,1)S(1)} %copy-done.25, bf16[512,2048]{1,0:T(8,128)(2,1)} %maximum_select_fusion.11, pred[]{:T(512)S(6)} %eq.24), kind=kLoop, calls=%fused_computation.12 | loop fusion | flops 58720256 | bytes 25165824 | tf_op jit(solution)/shard_map/convert_element_type | solution.py:771
  (517 shorter events, 524.4 us)
Async XLA Ops:
  7.2 84.3 %all-gather.5.cloned.1.call-start = ((), (), s32[]{:S(2)}) async-start(), calls=%async_computation | async-start | bytes 7077888 | tf_op jit(solution)/shard_map/all_gather | solution.py:801
  9.3 129.3 %all-gather.7.cloned.1.call-start = ((), (), s32[]{:S(2)}) async-start(), calls=%async_computation.1 | async-start | bytes 2359296 | tf_op jit(solution)/shard_map/all_gather | solution.py:801
  10.0 346.6 %all-gather.9.cloned.1.call-start = ((), (), s32[]{:S(2)}) async-start(), calls=%async_computation.2 | async-start | bytes 18874368 | tf_op jit(solution)/shard_map/all_gather | solution.py:801
  13.2 356.1 %all-gather.11.cloned.1.call-start = ((), (), s32[]{:S(2)}) async-start(), calls=%async_computation.3 | async-start | bytes 9437184 | tf_op jit(solution)/shard_map/all_gather | solution.py:801
  237.7 50.6 %collective-permute-start.6 = (bf16[256,2048]{1,0:T(8,128)(2,1)}, bf16[256,2048]{1,0:T(8,128)(2,1)}, u32[]{:S(2)}, u32[]{:S(2)}) collective-permute-start(bf16[256,2048]{1,0:T(8,128)(2,1)} %copy-done.5), channel_id=1, source_target_pairs={{0,1},{1,2},{2,3},{3,0},{4,5},{5,6},{6,7},{7,4},{8,9},{9,10},{10,1... | collective-permute-start | bytes 3145736 | tf_op jit(solution)/shard_map/ppermute | solution.py:707
  265.8 44.9 %collective-permute-start.14 = (bf16[256,2048]{1,0:T(8,128)(2,1)}, bf16[256,2048]{1,0:T(8,128)(2,1)}, u32[]{:S(2)}, u32[]{:S(2)}) collective-permute-start(bf16[256,2048]{1,0:T(8,128)(2,1)} %collective-permute-done.12), channel_id=1, source_target_pairs={{0,1},{1,2},{2,3},{3,0},{4,5},{5,6},{6,7},{7,4},{8,9},{9,10},{10,1... | collective-permute-start | bytes 3145736 | tf_op jit(solution)/shard_map/ppermute | solution.py:707
  288.2 44.9 %collective-permute-start.8 = (bf16[256,2048]{1,0:T(8,128)(2,1)}, bf16[256,2048]{1,0:T(8,128)(2,1)}, u32[]{:S(2)}, u32[]{:S(2)}) collective-permute-start(bf16[256,2048]{1,0:T(8,128)(2,1)} %collective-permute-done.6), channel_id=1, source_target_pairs={{0,1},{1,2},{2,3},{3,0},{4,5},{5,6},{6,7},{7,4},{8,9},{9,10},{10,1... | collective-permute-start | bytes 3145736 | tf_op jit(solution)/shard_map/ppermute | solution.py:707
  310.7 44.8 %collective-permute-start.16 = (bf16[256,2048]{1,0:T(8,128)(2,1)}, bf16[256,2048]{1,0:T(8,128)(2,1)S(1)}, u32[]{:S(2)}, u32[]{:S(2)}) collective-permute-start(bf16[256,2048]{1,0:T(8,128)(2,1)} %collective-permute-done.14), channel_id=1, source_target_pairs={{0,1},{1,2},{2,3},{3,0},{4,5},{5,6},{6,7},{7,4},{8,9},{9,10},{10,1... | collective-permute-start | bytes 3145736 | tf_op jit(solution)/shard_map/ppermute | solution.py:707
  333.2 84.4 %collective-permute-start.10 = (bf16[256,2048]{1,0:T(8,128)(2,1)}, bf16[256,2048]{1,0:T(8,128)(2,1)}, u32[]{:S(2)}, u32[]{:S(2)}) collective-permute-start(bf16[256,2048]{1,0:T(8,128)(2,1)} %collective-permute-done.8), channel_id=1, source_target_pairs={{0,1},{1,2},{2,3},{3,0},{4,5},{5,6},{6,7},{7,4},{8,9},{9,10},{10,1... | collective-permute-start | bytes 3145736 | tf_op jit(solution)/shard_map/ppermute | solution.py:707
  381.9 90.3 %collective-permute-start.7 = (bf16[256,2048]{1,0:T(8,128)(2,1)}, bf16[256,2048]{1,0:T(8,128)(2,1)}, u32[]{:S(2)}, u32[]{:S(2)}) collective-permute-start(bf16[256,2048]{1,0:T(8,128)(2,1)} %convolution_convert_fusion.6), channel_id=1, source_target_pairs={{0,1},{1,2},{2,3},{3,0},{4,5},{5,6},{6,7},{7,4},{8,9},{9,10},{10,1... | collective-permute-start | bytes 3145736 | tf_op jit(solution)/shard_map/ppermute | solution.py:707
  394.3 86.0 %collective-permute-start.13 = (bf16[256,2048]{1,0:T(8,128)(2,1)}, bf16[256,2048]{1,0:T(8,128)(2,1)}, u32[]{:S(2)}, u32[]{:S(2)}) collective-permute-start(bf16[256,2048]{1,0:T(8,128)(2,1)} %convolution_convert_fusion.3), channel_id=1, source_target_pairs={{0,1},{1,2},{2,3},{3,0},{4,5},{5,6},{6,7},{7,4},{8,9},{9,10},{10,1... | collective-permute-start | bytes 3145736 | tf_op jit(solution)/shard_map/ppermute | solution.py:707
  452.7 184.3 %collective-permute-start.54 = (bf16[1024,2048]{1,0:T(8,128)(2,1)}, bf16[1024,2048]{1,0:T(8,128)(2,1)}, u32[]{:S(2)}, u32[]{:S(2)}) collective-permute-start(bf16[1024,2048]{1,0:T(8,128)(2,1)} %convolution_convert_fusion.2), channel_id=1, source_target_pairs={{0,4},{4,0},{8,12},{12,8},{16,20},{20,16},{24,28},{28,24},{1,5},{5... | collective-permute-start | bytes 12582920 | tf_op jit(solution)/shard_map/ppermute | solution.py:727
  508.9 43.7 %collective-permute-start.11 = (bf16[256,2048]{1,0:T(8,128)(2,1)}, bf16[256,2048]{1,0:T(8,128)(2,1)S(1)}, u32[]{:S(2)}, u32[]{:S(2)}) collective-permute-start(bf16[256,2048]{1,0:T(8,128)(2,1)} %add_convert_fusion.6), channel_id=1, source_target_pairs={{0,1},{1,2},{2,3},{3,0},{4,5},{5,6},{6,7},{7,4},{8,9},{9,10},{10,1... | collective-permute-start | bytes 3145736 | tf_op jit(solution)/shard_map/ppermute | solution.py:707
  531.4 43.5 %collective-permute-start.17 = (bf16[256,2048]{1,0:T(8,128)(2,1)}, bf16[256,2048]{1,0:T(8,128)(2,1)}, u32[]{:S(2)}, u32[]{:S(2)}) collective-permute-start(bf16[256,2048]{1,0:T(8,128)(2,1)} %add_convert_fusion.4), channel_id=1, source_target_pairs={{0,1},{1,2},{2,3},{3,0},{4,5},{5,6},{6,7},{7,4},{8,9},{9,10},{10,1... | collective-permute-start | bytes 3145736 | tf_op jit(solution)/shard_map/ppermute | solution.py:707
  633.8 157.1 %collective-permute-start.44 = (bf16[1024,4096]{1,0:T(8,128)(2,1)}, bf16[1024,4096]{1,0:T(8,128)(2,1)}, u32[]{:S(2)}, u32[]{:S(2)}) collective-permute-start(bf16[1024,4096]{1,0:T(8,128)(2,1)} %convolution_convert_fusion), channel_id=1, source_target_pairs={{0,4},{4,0},{8,12},{12,8},{16,20},{20,16},{24,28},{28,24},{1,5},{5... | collective-permute-start | bytes 25165832 | tf_op jit(solution)/shard_map/ppermute | solution.py:727
  633.9 50.5 %collective-permute-start.18 = (bf16[256,2048]{1,0:T(8,128)(2,1)S(1)}, bf16[256,2048]{1,0:T(8,128)(2,1)}, u32[]{:S(2)}, u32[]{:S(2)}) collective-permute-start(bf16[256,2048]{1,0:T(8,128)(2,1)S(1)} %copy-done.9), channel_id=1, source_target_pairs={{0,1},{1,2},{2,3},{3,0},{4,5},{5,6},{6,7},{7,4},{8,9},{9,10},{10,1... | collective-permute-start | bytes 3145736 | tf_op jit(solution)/shard_map/ppermute | solution.py:707
  733.5 41.2 %collective-permute-start.58 = (bf16[256,2048]{1,0:T(8,128)(2,1)S(1)}, bf16[256,2048]{1,0:T(8,128)(2,1)}, u32[]{:S(2)}, u32[]{:S(2)}) collective-permute-start(bf16[256,2048]{1,0:T(8,128)(2,1)S(1)} %maximum_select_fusion.15), channel_id=1, source_target_pairs={{0,8},{4,12},{8,0},{12,4},{16,24},{20,28},{24,16},{28,20},{1,9},{5... | collective-permute-start | bytes 3145736 | tf_op jit(solution)/shard_map/ppermute | solution.py:727
  765.4 146.0 %collective-permute-start.24 = (bf16[1024,1536]{1,0:T(8,128)(2,1)}, bf16[1024,1536]{1,0:T(8,128)(2,1)}, u32[]{:S(2)}, u32[]{:S(2)}) collective-permute-start(bf16[1024,1536]{1,0:T(8,128)(2,1)} %convolution_convert_fusion.1), channel_id=1, source_target_pairs={{0,4},{4,0},{8,12},{12,8},{16,20},{20,16},{24,28},{28,24},{1,5},{5... | collective-permute-start | bytes 9437192 | tf_op jit(solution)/shard_map/ppermute | solution.py:727
  785.9 79.0 %collective-permute-start.22 = (bf16[256,2048]{1,0:T(8,128)(2,1)}, bf16[256,2048]{1,0:T(8,128)(2,1)}, u32[]{:S(2)}, u32[]{:S(2)}) collective-permute-start(bf16[256,2048]{1,0:T(8,128)(2,1)} %add_convert_fusion.3), channel_id=1, source_target_pairs={{0,1},{1,2},{2,3},{3,0},{4,5},{5,6},{6,7},{7,4},{8,9},{9,10},{10,1... | collective-permute-start | bytes 3145736 | tf_op jit(solution)/shard_map/ppermute | solution.py:707
  817.4 51.7 %collective-permute-start.49 = (bf16[256,4096]{1,0:T(8,128)(2,1)S(1)}, bf16[256,4096]{1,0:T(8,128)(2,1)S(1)}, u32[]{:S(2)}, u32[]{:S(2)}) collective-permute-start(bf16[256,4096]{1,0:T(8,128)(2,1)S(1)} %dynamic-slice_convert_fusion), channel_id=1, source_target_pairs={{0,16},{4,20},{8,24},{12,28},{16,0},{20,4},{24,8},{28,12},{1,17},{... | collective-permute-start | bytes 6291464 | tf_op jit(solution)/shard_map/ppermute | solution.py:727
  820.2 43.8 %collective-permute-start.36 = (bf16[128,512]{1,0:T(8,128)(2,1)S(1)}, bf16[128,512]{1,0:T(8,128)(2,1)S(1)}, u32[]{:S(2)}, u32[]{:S(2)}) collective-permute-start(bf16[128,512]{1,0:T(8,128)(2,1)S(1)} %dynamic-slice_convert_fusion.15), channel_id=1, source_target_pairs={{0,16},{4,20},{8,24},{12,28},{16,0},{20,4},{24,8},{28,12},{1,17},{... | collective-permute-start | bytes 393224 | tf_op jit(solution)/shard_map/ppermute | solution.py:727
  824.2 134.1 %collective-permute-start.41 = (bf16[128,512]{1,0:T(8,128)(2,1)S(1)}, bf16[128,512]{1,0:T(8,128)(2,1)S(1)}, u32[]{:S(2)}, u32[]{:S(2)}) collective-permute-start(bf16[128,512]{1,0:T(8,128)(2,1)S(1)} %add_convert_fusion.14), channel_id=1, source_target_pairs={{0,8},{4,12},{8,0},{12,4},{16,24},{20,28},{24,16},{28,20},{1,9},{5... | collective-permute-start | bytes 393224 | tf_op jit(solution)/shard_map/ppermute | solution.py:727
  864.1 45.8 %collective-permute-start.45 = (bf16[256,4096]{1,0:T(8,128)(2,1)S(1)}, bf16[256,4096]{1,0:T(8,128)(2,1)S(1)}, u32[]{:S(2)}, u32[]{:S(2)}) collective-permute-start(bf16[256,4096]{1,0:T(8,128)(2,1)S(1)} %dynamic-slice_convert_fusion.1), channel_id=1, source_target_pairs={{0,8},{4,12},{8,0},{12,4},{16,24},{20,28},{24,16},{28,20},{1,9},{5... | collective-permute-start | bytes 6291464 | tf_op jit(solution)/shard_map/ppermute | solution.py:727
  864.9 96.1 %collective-permute-start.37 = (bf16[128,512]{1,0:T(8,128)(2,1)S(1)}, bf16[128,512]{1,0:T(8,128)(2,1)S(1)}, u32[]{:S(2)}, u32[]{:S(2)}) collective-permute-start(bf16[128,512]{1,0:T(8,128)(2,1)S(1)} %add_convert_fusion.15), channel_id=1, source_target_pairs={{0,16},{4,20},{8,24},{12,28},{16,0},{20,4},{24,8},{28,12},{1,17},{... | collective-permute-start | bytes 393224 | tf_op jit(solution)/shard_map/ppermute | solution.py:727
  869.0 92.1 %collective-permute-start.23 = (bf16[256,2048]{1,0:T(8,128)(2,1)}, bf16[256,2048]{1,0:T(8,128)(2,1)S(1)}, u32[]{:S(2)}, u32[]{:S(2)}) collective-permute-start(bf16[256,2048]{1,0:T(8,128)(2,1)} %add_convert_fusion.2), channel_id=1, source_target_pairs={{0,1},{1,2},{2,3},{3,0},{4,5},{5,6},{6,7},{7,4},{8,9},{9,10},{10,1... | collective-permute-start | bytes 3145736 | tf_op jit(solution)/shard_map/ppermute | solution.py:707
  952.0 65.7 %collective-permute-start.52 = (bf16[256,4096]{1,0:T(8,128)(2,1)}, bf16[256,4096]{1,0:T(8,128)(2,1)}, u32[]{:S(2)}, u32[]{:S(2)}) collective-permute-start(bf16[256,4096]{1,0:T(8,128)(2,1)} %maximum_select_fusion.10), channel_id=1, source_target_pairs={{0,16},{4,20},{8,24},{12,28},{16,0},{20,4},{24,8},{28,12},{1,17},{... | collective-permute-start | bytes 6291464 | tf_op jit(solution)/shard_map/ppermute | solution.py:727
  954.3 59.5 %collective-permute-start.29 = (bf16[256,1536]{1,0:T(8,128)(2,1)}, bf16[256,1536]{1,0:T(8,128)(2,1)}, u32[]{:S(2)}, u32[]{:S(2)}) collective-permute-start(bf16[256,1536]{1,0:T(8,128)(2,1)} %dynamic-slice_convert_fusion.6), channel_id=1, source_target_pairs={{0,16},{4,20},{8,24},{12,28},{16,0},{20,4},{24,8},{28,12},{1,17},{... | collective-permute-start | bytes 2359304 | tf_op jit(solution)/shard_map/ppermute | solution.py:727
  958.3 66.1 %collective-permute-start.48 = (bf16[256,4096]{1,0:T(8,128)(2,1)}, bf16[256,4096]{1,0:T(8,128)(2,1)}, u32[]{:S(2)}, u32[]{:S(2)}) collective-permute-start(bf16[256,4096]{1,0:T(8,128)(2,1)} %maximum_select_fusion.9), channel_id=1, source_target_pairs={{0,8},{4,12},{8,0},{12,4},{16,24},{20,28},{24,16},{28,20},{1,9},{5... | collective-permute-start | bytes 6291464 | tf_op jit(solution)/shard_map/ppermute | solution.py:727
  961.0 156.8 %collective-permute-start.63 = (bf16[1024,2048]{1,0:T(8,128)(2,1)}, bf16[1024,2048]{1,0:T(8,128)(2,1)}, u32[]{:S(2)}, u32[]{:S(2)}) collective-permute-start(bf16[1024,2048]{1,0:T(8,128)(2,1)} %pad_maximum_fusion.3), channel_id=1, source_target_pairs={{0,4},{4,0},{8,12},{12,8},{16,20},{20,16},{24,28},{28,24},{1,5},{5... | collective-permute-start | bytes 12582920 | tf_op jit(solution)/shard_map/ppermute | solution.py:727
  961.2 94.0 %collective-permute-start.42 = (bf16[256,512]{1,0:T(8,128)(2,1)S(1)}, bf16[256,512]{1,0:T(8,128)(2,1)}, u32[]{:S(2)}, u32[]{:S(2)}) collective-permute-start(bf16[256,512]{1,0:T(8,128)(2,1)S(1)} %maximum_select_fusion.22), channel_id=1, source_target_pairs={{0,16},{4,20},{8,24},{12,28},{16,0},{20,4},{24,8},{28,12},{1,17},{... | collective-permute-start | bytes 786440 | tf_op jit(solution)/shard_map/ppermute | solution.py:727
  1038.5 106.9 %collective-permute-start.53 = (bf16[1024,4096]{1,0:T(8,128)(2,1)}, bf16[1024,4096]{1,0:T(8,128)(2,1)}, u32[]{:S(2)}, u32[]{:S(2)}) collective-permute-start(bf16[1024,4096]{1,0:T(8,128)(2,1)} %pad_maximum_fusion), channel_id=1, source_target_pairs={{0,4},{4,0},{8,12},{12,8},{16,20},{20,16},{24,28},{28,24},{1,5},{5... | collective-permute-start | bytes 25165832 | tf_op jit(solution)/shard_map/ppermute | solution.py:727
  1093.3 41.8 %collective-permute-start.33 = (bf16[1024,1536]{1,0:T(8,128)(2,1)}, bf16[1024,1536]{1,0:T(8,128)(2,1)}, u32[]{:S(2)}, u32[]{:S(2)}) collective-permute-start(bf16[1024,1536]{1,0:T(8,128)(2,1)} %pad_maximum_fusion.1), channel_id=1, source_target_pairs={{0,4},{4,0},{8,12},{12,8},{16,20},{20,16},{24,28},{28,24},{1,5},{5... | collective-permute-start | bytes 9437192 | tf_op jit(solution)/shard_map/ppermute | solution.py:727
  (128 other events, 1999.0 us)
Sparse Core Ops, SparseCore 0:
  10.5 48.2 all-gather.4
  60.7 27.8 all-gather.6
  91.0 89.8 all-gather.8
  182.7 54.3 all-gather.10

commit v2 on v1

--- a/solution.py
+++ b/solution.py
@@ -32,6 +32,14 @@
     )
 
 
+def anywhere(count):
+    return [pl.BlockSpec(memory_space=pl.ANY)] * count
+
+
+def cost(microseconds):
+    return pl.CostEstimate(flops=int(microseconds * 1e9), bytes_accessed=0, transcendentals=0)
+
+
 def lanes_of(rows):
     return lax.broadcasted_iota(jnp.int32, (rows, LANES), 1)
 
@@ -63,7 +71,7 @@
     return values if shift == 0 else pltpu.roll(values, shift, 1)
 
 
-def coefficients(projected, means, rsqrts, param_ref, streams, uses, parts, centred):
+def coefficients(projected, means, rsqrts, param_ref, sums_ref, streams, uses, parts):
     rows = projected[0].shape[0]
     lane = lanes_of(rows)
     gathered = jnp.zeros((rows, LANES), jnp.float32)
@@ -71,8 +79,8 @@
         total = projected[j]
         for part in range(1, parts):
             total = total + rolled(projected[j], -part * uses)
-        if not centred:
-            total = total - means[j] * param_ref[2:3, :]
+        if sums_ref is not None:
+            total = total - means[j] * sums_ref[0:1, :]
         total = total * rsqrts[j]
         inside = (lane >= j * uses) & (lane < (j + 1) * uses)
         gathered = jnp.where(inside, rolled(total, j * uses), gathered)
@@ -111,10 +119,26 @@
     return centre_stats(total, lambda start: entering_ref[rows, start : start + CHUNK], width)
 
 
-def open_attention_kernel(streams, uses, width, x_ref, w_ref, param_ref, normed_ref, saved_ref, raw_ref, entering_ref):
+def weight_parts(w_ref, parts_ref, sums_ref, uses, parts):
+    @pl.when(pl.program_id(0) == 0)
+    def _():
+        rest = w_ref[...]
+        sums_ref[0:1, :] = jnp.sum(rest, axis=0, keepdims=True)
+        total = None
+        for part in range(parts):
+            one = rest.astype(jnp.bfloat16).astype(jnp.float32)
+            rest = rest - one
+            total = one if total is None else total + rolled(one, part * uses)
+        parts_ref[...] = total.astype(jnp.bfloat16)
+
+
+def open_attention_kernel(
+    streams, uses, width, x_ref, w_ref, param_ref, normed_ref, saved_ref, raw_ref, entering_ref, parts_ref, sums_ref
+):
     block = x_ref.shape[0]
+    weight_parts(w_ref, parts_ref, sums_ref, uses, 3)
     stacked = jnp.concatenate([x_ref[:, j * width : (j + 1) * width] for j in range(streams)], axis=0)
-    raw_ref[...] = jnp.dot(stacked, w_ref[...], preferred_element_type=jnp.float32)
+    raw_ref[...] = jnp.dot(stacked, parts_ref[...], preferred_element_type=jnp.float32)
 
     def body(index, carry):
         first = pl.multiple_of(index * GROUP, GROUP)
@@ -133,7 +157,7 @@
             means.append(mean)
             rsqrts.append(rsqrt)
             projected.append(raw_ref[pl.ds(pl.multiple_of(j * block + first, GROUP), GROUP), :])
-        gathered, bent, coeffs = coefficients(projected, means, rsqrts, param_ref, streams, uses, 3, False)
+        gathered, bent, coeffs = coefficients(projected, means, rsqrts, param_ref, sums_ref, streams, uses, 3)
         mean_e, rsqrt_e = entering_norm(read, coeffs, streams, uses, width, entering_ref, rows)
         for start in range(0, width, CHUNK):
             normed_ref[rows, start : start + CHUNK] = (
@@ -149,9 +173,10 @@
     streams, uses, width,
     x_ref, saved_a_ref, arrived_ref, partial_ref, g_ref, valid_ref, w_ref, param_ref,
     normed_ref, grad_ref, saved_ref, h_ref, out_ref,
-    high_ref, low_ref, raw_ref, entering_ref, stats_ref,
+    high_ref, low_ref, raw_ref, entering_ref, stats_ref, parts_ref, sums_ref,
 ):
     block = x_ref.shape[0]
+    weight_parts(w_ref, parts_ref, sums_ref, uses, 2)
     count = streams * uses
 
     def first_pass(index, carry):
@@ -192,8 +217,8 @@
         return carry
 
     lax.fori_loop(0, block // GROUP, first_pass, 0)
-    raw_ref[...] = jnp.dot(high_ref[...], w_ref[...], preferred_element_type=jnp.float32) + jnp.dot(
-        low_ref[...], w_ref[...], preferred_element_type=jnp.float32
+    raw_ref[...] = jnp.dot(high_ref[...], parts_ref[...], preferred_element_type=jnp.float32) + jnp.dot(
+        low_ref[...], parts_ref[...], preferred_element_type=jnp.float32
     )
 
     def second_pass(index, carry):
@@ -203,7 +228,7 @@
         means = [column(stats, j) for j in range(streams)]
         rsqrts = [column(stats, streams + j) for j in range(streams)]
         projected = [raw_ref[pl.ds(pl.multiple_of(j * block + first, GROUP), GROUP), :] for j in range(streams)]
-        gathered, bent, coeffs = coefficients(projected, means, rsqrts, param_ref, streams, uses, 2, True)
+        gathered, bent, coeffs = coefficients(projected, means, rsqrts, param_ref, None, streams, uses, 2)
 
         def read(j, start):
             return h_ref[rows, j * width + start : j * width + start + CHUNK]
@@ -242,7 +267,9 @@
     lax.fori_loop(0, h_ref.shape[0] // GROUP, body, 0)
 
 
-def close_kernel(streams, uses, width, inner, *refs):
+def close_kernel(streams, uses, width, inner, kept, *refs):
+    inputs = 12 if inner else 8
+    refs = refs[:inputs] + refs[inputs + kept :]
     if inner:
         (h_ref, saved_ref, g_ref, arrived_ref, partial_ref, arrived_f_ref, partial_f_ref, valid_ref, saved_a_ref,
          out_a_ref, wt_ref, param_ref, grad_ref, below_ref, branch_ref, weight_ref, small_ref,
@@ -429,23 +456,19 @@
 
 def mix_tables(static, weight, scale):
     streams, uses = static.shape
-    width = weight.shape[0]
     high = rounded(weight)
     middle = rounded(weight - high)
-    low = rounded(weight - high - middle)
-    forward = jnp.pad(jnp.concatenate([high, middle, low], axis=1), ((0, 0), (0, LANES - 3 * uses))).astype(jnp.bfloat16)
+    forward = jnp.pad(weight, ((0, 0), (0, LANES - uses)))
     tall = [jnp.tile(part.T, (streams, 1)) for part in (high, high, middle)]
     backward = jnp.pad(jnp.concatenate(tall, axis=0), ((0, LANES - 3 * streams * uses), (0, 0))).astype(jnp.bfloat16)
-    total = jnp.sum(weight, axis=0)
     count = streams * uses
 
     def row(values):
         return jnp.pad(values, (0, LANES - values.shape[0]))[None]
 
-    params = jnp.concatenate(
-        [row(static.reshape(count)), row(jnp.tile(scale, streams)), row(total), row(jnp.tile(total, streams)), jnp.zeros((4, LANES), jnp.float32)]
-    )
-    return forward, backward, params
+    constants = jnp.concatenate([row(static.reshape(count)), row(jnp.tile(scale, streams)), jnp.zeros((6, LANES), jnp.float32)])
+    with_sums = jnp.concatenate([constants[:3], row(jnp.tile(jnp.sum(weight, axis=0), streams)), constants[4:]])
+    return forward, backward, constants, with_sums
 
 
 def open_attention(x, tables, streams, uses):
@@ -458,8 +481,14 @@
         in_specs=specs_for(arrays, block, {1, 2}),
         out_specs=[pl.BlockSpec((block, width), lambda i: (i, 0)), pl.BlockSpec((block, LANES), lambda i: (i, 0))],
         out_shape=[jax.ShapeDtypeStruct((rows, width), jnp.bfloat16), jax.ShapeDtypeStruct((rows, LANES), jnp.float32)],
-        scratch_shapes=[pltpu.VMEM((streams * block, LANES), jnp.float32), pltpu.VMEM((block, width), jnp.float32)],
+        scratch_shapes=[
+            pltpu.VMEM((streams * block, LANES), jnp.float32),
+            pltpu.VMEM((block, width), jnp.float32),
+            pltpu.VMEM((width, LANES), jnp.bfloat16),
+            pltpu.VMEM((8, LANES), jnp.float32),
+        ],
         compiler_params=PARAMS,
+        cost_estimate=cost(13),
         name="open_attention",
     )(*arrays)
 
@@ -490,8 +519,11 @@
             pltpu.VMEM((streams * block, LANES), jnp.float32),
             pltpu.VMEM((block, width), jnp.float32),
             pltpu.VMEM((block, LANES), jnp.float32),
+            pltpu.VMEM((width, LANES), jnp.bfloat16),
+            pltpu.VMEM((8, LANES), jnp.float32),
         ],
         compiler_params=PARAMS,
+        cost_estimate=cost(21),
         name="open_feedforward",
     )(*arrays)
 
@@ -507,15 +539,16 @@
         out_specs=pl.BlockSpec((block, streams * width), lambda i: (i, 0)),
         out_shape=jax.ShapeDtypeStruct((rows, streams * width), jnp.bfloat16),
         compiler_params=PARAMS,
+        cost_estimate=cost(8),
         name="finish",
     )(*arrays)
 
 
-def close_mix(inner, arrays, tables, streams, uses):
+def close_mix(inner, arrays, tables, streams, uses, tokens=()):
     h = arrays[0]
     rows, width = h.shape[0], h.shape[1] // streams
     block = rows_block(rows)
-    arrays = [*arrays, tables[1], tables[2]]
+    arrays = [*arrays, tables[1], tables[3]]
     last = len(arrays)
 
     def by_rows(columns):
@@ -535,9 +568,9 @@
     out_specs += [fixed(16, width), fixed(8, LANES)]
     out_shape += [jax.ShapeDtypeStruct((16, width), jnp.float32), jax.ShapeDtypeStruct((8, LANES), jnp.float32)]
     return pl.pallas_call(
-        functools.partial(close_kernel, streams, uses, width, inner),
+        functools.partial(close_kernel, streams, uses, width, inner, len(tokens)),
         grid=(rows // block,),
-        in_specs=specs_for(arrays, block, {last - 2, last - 1}),
+        in_specs=specs_for(arrays, block, {last - 2, last - 1}) + anywhere(len(tokens)),
         out_specs=out_specs,
         out_shape=out_shape,
         scratch_shapes=[
@@ -549,8 +582,9 @@
             pltpu.VMEM((2, GROUP, LANES), jnp.float32),
         ],
         compiler_params=PARAMS,
+        cost_estimate=cost(30 if inner else 25),
         name="close_feedforward" if inner else "close_attention",
-    )(*arrays)
+    )(*arrays, *tokens)
 
 
 def mix_grads(weight_sum, small, streams, uses):
@@ -614,10 +648,10 @@
         out_ref[step * block : (step + 1) * block, :] = attended_ref[rows, :]
 
 
-def attend_back_kernel(size, *refs):
+def attend_back_kernel(size, kept, *refs):
     mine_ref, start_ref, cosine_ref, sine_ref, q_ref, k_ref, v_ref, log_ref = refs[:8]
     grads = refs[8 : 8 + size]
-    dqkv_ref, d_out_ref, dq_ref, dk_ref, dv_ref = refs[8 + size :]
+    dqkv_ref, d_out_ref, dq_ref, dk_ref, dv_ref = refs[8 + size + kept :]
     mine = mine_ref[0]
     head, heads = pl.program_id(0), pl.num_programs(0)
     block = grads[0].shape[0]
@@ -679,27 +713,193 @@
         out_shape=[flat] * 4 + [jax.ShapeDtypeStruct(flat.shape, jnp.float32)],
         scratch_shapes=[pltpu.VMEM((total, HEAD_DIM), jnp.bfloat16)],
         compiler_params=PARAMS,
+        cost_estimate=cost(15),
         name="attend",
     )(mine, starts, cosine, sine, *[raw for raw in raw_blocks for _ in range(3)])
 
 
-def attend_back(heads_kept, grad_blocks, mine, starts, cosine, sine):
+def attend_back(heads_kept, grad_blocks, mine, starts, cosine, sine, tokens):
     size, block = len(grad_blocks), grad_blocks[0].shape[0]
     total, columns = heads_kept[0].shape
     heads = columns // HEAD_DIM
     return pl.pallas_call(
-        functools.partial(attend_back_kernel, size),
+        functools.partial(attend_back_kernel, size, len(tokens)),
         grid=(heads,),
         in_specs=[pl.BlockSpec(memory_space=pltpu.SMEM)]
         + [whole_spec(a.shape) for a in (starts, cosine, sine)]
         + [head_spec(total)] * 4
-        + [head_spec(block)] * size,
+        + [head_spec(block)] * size
+        + anywhere(len(tokens)),
         out_specs=whole_spec((total, 3 * columns)),
         out_shape=jax.ShapeDtypeStruct((total, 3 * columns), jnp.bfloat16),
         scratch_shapes=[pltpu.VMEM((total, HEAD_DIM), jnp.bfloat16)] + [pltpu.VMEM((total, HEAD_DIM), jnp.float32)] * 3,
         compiler_params=PARAMS,
+        cost_estimate=cost(18),
         name="attend_back",
-    )(mine, starts, cosine, sine, *heads_kept, *grad_blocks)
+    )(mine, starts, cosine, sine, *heads_kept, *grad_blocks, *tokens)
+
+
+UNIT_TILE = 512
+
+
+def forward_units_kernel(kept, *refs):
+    x_ref, gate_w_ref, up_w_ref, down_w_ref = refs[:4]
+    gate_ref, up_ref, partial_ref, rows_ref, hidden_ref = refs[4 + kept : 9 + kept]
+    x = x_ref[...]
+    gate, up = matmul(x, gate_w_ref[...]), matmul(x, up_w_ref[...])
+    gate_ref[...] = gate
+    up_ref[...] = up
+    hidden = (gate / (1.0 + jnp.exp(-gate)) * up).astype(jnp.bfloat16)
+    hidden_ref[...] = hidden
+    part = times_transposed(hidden, down_w_ref[...])
+
+    @pl.when(pl.program_id(0) == 0)
+    def _():
+        partial_ref[...] = part
+        rows_ref[...] = x
+
+    @pl.when(pl.program_id(0) > 0)
+    def _():
+        partial_ref[...] += part
+
+
+def backward_units_kernel(kept, *refs):
+    d_ref, gate_ref, up_ref, down_w_ref, gate_w_ref, up_w_ref = refs[:6]
+    partial_ref, rows_ref, d_gate_ref, d_up_ref = refs[6 + kept : 10 + kept]
+    d_out = d_ref[...]
+    d_hidden = matmul(d_out, down_w_ref[...])
+    gate = gate_ref[...]
+    sigmoid = 1.0 / (1.0 + jnp.exp(-gate))
+    d_gate = (d_hidden * up_ref[...] * (sigmoid + gate * sigmoid * (1.0 - sigmoid))).astype(jnp.bfloat16)
+    d_up = (d_hidden * gate * sigmoid).astype(jnp.bfloat16)
+    d_gate_ref[...] = d_gate
+    d_up_ref[...] = d_up
+    part = times_transposed(d_gate, gate_w_ref[...]) + times_transposed(d_up, up_w_ref[...])
+
+    @pl.when(pl.program_id(0) == 0)
+    def _():
+        partial_ref[...] = part
+        rows_ref[...] = d_out
+
+    @pl.when(pl.program_id(0) > 0)
+    def _():
+        partial_ref[...] += part
+
+
+def forward_units(step, size, x, gate_up, down, filled, passed, tokens):
+    rows, width = x.shape
+    units = down.shape[1]
+    tile = min(UNIT_TILE, units)
+    tiles = units // tile
+    weight = functools.partial(pl.BlockSpec, (width, tile))
+    kept = len(filled) + len(passed) + len(tokens)
+    arrays = [x, gate_up, gate_up, down]
+    outs = pl.pallas_call(
+        functools.partial(forward_units_kernel, kept),
+        grid=(tiles,),
+        in_specs=[
+            pl.BlockSpec((rows, width), lambda i: (0, 0)),
+            weight(lambda i: (0, i)),
+            weight(lambda i: (0, tiles + i)),
+            weight(lambda i: (0, i)),
+        ]
+        + anywhere(kept),
+        out_specs=[
+            pl.BlockSpec((rows, tile), lambda i: (0, i)),
+            pl.BlockSpec((rows, tile), lambda i: (0, i)),
+            pl.BlockSpec((rows, width), lambda i: (0, 0)),
+            pl.BlockSpec((rows, width), lambda i: (step, 0)),
+            pl.BlockSpec((rows, tile), lambda i: (step, i)),
+        ]
+        + anywhere(len(passed)),
+        out_shape=[
+            jax.ShapeDtypeStruct((rows, units), jnp.float32),
+            jax.ShapeDtypeStruct((rows, units), jnp.float32),
+            jax.ShapeDtypeStruct((rows, width), jnp.float32),
+            jax.ShapeDtypeStruct((size * rows, width), jnp.bfloat16),
+            jax.ShapeDtypeStruct((size * rows, units), jnp.bfloat16),
+        ]
+        + [jax.ShapeDtypeStruct(a.shape, a.dtype) for a in passed],
+        input_output_aliases={
+            **{4 + k: 3 + k for k in range(len(filled))},
+            **{4 + len(filled) + k: 5 + k for k in range(len(passed))},
+        },
+        compiler_params=PARAMS,
+        cost_estimate=cost(9),
+        name="forward_units",
+    )(*arrays, *filled, *passed, *tokens)
+    return outs[0], outs[1], outs[2], outs[3:5], outs[5:]
+
+
+def backward_units(step, size, d_out, gate, up, gate_up, down, filled, tokens):
+    rows, width = d_out.shape
+    units = down.shape[1]
+    tile = min(UNIT_TILE, units)
+    tiles = units // tile
+    weight = functools.partial(pl.BlockSpec, (width, tile))
+    kept = len(filled) + len(tokens)
+    by_tile = pl.BlockSpec((rows, tile), lambda i: (0, i))
+    outs = pl.pallas_call(
+        functools.partial(backward_units_kernel, kept),
+        grid=(tiles,),
+        in_specs=[
+            pl.BlockSpec((rows, width), lambda i: (0, 0)),
+            by_tile,
+            by_tile,
+            weight(lambda i: (0, i)),
+            weight(lambda i: (0, i)),
+            weight(lambda i: (0, tiles + i)),
+        ]
+        + anywhere(kept),
+        out_specs=[
+            pl.BlockSpec((rows, width), lambda i: (0, 0)),
+            pl.BlockSpec((rows, width), lambda i: (step, 0)),
+            pl.BlockSpec((rows, tile), lambda i: (step, i)),
+            pl.BlockSpec((rows, tile), lambda i: (step, i)),
+        ],
+        out_shape=[
+            jax.ShapeDtypeStruct((rows, width), jnp.float32),
+            jax.ShapeDtypeStruct((size * rows, width), jnp.bfloat16),
+            jax.ShapeDtypeStruct((size * rows, units), jnp.bfloat16),
+            jax.ShapeDtypeStruct((size * rows, units), jnp.bfloat16),
+        ],
+        input_output_aliases={6 + k: 1 + k for k in range(len(filled))},
+        compiler_params=PARAMS,
+        cost_estimate=cost(10),
+        name="backward_units",
+    )(d_out, gate, up, down, gate_up, gate_up, *filled, *tokens)
+    return outs[0], outs[1:]
+
+
+def assemble_kernel(count, pieces, table_ref, *refs):
+    out_ref = refs[-1]
+    for k in range(count):
+
+        @pl.when(pl.program_id(0) // pieces == k)
+        def _(k=k):
+            out_ref[...] = refs[k][...].astype(jnp.float32)
+
+
+def assemble(arrays, part, columns, table):
+    count = len(arrays)
+    pieces = table.shape[0] // count
+    rows = arrays[0].shape[0] // pieces
+    return pl.pallas_call(
+        functools.partial(assemble_kernel, count, pieces),
+        grid_spec=pltpu.PrefetchScalarGridSpec(
+            num_scalar_prefetch=1,
+            grid=(count * pieces,),
+            in_specs=[
+                pl.BlockSpec((rows, columns), lambda i, t, k=k: (jnp.clip(i - k * pieces, 0, pieces - 1), part))
+                for k in range(count)
+            ],
+            out_specs=pl.BlockSpec((rows, columns), lambda i, t: (t[i], 0)),
+        ),
+        out_shape=jax.ShapeDtypeStruct((count * arrays[0].shape[0], columns), jnp.float32),
+        compiler_params=PARAMS,
+        cost_estimate=cost(8 * columns / 2048),
+        name="assemble",
+    )(table, *arrays)
 
 
 def ring_shift(block):
@@ -715,7 +915,7 @@
 
 
 def ring_scatter(partials):
-    total = partials[1]
+    total = partials[1 % len(partials)]
     for step in range(2, len(partials) + 1):
         arrived = ring_shift(total.astype(jnp.bfloat16))
         own = partials[step % len(partials)]
@@ -731,33 +931,56 @@
     return (lax.axis_index(axis) >> bit) & 1
 
 
-def halves_by(bit_value, mine, other):
-    return jnp.where(
-        bit_value == 0, jnp.concatenate([mine, other], axis=0), jnp.concatenate([other, mine], axis=0)
-    )
-
-
-def product_sum(left, right):
+def axis_orders():
     bits = (lax.axis_size("dp") - 1).bit_length()
-    half = left.shape[1] // 2
+    return list(range(1, bits)), list(range(bits - 1, 0, -1))
+
+
+def core_products(pairs):
+    half = pairs[0][0].shape[1] // 2
     core = bit_of("dp", 0)
-    away = transposed_times(lax.dynamic_slice_in_dim(left, (1 - core) * half, half, 1), right)
-    arrived = swap(away.astype(jnp.bfloat16), "dp", 0)
-    total = transposed_times(lax.dynamic_slice_in_dim(left, core * half, half, 1), right)
-    total = total + arrived.astype(jnp.float32)
-    gathered = []
-    for part, order in zip(jnp.split(total, 2), (list(range(1, bits)), list(range(bits - 1, 0, -1)))):
-        for bit in order:
-            rows, which = part.shape[0] // 2, bit_of("dp", bit)
-            away = lax.dynamic_slice_in_dim(part, (1 - which) * rows, rows).astype(jnp.bfloat16)
-            arrived = swap(away, "dp", bit)
-            part = lax.dynamic_slice_in_dim(part, which * rows, rows) + arrived.astype(jnp.float32)
-        part = part.astype(jnp.bfloat16)
-        for bit in reversed(order):
-            part = halves_by(bit_of("dp", bit), part, swap(part, "dp", bit))
-        gathered.append(part)
-    mine = jnp.concatenate(gathered)
-    return mine, swap(mine, "dp", 0)
+
+    def products(which):
+        each = [
+            transposed_times(lax.dynamic_slice_in_dim(left, which * half, half, 1), right) for left, right in pairs
+        ]
+        return each[0] if len(each) == 1 else jnp.concatenate(each, axis=1)
+
+    arrived = swap(products(1 - core).astype(jnp.bfloat16), "dp", 0)
+    return products(core) + arrived.astype(jnp.float32)
+
+
+def butterfly(part, order):
+    marks = []
+    for bit in order:
+        rows, which = part.shape[0] // 2, bit_of("dp", bit)
+        away = lax.dynamic_slice_in_dim(part, (1 - which) * rows, rows).astype(jnp.bfloat16)
+        arrived = swap(away, "dp", bit)
+        marks += [away, arrived]
+        part = lax.dynamic_slice_in_dim(part, which * rows, rows) + arrived.astype(jnp.float32)
+    part = part.astype(jnp.bfloat16)
+    for bit in reversed(order):
+        part = jnp.concatenate([part, swap(part, "dp", bit)])
+    return part, marks
+
+
+def piece_rows(orders):
+    levels = len(orders[0])
+    entries = []
+    for flip in (0, 1):
+        core = bit_of("dp", 0) ^ flip
+        for k, order in enumerate(orders):
+            for position in range(1 << levels):
+                row = jnp.int32(0)
+                for level, bit in enumerate(order):
+                    digit = (position >> (levels - 1 - level)) & 1
+                    row = row * 2 + (bit_of("dp", bit) ^ digit)
+                entries.append((core * len(orders) + k) * (1 << levels) + row)
+    return jnp.stack(entries).astype(jnp.int32)
+
+
+def with_partner(parts):
+    return [*parts, *(swap(part, "dp", 0) for part in parts)]
 
 
 def sum_everywhere(values):
@@ -765,10 +988,6 @@
         for bit in range((lax.axis_size(axis) - 1).bit_length()):
             values = values + swap(values, axis, bit)
     return values
-
-
-def in_order(halves):
-    return halves_by(bit_of("dp", 0), *halves).astype(jnp.float32)
 
 
 def segments_from(slot_lengths, group_rows):
@@ -851,54 +1070,89 @@
         inputs, saved_a, arrived_a, own_a, cotangents, valid, tables_f, *sizes
     )
     feedforward_blocks = ring_gather(normed_f)
-    grad_blocks = ring_gather(d_out_f)
-    hidden_blocks, unit_grads = [], []
-    for block, grad in zip(feedforward_blocks, grad_blocks):
-        gate_up = matmul(block, gate_up_full)
-        gate, up = gate_up[:, :units], gate_up[:, units:]
-        hidden_blocks.append((gate / (1.0 + jnp.exp(-gate)) * up).astype(jnp.bfloat16))
-        d_hidden = matmul(grad, down_full)
-        sigmoid = 1.0 / (1.0 + jnp.exp(-gate))
-        d_gate = (d_hidden * up * (sigmoid + gate * sigmoid * (1.0 - sigmoid))).astype(jnp.bfloat16)
-        d_up = (d_hidden * gate * sigmoid).astype(jnp.bfloat16)
-        unit_grads.append(jnp.concatenate([d_gate, d_up], axis=1))
-    arrived_f, own_f = ring_scatter([times_transposed(hidden, down_full) for hidden in hidden_blocks])
+    gates, ups, partials_f, filled = [], [], [], []
+    for step, block in enumerate(feedforward_blocks):
+        last = step == size - 1
+        passed = [d_out_f] if step == size - 2 else [partials_f[1].astype(jnp.bfloat16)] if last and step > 1 else []
+        gate, up, partial, filled, passed = forward_units(step, size, block, gate_up_full, down_full, filled, passed, [])
+        gates.append(gate)
+        ups.append(up)
+        partials_f.append(partial)
+        if step == size - 2:
+            (d_out_f,) = passed
+        elif last and step > 1:
+            partials_f[1] = passed[0]
+    feedforward_rows, hidden_rows = filled
+    partials_n, filled = [], []
+    for step, grad in enumerate(ring_gather(d_out_f)):
+        partial, filled = backward_units(step, size, grad, gates[step], ups[step], gate_up_full, down_full, filled, [])
+        partials_n.append(partial)
+    grad_rows, d_gate_rows, d_up_rows = filled
+    arrived_f, own_f = ring_scatter(partials_f)
     out_streams = finish(middle, saved_f, arrived_f, own_f, *sizes)
-    arrived_n, own_n = ring_scatter([times_transposed(grads, gate_up_full) for grads in unit_grads])
-    down_grad = product_sum(jnp.concatenate(grad_blocks), jnp.concatenate(hidden_blocks))
-    gate_up_grad = product_sum(jnp.concatenate(feedforward_blocks), jnp.concatenate(unit_grads))
-
+    arrived_n, own_n = ring_scatter(partials_n)
+
+    orders = axis_orders()
+    whole_table, half_tables = piece_rows(orders), [piece_rows([order]) for order in orders]
+    down_parts = [
+        butterfly(part, order) for part, order in zip(jnp.split(core_products([(grad_rows, hidden_rows)]), 2), orders)
+    ]
+    gate_up_parts = [
+        butterfly(core_products([(feedforward_rows, grads)]), order)
+        for grads, order in zip((d_gate_rows, d_up_rows), orders)
+    ]
     middle_grad, d_out_a, d_branch_a, weight_sum_f, small_f = close_mix(
         True,
         [middle, saved_f, cotangents, arrived_n, own_n, arrived_f, own_f, valid, saved_a, out_a],
         tables_f,
         *sizes,
+        tokens=[marks[0] for _, marks in gate_up_parts],
+    )
+    down_grad = assemble(with_partner([part for part, _ in down_parts]), 0, units, whole_table)
+    gate_grad, up_grad = (
+        assemble(with_partner([part]), 0, units, table) for (part, _), table in zip(gate_up_parts, half_tables)
     )
     output_grads = ring_gather(d_out_a)
     attended_grads = [matmul(block, out_full).astype(jnp.bfloat16) for block in output_grads]
-    d_qkv = attend_back([query, key, value, log_totals], attended_grads, place_index, starts, cosine, sine)
+    d_qkv = attend_back(
+        [query, key, value, log_totals],
+        attended_grads,
+        place_index,
+        starts,
+        cosine,
+        sine,
+        [marks[-1] for _, marks in [*gate_up_parts, *down_parts]],
+    )
     arrived_i, own_i = ring_scatter([times_transposed(block, qkv_full) for block in jnp.split(d_qkv, size)])
-    out_grad = product_sum(jnp.concatenate(output_grads), attended)
-    qkv_grad = product_sum(jnp.concatenate(input_blocks), d_qkv)
+    attention_parts = [
+        butterfly(part, order)
+        for part, order in zip(
+            jnp.split(
+                core_products([(jnp.concatenate(output_grads), attended), (jnp.concatenate(input_blocks), d_qkv)]), 2
+            ),
+            orders,
+        )
+    ]
     input_grad, weight_sum_a, small_a = close_mix(
-        False, [inputs, saved_a, middle_grad, arrived_i, own_i, d_branch_a], tables_a, *sizes
-    )
-
-    def summed(weight_sum, small):
-        height = width // LANES
-        flat = sum_everywhere(
-            jnp.concatenate([weight_sum.reshape(weight_sum.shape[0] * height, LANES)[: 2 * uses * height], small])
-        )
-        return mix_grads(flat[: 2 * uses * height].reshape(2 * uses, width), flat[2 * uses * height :], *sizes)
-
-    static_f, weight_f, scale_f = summed(weight_sum_f, small_f)
-    static_a, weight_a, scale_a = summed(weight_sum_a, small_a)
-    query_grad, key_grad, value_grad = (
-        in_order([part[:, i * query_weight.shape[1] : (i + 1) * query_weight.shape[1]] for part in qkv_grad])
-        for i in range(3)
-    )
-    gate_grad, up_grad = (
-        in_order([part[:, i * units : (i + 1) * units] for part in gate_up_grad]) for i in range(2)
+        False,
+        [inputs, saved_a, middle_grad, arrived_i, own_i, d_branch_a],
+        tables_a,
+        *sizes,
+        tokens=[marks[1] for _, marks in attention_parts] + [down_grad, gate_grad, up_grad],
+    )
+    attention_halves = with_partner([part for part, _ in attention_parts])
+    out_grad, query_grad, key_grad, value_grad = (
+        assemble(attention_halves, part, out_weight.shape[1], whole_table) for part in range(4)
+    )
+    height = width // LANES
+    taken = 2 * uses * height
+
+    def flat(weight_sum, small):
+        return jnp.concatenate([weight_sum.reshape(weight_sum.shape[0] * height, LANES)[:taken], small])
+
+    sums = sum_everywhere(jnp.concatenate([flat(weight_sum_a, small_a), flat(weight_sum_f, small_f)]))
+    (static_a, weight_a, scale_a), (static_f, weight_f, scale_f) = (
+        mix_grads(part[:taken].reshape(2 * uses, width), part[taken:], *sizes) for part in jnp.split(sums, 2)
     )
     shape = streams.shape
     return (
@@ -907,10 +1161,10 @@
         query_grad,
         key_grad,
         value_grad,
-        in_order(out_grad),
+        out_grad,
         gate_grad,
         up_grad,
-        in_order(down_grad),
+        down_grad,
         jnp.stack([static_a, static_f]),
         jnp.stack([weight_a, weight_f]),
         jnp.stack([scale_a, scale_f]),

time: 1180 us -> 983 us (0.83)
  Pallas kernels: 128 us -> 327 us
  waiting for transfers between devices: 494 us -> 324 us
  matrix products: 259 us -> 106 us
  other arithmetic: 109 us -> 58.8 us
  starting transfers between devices: 69.1 us -> 41.1 us
    pallas_call x1 -> x16, Pallas kernels: 17.2 us -> 215 us  [the longest x7 78.6 us: assemble(): pl.pallas_call(functools.partial(assemble_kernel, count, pieces), grid_sp...]
    ppermute x50 -> x39, waiting for transfers between devices: 213 us -> 90.3 us  [swap(): lax.ppermute(values, axis, [(i, i ^ 1 << bit) for i in range(lax.axis_siz...]
    dot_general x16 -> x8, matrix products: 95.5 us -> 22.1 us  [matmul(): return jnp.dot(left, right, preferred_element_type=jnp.float32)]
    dot_general x16 -> x8, matrix products: 96.9 us -> 23.7 us  [times_transposed(): lax.dot_general(left, right, (((1,), (1,)), ((), ())), preferred_element_...]
    ppermute x24, waiting for transfers between devices: 280 us -> 233 us  [ring_shift(): lax.ppermute(block, 'tensor', [(i, (i + 1) % size) for i in range(size)])]
    convert_element_type x15 -> x7, other arithmetic: 41.5 us -> 1.27 us  [the longest x6 1.13 us: butterfly(): part = part.astype(jnp.bfloat16)]
    ppermute x50 -> x39, starting transfers between devices: 55.7 us -> 25 us  [swap(): lax.ppermute(values, axis, [(i, i ^ 1 << bit) for i in range(lax.axis_siz...]
    select_n x16 -> x0, other arithmetic: 25.6 us -> none  [halves_by(): jnp.where(bit_value == 0, jnp.concatenate([mine, other], axis=0), jnp.con...]
  transfers between devices with their start and end apart: 78 -> 67, of which waited for: 36 -> 29; matrix products, arithmetic and copies ran while one was open for 37% -> 25% of each run, Pallas kernels for 11% -> 29%
where the time goes in v2:
time: 983 us; the launch traced here: 973 us
  Pallas kernels  327 us (33%)
  waiting for transfers between devices  324 us (33%)
  matrix products  106 us (11%)
  local copies, waits for them, and re-layouts  99.7 us (10%)
  other arithmetic  58.8 us (6%)
  starting transfers between devices  41.1 us (4%)
  between operations  15.4 us (2%)
    ppermute x24, waiting for transfers between devices, ring_shift(): lax.ppermute(block, 'tensor', [(i, (i + 1) % size) for i in range(size)])  233 us
    ppermute x39, waiting for transfers between devices, swap(): lax.ppermute(values, axis, [(i, i ^ 1 << bit) for i in range(lax.axis_siz...  90.3 us
    pallas_call x7, Pallas kernels, assemble(): pl.pallas_call(functools.partial(assemble_kernel, count, pieces), grid_sp...  78.6 us
    pallas_call x4, Pallas kernels, forward_units(): pl.pallas_call(functools.partial(forward_units_kernel, kept), grid=(tiles...  60.2 us
    dot_general x10, matrix products, transposed_times(): lax.dot_general(left, right, (((0,), (0,)), ((), ())), preferred_element_...  60.2 us
    pallas_call x4, Pallas kernels, backward_units(): pl.pallas_call(functools.partial(backward_units_kernel, kept), grid=(tile...  58.9 us
    pallas_call x2, Pallas kernels, close_mix(): pl.pallas_call(functools.partial(close_kernel, streams, uses, width, inne...  55.1 us
    unnamed x162, local copies, waits for them, and re-layouts  41.8 us
  transfers between devices with their start and end apart: 67, of which 29 were waited for; matrix products, arithmetic and copies ran while one was open for 25% of the time, Pallas kernels for 29%

profile of v2, /device:TPU:0, one launch (start us, length us, event | category | flops | bytes accessed | tf_op | source)
XLA Modules:
  0.0 972.7 jit_solution(3476277691832171191)
XLA Ops:
  22.7 12.9 %open_attention.1 = (bf16[256,2048]{1,0:T(8,128)(2,1)S(1)}, f32[256,128]{1,0:T(8,128)S(1)}) custom-call(bf16[256,8192]{1,0:T(8,128)(2,1)} %bitcast.123, f32[2048,128]{1,0:T(8,128)S(1)} %pad.35.w_ref, f32[8,128]{1,0:T(8,128)S(1)} %get-tuple-element.192.param_ref), custom_call_target="tpu_custom_call" | custom-call | flops 12999999488 | tf_op jit(solution)/shard_map/open_attention/pallas_call | solution.py:478
  39.1 24.8 %collective-permute-done = bf16[256,2048]{1,0:T(8,128)(2,1)} collective-permute-done((bf16[256,2048]{1,0:T(8,128)(2,1)S(1)}, bf16[256,2048]{1,0:T(8,128)(2,1)}, u32[]{:S(2)}, u32[]{:S(2)}) %collective-permute-start) | collective-permute-done | bytes 1048608 | tf_op jit(solution)/shard_map/ppermute | solution.py:907
  66.5 23.9 %collective-permute-done.1 = bf16[256,2048]{1,0:T(8,128)(2,1)} collective-permute-done((bf16[256,2048]{1,0:T(8,128)(2,1)}, bf16[256,2048]{1,0:T(8,128)(2,1)}, u32[]{:S(2)}, u32[]{:S(2)}) %collective-permute-start.1) | collective-permute-done | bytes 1048608 | tf_op jit(solution)/shard_map/ppermute | solution.py:907
  104.3 12.0 %collective-permute-done.2 = bf16[256,2048]{1,0:T(8,128)(2,1)S(1)} collective-permute-done((bf16[256,2048]{1,0:T(8,128)(2,1)}, bf16[256,2048]{1,0:T(8,128)(2,1)S(1)}, u32[]{:S(2)}, u32[]{:S(2)}) %collective-permute-start.2) | collective-permute-done | bytes 1048608 | tf_op jit(solution)/shard_map/ppermute | solution.py:907
  119.5 14.4 %attend.1 = (bf16[1024,512]{1,0:T(8,128)(2,1)S(1)}, bf16[1024,512]{1,0:T(8,128)(2,1)S(1)}, bf16[1024,512]{1,0:T(8,128)(2,1)}, bf16[1024,512]{1,0:T(8,128)(2,1)}, f32[1024,512]{1,0:T(8,128)}) custom-call(s32[1]{0:T(128)} %bitcast.4.refs_0_, s32[1024,128]{1,0:T(8,128)S(1)} %broadcast_in_dim.74.refs_1_, f32[1024,128]{1,0:T(8,128)S(1)} %get-tuple-element.197.refs_2_, ...), custom_call_target="tpu_custom_call" | custom-call | flops 15000000512 | tf_op jit(solution)/shard_map/attend/pallas_call | solution.py:706
  139.4 24.3 %collective-permute-done.3 = bf16[256,2048]{1,0:T(8,128)(2,1)S(1)} collective-permute-done((bf16[256,2048]{1,0:T(8,128)(2,1)S(1)}, bf16[256,2048]{1,0:T(8,128)(2,1)S(1)}, u32[]{:S(2)}, u32[]{:S(2)}) %collective-permute-start.3) | collective-permute-done | bytes 1048608 | tf_op jit(solution)/shard_map/ppermute | solution.py:907
  167.9 21.7 %collective-permute-done.4 = bf16[256,2048]{1,0:T(8,128)(2,1)S(1)} collective-permute-done((bf16[256,2048]{1,0:T(8,128)(2,1)S(1)}, bf16[256,2048]{1,0:T(8,128)(2,1)S(1)}, u32[]{:S(2)}, u32[]{:S(2)}) %collective-permute-start.4) | collective-permute-done | bytes 1048608 | tf_op jit(solution)/shard_map/ppermute | solution.py:907
  213.7 21.8 %open_feedforward.1 = (bf16[256,2048]{1,0:T(8,128)(2,1)S(1)}, bf16[256,2048]{1,0:T(8,128)(2,1)S(1)}, f32[256,128]{1,0:T(8,128)S(1)}, f32[256,8192]{1,0:T(8,128)}, f32[256,2048]{1,0:T(8,128)}) custom-call(bf16[256,8192]{1,0:T(8,128)(2,1)} %bitcast.124, f32[256,128]{1,0:T(8,128)S(1)} %get-tuple-element.70.saved_a_ref.refs_8_.refs_1_, ...), custom_call_target="tpu_custom_call" | custom-call | flops 20999999488 | tf_op jit(solution)/shard_map/open_feedforward/pallas_call | solution.py:504
  236.7 22.2 %collective-permute-done.6.refs_0_ = bf16[256,2048]{1,0:T(8,128)(2,1)S(1)} collective-permute-done((bf16[256,2048]{1,0:T(8,128)(2,1)S(1)}, bf16[256,2048]{1,0:T(8,128)(2,1)S(1)}, u32[]{:S(2)}, u32[]{:S(2)}) %collective-permute-start.6) | collective-permute-done | bytes 1048608 | tf_op jit(solution)/shard_map/ppermute | solution.py:907
  263.6 18.3 %collective-permute-done.7.refs_0_ = bf16[256,2048]{1,0:T(8,128)(2,1)S(1)} collective-permute-done((bf16[256,2048]{1,0:T(8,128)(2,1)S(1)}, bf16[256,2048]{1,0:T(8,128)(2,1)S(1)}, u32[]{:S(2)}, u32[]{:S(2)}) %collective-permute-start.7) | collective-permute-done | bytes 1048608 | tf_op jit(solution)/shard_map/ppermute | solution.py:907
  283.4 14.6 %forward_units.4 = (f32[256,2048]{1,0:T(8,128)S(1)}, f32[256,2048]{1,0:T(8,128)}, f32[256,2048]{1,0:T(8,128)}, bf16[1024,2048]{1,0:T(8,128)(2,1)}, bf16[1024,2048]{1,0:T(8,128)(2,1)}) custom-call(bf16[256,2048]{1,0:T(8,128)(2,1)S(1)} %copy-done.4, bf16[2048,4096]{1,0:T(8,128)(2,1)} %all-gather.9.cloned.1.call-done.refs_1_.refs_2_.refs_4_.refs_5_, ...), custom_call_target="tpu_custom_call" | custom-call | flops 8999999488 | tf_op jit(solution)/shard_map/forward_units/pallas_call | solution.py:797
  299.3 14.6 %forward_units.5 = (f32[256,2048]{1,0:T(8,128)S(1)}, f32[256,2048]{1,0:T(8,128)}, f32[256,2048]{1,0:T(8,128)}, bf16[1024,2048]{1,0:T(8,128)(2,1)}, bf16[1024,2048]{1,0:T(8,128)(2,1)}) custom-call(bf16[256,2048]{1,0:T(8,128)(2,1)S(1)} %collective-permute-done.6.refs_0_, ...), custom_call_target="tpu_custom_call", output_to_operand_aliasing={{3}: (4, {}), {4}: (5, {})} | custom-call | flops 8999999488 | tf_op jit(solution)/shard_map/forward_units/pallas_call | solution.py:797
  315.2 15.1 %forward_units.6 = (f32[256,2048]{1,0:T(8,128)}, f32[256,2048]{1,0:T(8,128)}, f32[256,2048]{1,0:T(8,128)}, bf16[1024,2048]{1,0:T(8,128)(2,1)}, bf16[1024,2048]{1...) custom-call(bf16[256,2048]{1,0:T(8,128)(2,1)S(1)} %collective-permute-done.7., ...), custom_call_target="tpu_custom_call", output_to_operand_aliasing={{3}: (4, {}), {4}: (5, {}), {5}: (6, {})} | custom-call | flops 8999999488 | tf_op jit(solution)/shard_map/forward_units/pallas_call | solution.py:797
  356.5 16.0 %forward_units.7 = (f32[256,2048]{1,0:T(8,128)}, f32[256,2048]{1,0:T(8,128)}, f32[256,2048]{1,0:T(8,128)}, bf16[1024,2048]{1,0:T(8,128)(2,1)}, bf16[1024,2048]{1...) custom-call(bf16[256,2048]{1,0:T(8,128)(2,1)} %collective-permute-done.8.refs, ...), custom_call_target="tpu_custom_call", output_to_operand_aliasing={{3}: (4, {}), {4}: (5, {}), {5}: (6, {})} | custom-call | flops 8999999488 | tf_op jit(solution)/shard_map/forward_units/pallas_call | solution.py:797
  376.8 14.7 %backward_units.4 = (f32[256,2048]{1,0:T(8,128)S(1)}, bf16[1024,2048]{1,0:T(8,128)(2,1)}, bf16[1024,2048]{1,0:T(8,128)(2,1)}, bf16[1024,2048]{1,0:T(8,128)(2,1)}) custom-call(bf16[256,2048]{1,0:T(8,128)(2,1)S(1)} %get-tuple-element.88.refs_0_, f32[256,2048]{1,0:T(8,128)} %copy-done.1, f32[256,2048]{1,0:T(8,128)} %get-tuple-element.92.refs_2_, ...), custom_call_target="tpu_custom_call" | custom-call | flops 10000000000 | tf_op jit(solution)/shard_map/backward_units/pallas_call | solution.py:842
  393.3 14.7 %backward_units.5 = (f32[256,2048]{1,0:T(8,128)S(1)}, bf16[1024,2048]{1,0:T(8,128)(2,1)}, bf16[1024,2048]{1,0:T(8,128)(2,1)}, bf16[1024,2048]{1,0:T(8,128)(2,1)}) custom-call(bf16[256,2048]{1,0:T(8,128)(2,1)S(1)} %collective-permute-done.12.refs_0_, f32[256,2048]{1,0:T(8,128)} %copy-done, ...), custom_call_target="tpu_custom_call", output_to_operand_aliasing={{1}: (6, {}), {2}: (7, {}), {3}: (8, {})} | custom-call | flops 10000000000 | tf_op jit(solution)/shard_map/backward_units/pallas_call | solution.py:842
  408.2 14.7 %backward_units.6 = (f32[256,2048]{1,0:T(8,128)S(1)}, bf16[1024,2048]{1,0:T(8,128)(2,1)}, bf16[1024,2048]{1,0:T(8,128)(2,1)}, bf16[1024,2048]{1,0:T(8,128)(2,1)}) custom-call(bf16[256,2048]{1,0:T(8,128)(2,1)S(1)} %collective-permute-done.14.refs_0_, ...), custom_call_target="tpu_custom_call", output_to_operand_aliasing={{1}: (6, {}), {2}: (7, {}), {3}: (8, {})} | custom-call | flops 10000000000 | tf_op jit(solution)/shard_map/backward_units/pallas_call | solution.py:842
  424.5 14.9 %backward_units.7 = (f32[256,2048]{1,0:T(8,128)S(1)}, bf16[1024,2048]{1,0:T(8,128)(2,1)}, bf16[1024,2048]{1,0:T(8,128)(2,1)}, bf16[1024,2048]{1,0:T(8,128)(2,1)}) custom-call(bf16[256,2048]{1,0:T(8,128)(2,1)S(1)} %collective-permute-done.16.refs_0_, ...), custom_call_target="tpu_custom_call", output_to_operand_aliasing={{1}: (6, {}), {2}: (7, {}), {3}: (8, {})} | custom-call | flops 10000000000 | tf_op jit(solution)/shard_map/backward_units/pallas_call | solution.py:842
  477.7 22.2 %collective-permute-done.15 = bf16[256,2048]{1,0:T(8,128)(2,1)} collective-permute-done((bf16[256,2048]{1,0:T(8,128)(2,1)}, bf16[256,2048]{1,0:T(8,128)(2,1)}, u32[]{:S(2)}, u32[]{:S(2)}) %collective-permute-start.15) | collective-permute-done | bytes 1048608 | tf_op jit(solution)/shard_map/ppermute | solution.py:907
  544.3 29.8 %close_feedforward.1 = (f32[256,8192]{1,0:T(8,128)}, bf16[256,2048]{1,0:T(8,128)(2,1)S(1)}, f32[256,128]{1,0:T(8,128)S(1)}, f32[16,2048]{1,0:T(8,128)S(1)}, f32[8,128]{1,0:T(8,128)S(1)}) custom-call(f32[256,8192]{1,0:T(8,128)} %get-tuple-element.73.h_ref.refs_0_, f32[256,128]{1,0:T(8,128)S(1)} %get-tuple-element.74.saved_ref.refs_1_, ...), custom_call_target="tpu_custom_call" | custom-call | flops 30000001024 | tf_op jit(solution)/shard_map/close_feedforward/pallas_call | solution.py:570
  585.2 11.2 %collective-permute-done.28 = bf16[256,2048]{1,0:T(8,128)(2,1)} collective-permute-done((bf16[256,2048]{1,0:T(8,128)(2,1)}, bf16[256,2048]{1,0:T(8,128)(2,1)}, u32[]{:S(2)}, u32[]{:S(2)}) %collective-permute-start.28) | collective-permute-done | bytes 1048608 | tf_op jit(solution)/shard_map/ppermute | solution.py:927
  630.4 20.5 %collective-permute-done.22 = bf16[256,2048]{1,0:T(8,128)(2,1)S(1)} collective-permute-done((bf16[256,2048]{1,0:T(8,128)(2,1)S(1)}, bf16[256,2048]{1,0:T(8,128)(2,1)S(1)}, u32[]{:S(2)}, u32[]{:S(2)}) %collective-permute-start.22) | collective-permute-done | bytes 1048608 | tf_op jit(solution)/shard_map/ppermute | solution.py:907
  655.3 17.5 %attend_back.1 = bf16[1024,1536]{1,0:T(8,128)(2,1)} custom-call(s32[1]{0:T(128)} %bitcast.4.refs_0_, s32[1024,128]{1,0:T(8,128)S(1)} %copy-done.10, f32[1024,128]{1,0:T(8,128)S(1)} %copy-done.6, f32[1024,128]{1,0:T(8,128)S(1)} %copy-done.8, bf16[1024,512]{1,0:T(8,128)(2,1)} %copy-done.18, bf16[1024,512]{1,0:T(8,128)(2,1)} %copy-done.19, ...), custom_call_target="tpu_custom_call" | custom-call | flops 17999998976 | tf_op jit(solution)/shard_map/attend_back/pallas_call | solution.py:725
  715.4 16.3 %collective-permute-done.32 = bf16[256,2048]{1,0:T(8,128)(2,1)} collective-permute-done((bf16[256,2048]{1,0:T(8,128)(2,1)}, bf16[256,2048]{1,0:T(8,128)(2,1)}, u32[]{:S(2)}, u32[]{:S(2)}) %collective-permute-start.32) | collective-permute-done | bytes 1048608 | tf_op jit(solution)/shard_map/ppermute | solution.py:907
  736.8 19.0 %collective-permute-done.48 = bf16[512,2048]{1,0:T(8,128)(2,1)} collective-permute-done((bf16[512,2048]{1,0:T(8,128)(2,1)}, bf16[512,2048]{1,0:T(8,128)(2,1)}, u32[]{:S(2)}, u32[]{:S(2)}) %collective-permute-start.48) | collective-permute-done | bytes 2097184 | tf_op jit(solution)/shard_map/ppermute | solution.py:927
  764.0 12.2 %collective-permute-done.37.refs_9_ = bf16[256,2048]{1,0:T(8,128)(2,1)S(1)} collective-permute-done((bf16[256,2048]{1,0:T(8,128)(2,1)S(1)}, bf16[256,2048]{1,0:T(8,128)(2,1)S(1)}, u32[]{:S(2)}, u32[]{:S(2)}) %collective-permute-start.37) | collective-permute-done | bytes 1048608 | tf_op jit(solution)/shard_map/ppermute | solution.py:927
  781.6 11.5 %collective-permute-done.53 = bf16[128,2048]{1,0:T(8,128)(2,1)S(1)} collective-permute-done((bf16[128,2048]{1,0:T(8,128)(2,1)S(1)}, bf16[128,2048]{1,0:T(8,128)(2,1)S(1)}, u32[]{:S(2)}, u32[]{:S(2)}) %collective-permute-start.53) | collective-permute-done | bytes 524320 | tf_op jit(solution)/shard_map/ppermute | solution.py:927
  806.0 14.3 %assemble.7.refs_10_ = f32[2048,2048]{1,0:T(8,128)} custom-call(s32[16]{0:T(128)S(1)} %stack.142.table_ref, bf16[512,2048]{1,0:T(8,128)(2,1)S(1)} %pad_maximum_fusion.4.refs_0_, bf16[512,2048]{1,0:T(8,128)(2,1)} %pad_maximum_fusion.5.refs_1_, bf16[512,2048]{1,0:T(8,128)(2,1)} %collective-permute-done.42.refs_2_, ...), custom_call_target="tpu_custom_call" | custom-call | flops 8000000000 | tf_op jit(solution)/shard_map/assemble/pallas_call | solution.py:887
  825.5 11.5 %assemble.9.refs_12_ = f32[2048,2048]{1,0:T(8,128)} custom-call(s32[8]{0:T(128)S(1)} %stack.160.table_ref, bf16[1024,2048]{1,0:T(8,128)(2,1)} %pad_maximum_fusion.2.refs_0_, bf16[1024,2048]{1,0:T(8,128)(2,1)} %collective-permute-done.49.refs_1_), custom_call_target="tpu_custom_call" | custom-call | flops 8000000000 | tf_op jit(solution)/shard_map/assemble/pallas_call | solution.py:887
  837.0 11.5 %assemble.8.refs_11_ = f32[2048,2048]{1,0:T(8,128)} custom-call(s32[8]{0:T(128)S(1)} %stack.151.table_ref, bf16[1024,2048]{1,0:T(8,128)(2,1)} %pad_maximum_fusion.1.refs_0_, bf16[1024,2048]{1,0:T(8,128)(2,1)} %collective-permute-done.46.refs_1_), custom_call_target="tpu_custom_call" | custom-call | flops 8000000000 | tf_op jit(solution)/shard_map/assemble/pallas_call | solution.py:887
  848.5 25.3 %close_attention.1 = (bf16[256,8192]{1,0:T(8,128)(2,1)}, f32[16,2048]{1,0:T(8,128)S(1)}, f32[8,128]{1,0:T(8,128)S(1)}) custom-call(bf16[256,8192]{1,0:T(8,128)(2,1)} %bitcast.125, f32[256,128]{1,0:T(8,128)S(1)} %get-tuple-element.70.saved_a_ref.refs_8_.refs_1_, f32[256,8192]{1,0:T(8,128)} %get-tuple-element.114.refs_2_, ...), custom_call_target="tpu_custom_call" | custom-call | flops 24999999488 | tf_op jit(solution)/shard_map/close_attention/pallas_call | solution.py:570
  924.7 10.3 %assemble.13 = f32[2048,512]{1,0:T(8,128)} custom-call(s32[16]{0:T(128)S(1)} %stack.142.table_ref, bf16[512,2048]{1,0:T(8,128)(2,1)S(1)} %pad_maximum_fusion.8.refs_0_, bf16[512,2048]{1,0:T(8,128)(2,1)} %pad_maximum_fusion.9.refs_1_, bf16[512,2048]{1,0:T(8,128)(2,1)} %collective-permute-done.56.refs_2_, bf16[512,2048]{1,0:T(8,128)(2,1)} %collective-permute-done.57.refs_3_), custom_call_target="tpu_custom_call" | custom-call | flops 2000000000 | tf_op jit(solution)/shard_map/assemble/pallas_call | solution.py:887
  (452 shorter events, 408.8 us)
Async XLA Ops:
  7.2 83.7 %all-gather.5.cloned.1.call-start = ((), (), s32[]{:S(2)}) async-start(), calls=%async_computation | async-start | bytes 7077888 | tf_op jit(solution)/shard_map/all_gather | solution.py:1020
  9.5 127.3 %all-gather.7.cloned.1.call-start = ((), (), s32[]{:S(2)}) async-start(), calls=%async_computation.1 | async-start | bytes 2359296 | tf_op jit(solution)/shard_map/all_gather | solution.py:1020
  10.2 272.0 %all-gather.11.cloned.1.call-start = ((), (), s32[]{:S(2)}) async-start(), calls=%async_computation.3 | async-start | bytes 9437184 | tf_op jit(solution)/shard_map/all_gather | solution.py:1020
  10.9 271.3 %all-gather.9.cloned.1.call-start = ((), (), s32[]{:S(2)}) async-start(), calls=%async_computation.2 | async-start | bytes 18874368 | tf_op jit(solution)/shard_map/all_gather | solution.py:1020
  282.0 74.5 %collective-permute-start.8 = (bf16[256,2048]{1,0:T(8,128)(2,1)S(1)}, bf16[256,2048]{1,0:T(8,128)(2,1)}, u32[]{:S(2)}, u32[]{:S(2)}) collective-permute-start(bf16[256,2048]{1,0:T(8,128)(2,1)S(1)} %collective-permute-done.7.refs_0_), channel_id=1, source_target_pairs={{0,1},{1,2},{2,3},{3,0},{4,5},{5,6},{6,7},{7,4},{8,9},{9,10},{10,1... | collective-permute-start | bytes 3145736 | tf_op jit(solution)/shard_map/ppermute | solution.py:907
  372.5 75.4 %collective-permute-start.9 = (bf16[256,2048]{1,0:T(8,128)(2,1)S(1)}, bf16[256,2048]{1,0:T(8,128)(2,1)}, u32[]{:S(2)}, u32[]{:S(2)}) collective-permute-start(bf16[256,2048]{1,0:T(8,128)(2,1)S(1)} %get-tuple-element.84), channel_id=1, source_target_pairs={{0,1},{1,2},{2,3},{3,0},{4,5},{5,6},{6,7},{7,4},{8,9},{9,10},{10,1... | collective-permute-start | bytes 3145736 | tf_op jit(solution)/shard_map/ppermute | solution.py:907
  408.1 48.5 %collective-permute-start.13 = (bf16[256,2048]{1,0:T(8,128)(2,1)S(1)}, bf16[256,2048]{1,0:T(8,128)(2,1)}, u32[]{:S(2)}, u32[]{:S(2)}) collective-permute-start(bf16[256,2048]{1,0:T(8,128)(2,1)S(1)} %convert_element_type.225), channel_id=1, source_target_pairs={{0,1},{1,2},{2,3},{3,0},{4,5},{5,6},{6,7},{7,4},{8,9},{9,10},{10,1... | collective-permute-start | bytes 3145736 | tf_op jit(solution)/shard_map/ppermute | solution.py:907
  447.9 53.8 %collective-permute-start.19 = (bf16[1024,2048]{1,0:T(8,128)(2,1)}, bf16[1024,2048]{1,0:T(8,128)(2,1)}, u32[]{:S(2)}, u32[]{:S(2)}) collective-permute-start(bf16[1024,2048]{1,0:T(8,128)(2,1)} %convolution_convert_fusion.2), channel_id=1, source_target_pairs={{0,4},{4,0},{8,12},{12,8},{16,20},{20,16},{24,28},{28,24},{1,5},{5... | collective-permute-start | bytes 12582920 | tf_op jit(solution)/shard_map/ppermute | solution.py:927
  456.6 57.6 %collective-permute-start.18 = (bf16[1024,2048]{1,0:T(8,128)(2,1)}, bf16[1024,2048]{1,0:T(8,128)(2,1)S(1)}, u32[]{:S(2)}, u32[]{:S(2)}) collective-permute-start(bf16[1024,2048]{1,0:T(8,128)(2,1)} %convolution_convert_fusion.3), channel_id=1, source_target_pairs={{0,4},{4,0},{8,12},{12,8},{16,20},{20,16},{24,28},{28,24},{1,5},{5... | collective-permute-start | bytes 12582920 | tf_op jit(solution)/shard_map/ppermute | solution.py:927
  459.2 40.8 %collective-permute-start.15 = (bf16[256,2048]{1,0:T(8,128)(2,1)}, bf16[256,2048]{1,0:T(8,128)(2,1)}, u32[]{:S(2)}, u32[]{:S(2)}) collective-permute-start(bf16[256,2048]{1,0:T(8,128)(2,1)} %add_convert_fusion.5), channel_id=1, source_target_pairs={{0,1},{1,2},{2,3},{3,0},{4,5},{5,6},{6,7},{7,4},{8,9},{9,10},{10,1... | collective-permute-start | bytes 3145736 | tf_op jit(solution)/shard_map/ppermute | solution.py:907
  468.1 58.3 %collective-permute-start.27 = (bf16[1024,2048]{1,0:T(8,128)(2,1)}, bf16[1024,2048]{1,0:T(8,128)(2,1)}, u32[]{:S(2)}, u32[]{:S(2)}) collective-permute-start(bf16[1024,2048]{1,0:T(8,128)(2,1)} %convolution_convert_fusion.1), channel_id=1, source_target_pairs={{0,4},{4,0},{8,12},{12,8},{16,20},{20,16},{24,28},{28,24},{1,5},{5... | collective-permute-start | bytes 12582920 | tf_op jit(solution)/shard_map/ppermute | solution.py:927
  477.7 64.6 %collective-permute-start.11 = (bf16[256,2048]{1,0:T(8,128)(2,1)S(1)}, bf16[256,2048]{1,0:T(8,128)(2,1)S(1)}, u32[]{:S(2)}, u32[]{:S(2)}) collective-permute-start(bf16[256,2048]{1,0:T(8,128)(2,1)S(1)} %add_convert_fusion.6), channel_id=1, source_target_pairs={{0,1},{1,2},{2,3},{3,0},{4,5},{5,6},{6,7},{7,4},{8,9},{9,10},{10,1... | collective-permute-start | bytes 3145736 | tf_op jit(solution)/shard_map/ppermute | solution.py:907
  501.5 42.8 %collective-permute-start.17 = (bf16[256,2048]{1,0:T(8,128)(2,1)S(1)}, bf16[256,2048]{1,0:T(8,128)(2,1)S(1)}, u32[]{:S(2)}, u32[]{:S(2)}) collective-permute-start(bf16[256,2048]{1,0:T(8,128)(2,1)S(1)} %add_convert_fusion.4), channel_id=1, source_target_pairs={{0,1},{1,2},{2,3},{3,0},{4,5},{5,6},{6,7},{7,4},{8,9},{9,10},{10,1... | collective-permute-start | bytes 3145736 | tf_op jit(solution)/shard_map/ppermute | solution.py:907
  514.2 96.7 %collective-permute-start.25 = (bf16[512,2048]{1,0:T(8,128)(2,1)}, bf16[512,2048]{1,0:T(8,128)(2,1)}, u32[]{:S(2)}, u32[]{:S(2)}) collective-permute-start(bf16[512,2048]{1,0:T(8,128)(2,1)} %dynamic-slice_convert_fusion.refs_13_), channel_id=1, source_target_pairs={{0,16},{4,20},{8,24},{12,28},{16,0},{20,4},{24,8},{28,12},{1,17},{... | collective-permute-start | bytes 6291464 | tf_op jit(solution)/shard_map/ppermute | solution.py:927
  525.0 88.4 %collective-permute-start.23 = (bf16[512,2048]{1,0:T(8,128)(2,1)}, bf16[512,2048]{1,0:T(8,128)(2,1)}, u32[]{:S(2)}, u32[]{:S(2)}) collective-permute-start(bf16[512,2048]{1,0:T(8,128)(2,1)} %dynamic-slice_convert_fusion.1.refs_12_), channel_id=1, source_target_pairs={{0,8},{4,12},{8,0},{12,4},{16,24},{20,28},{24,16},{28,20},{1,9},{5... | collective-permute-start | bytes 6291464 | tf_op jit(solution)/shard_map/ppermute | solution.py:927
  540.4 43.0 %collective-permute-start.30 = (bf16[256,2048]{1,0:T(8,128)(2,1)}, bf16[256,2048]{1,0:T(8,128)(2,1)}, u32[]{:S(2)}, u32[]{:S(2)}) collective-permute-start(bf16[256,2048]{1,0:T(8,128)(2,1)} %dynamic-slice_convert_fusion.4), channel_id=1, source_target_pairs={{0,16},{4,20},{8,24},{12,28},{16,0},{20,4},{24,8},{28,12},{1,17},{... | collective-permute-start | bytes 3145736 | tf_op jit(solution)/shard_map/ppermute | solution.py:927
  542.3 54.1 %collective-permute-start.28 = (bf16[256,2048]{1,0:T(8,128)(2,1)}, bf16[256,2048]{1,0:T(8,128)(2,1)}, u32[]{:S(2)}, u32[]{:S(2)}) collective-permute-start(bf16[256,2048]{1,0:T(8,128)(2,1)} %dynamic-slice_convert_fusion.5), channel_id=1, source_target_pairs={{0,8},{4,12},{8,0},{12,4},{16,24},{20,28},{24,16},{28,20},{1,9},{5... | collective-permute-start | bytes 3145736 | tf_op jit(solution)/shard_map/ppermute | solution.py:927
  613.3 40.6 %collective-permute-start.26 = (bf16[256,2048]{1,0:T(8,128)(2,1)S(1)}, bf16[256,2048]{1,0:T(8,128)(2,1)S(1)}, u32[]{:S(2)}, u32[]{:S(2)}) collective-permute-start(bf16[256,2048]{1,0:T(8,128)(2,1)S(1)} %dynamic-slice_convert_fusion.6), channel_id=1, source_target_pairs={{0,8},{4,12},{8,0},{12,4},{16,24},{20,28},{24,16},{28,20},{1,9},{5... | collective-permute-start | bytes 3145736 | tf_op jit(solution)/shard_map/ppermute | solution.py:927
  627.5 54.8 %collective-permute-start.41 = (bf16[256,2048]{1,0:T(8,128)(2,1)}, bf16[256,2048]{1,0:T(8,128)(2,1)}, u32[]{:S(2)}, u32[]{:S(2)}) collective-permute-start(bf16[256,2048]{1,0:T(8,128)(2,1)} %pad_maximum_fusion.11), channel_id=1, source_target_pairs={{0,16},{4,20},{8,24},{12,28},{16,0},{20,4},{24,8},{28,12},{1,17},{... | collective-permute-start | bytes 3145736 | tf_op jit(solution)/shard_map/ppermute | solution.py:927
  628.6 56.7 %collective-permute-start.39 = (bf16[256,2048]{1,0:T(8,128)(2,1)}, bf16[256,2048]{1,0:T(8,128)(2,1)}, u32[]{:S(2)}, u32[]{:S(2)}) collective-permute-start(bf16[256,2048]{1,0:T(8,128)(2,1)} %pad_maximum_fusion.10), channel_id=1, source_target_pairs={{0,8},{4,12},{8,0},{12,4},{16,24},{20,28},{24,16},{28,20},{1,9},{5... | collective-permute-start | bytes 3145736 | tf_op jit(solution)/shard_map/ppermute | solution.py:927
  685.3 119.6 %collective-permute-start.43 = (bf16[512,2048]{1,0:T(8,128)(2,1)}, bf16[512,2048]{1,0:T(8,128)(2,1)}, u32[]{:S(2)}, u32[]{:S(2)}) collective-permute-start(bf16[512,2048]{1,0:T(8,128)(2,1)} %pad_maximum_fusion.5.refs_1_), channel_id=1, source_target_pairs={{0,4},{4,0},{8,12},{12,8},{16,20},{20,16},{24,28},{28,24},{1,5},{5... | collective-permute-start | bytes 6291464 | tf_op jit(solution)/shard_map/ppermute | solution.py:927
  687.1 118.6 %collective-permute-start.42 = (bf16[512,2048]{1,0:T(8,128)(2,1)S(1)}, bf16[512,2048]{1,0:T(8,128)(2,1)}, u32[]{:S(2)}, u32[]{:S(2)}) collective-permute-start(bf16[512,2048]{1,0:T(8,128)(2,1)S(1)} %pad_maximum_fusion.4.refs_0_), channel_id=1, source_target_pairs={{0,4},{4,0},{8,12},{12,8},{16,20},{20,16},{24,28},{28,24},{1,5},{5... | collective-permute-start | bytes 6291464 | tf_op jit(solution)/shard_map/ppermute | solution.py:927
  706.9 48.9 %collective-permute-start.48 = (bf16[512,2048]{1,0:T(8,128)(2,1)}, bf16[512,2048]{1,0:T(8,128)(2,1)}, u32[]{:S(2)}, u32[]{:S(2)}) collective-permute-start(bf16[512,2048]{1,0:T(8,128)(2,1)} %pad_maximum_fusion.7), channel_id=1, source_target_pairs={{0,16},{4,20},{8,24},{12,28},{16,0},{20,4},{24,8},{28,12},{1,17},{... | collective-permute-start | bytes 6291464 | tf_op jit(solution)/shard_map/ppermute | solution.py:927
  708.4 51.0 %collective-permute-start.45 = (bf16[512,2048]{1,0:T(8,128)(2,1)}, bf16[512,2048]{1,0:T(8,128)(2,1)}, u32[]{:S(2)}, u32[]{:S(2)}) collective-permute-start(bf16[512,2048]{1,0:T(8,128)(2,1)} %pad_maximum_fusion.6), channel_id=1, source_target_pairs={{0,8},{4,12},{8,0},{12,4},{16,24},{20,28},{24,16},{28,20},{1,9},{5... | collective-permute-start | bytes 6291464 | tf_op jit(solution)/shard_map/ppermute | solution.py:927
  731.7 44.5 %collective-permute-start.37 = (bf16[256,2048]{1,0:T(8,128)(2,1)S(1)}, bf16[256,2048]{1,0:T(8,128)(2,1)S(1)}, u32[]{:S(2)}, u32[]{:S(2)}) collective-permute-start(bf16[256,2048]{1,0:T(8,128)(2,1)S(1)} %dynamic-slice_convert_fusion.2), channel_id=1, source_target_pairs={{0,16},{4,20},{8,24},{12,28},{16,0},{20,4},{24,8},{28,12},{1,17},{... | collective-permute-start | bytes 3145736 | tf_op jit(solution)/shard_map/ppermute | solution.py:927
  776.2 49.3 %collective-permute-start.49 = (bf16[1024,2048]{1,0:T(8,128)(2,1)}, bf16[1024,2048]{1,0:T(8,128)(2,1)}, u32[]{:S(2)}, u32[]{:S(2)}) collective-permute-start(bf16[1024,2048]{1,0:T(8,128)(2,1)} %pad_maximum_fusion.2.refs_0_), channel_id=1, source_target_pairs={{0,4},{4,0},{8,12},{12,8},{16,20},{20,16},{24,28},{28,24},{1,5},{5... | collective-permute-start | bytes 12582920 | tf_op jit(solution)/shard_map/ppermute | solution.py:927
  778.8 58.2 %collective-permute-start.46 = (bf16[1024,2048]{1,0:T(8,128)(2,1)}, bf16[1024,2048]{1,0:T(8,128)(2,1)}, u32[]{:S(2)}, u32[]{:S(2)}) collective-permute-start(bf16[1024,2048]{1,0:T(8,128)(2,1)} %pad_maximum_fusion.1.refs_0_), channel_id=1, source_target_pairs={{0,4},{4,0},{8,12},{12,8},{16,20},{20,16},{24,28},{28,24},{1,5},{5... | collective-permute-start | bytes 12582920 | tf_op jit(solution)/shard_map/ppermute | solution.py:927
  804.7 43.8 %collective-permute-start.34 = (bf16[256,2048]{1,0:T(8,128)(2,1)S(1)}, bf16[256,2048]{1,0:T(8,128)(2,1)S(1)}, u32[]{:S(2)}, u32[]{:S(2)}) collective-permute-start(bf16[256,2048]{1,0:T(8,128)(2,1)S(1)} %add_convert_fusion.2), channel_id=1, source_target_pairs={{0,1},{1,2},{2,3},{3,0},{4,5},{5,6},{6,7},{7,4},{8,9},{9,10},{10,1... | collective-permute-start | bytes 3145736 | tf_op jit(solution)/shard_map/ppermute | solution.py:907
  821.3 52.7 %collective-permute-start.55 = (bf16[256,2048]{1,0:T(8,128)(2,1)}, bf16[256,2048]{1,0:T(8,128)(2,1)}, u32[]{:S(2)}, u32[]{:S(2)}) collective-permute-start(bf16[256,2048]{1,0:T(8,128)(2,1)} %pad_maximum_fusion.13), channel_id=1, source_target_pairs={{0,16},{4,20},{8,24},{12,28},{16,0},{20,4},{24,8},{28,12},{1,17},{... | collective-permute-start | bytes 3145736 | tf_op jit(solution)/shard_map/ppermute | solution.py:927
  824.2 53.9 %collective-permute-start.52 = (bf16[256,2048]{1,0:T(8,128)(2,1)}, bf16[256,2048]{1,0:T(8,128)(2,1)}, u32[]{:S(2)}, u32[]{:S(2)}) collective-permute-start(bf16[256,2048]{1,0:T(8,128)(2,1)} %pad_maximum_fusion.12), channel_id=1, source_target_pairs={{0,8},{4,12},{8,0},{12,4},{16,24},{20,28},{24,16},{28,20},{1,9},{5... | collective-permute-start | bytes 3145736 | tf_op jit(solution)/shard_map/ppermute | solution.py:927
  876.8 47.9 %collective-permute-start.57 = (bf16[512,2048]{1,0:T(8,128)(2,1)}, bf16[512,2048]{1,0:T(8,128)(2,1)}, u32[]{:S(2)}, u32[]{:S(2)}) collective-permute-start(bf16[512,2048]{1,0:T(8,128)(2,1)} %pad_maximum_fusion.9.refs_1_), channel_id=1, source_target_pairs={{0,4},{4,0},{8,12},{12,8},{16,20},{20,16},{24,28},{28,24},{1,5},{5... | collective-permute-start | bytes 6291464 | tf_op jit(solution)/shard_map/ppermute | solution.py:927
  879.6 45.1 %collective-permute-start.56 = (bf16[512,2048]{1,0:T(8,128)(2,1)S(1)}, bf16[512,2048]{1,0:T(8,128)(2,1)}, u32[]{:S(2)}, u32[]{:S(2)}) collective-permute-start(bf16[512,2048]{1,0:T(8,128)(2,1)S(1)} %pad_maximum_fusion.8.refs_0_), channel_id=1, source_target_pairs={{0,4},{4,0},{8,12},{12,8},{16,20},{20,16},{24,28},{28,24},{1,5},{5... | collective-permute-start | bytes 6291464 | tf_op jit(solution)/shard_map/ppermute | solution.py:927
  (109 other events, 1557.8 us)
Sparse Core Ops, SparseCore 0:
  10.5 48.2 all-gather.4
  60.7 27.9 all-gather.6
  90.6 54.3 all-gather.10
  147.3 89.8 all-gather.8

commit v3 on v2

--- a/solution.py
+++ b/solution.py
@@ -1,4 +1,5 @@
 import functools
+import math
 import jax
 import jax.numpy as jnp
 from jax import lax
@@ -32,12 +33,46 @@
     )
 
 
+MARKS = {}
+
+
+def marked(results, mark):
+    for one in results:
+        MARKS[id(one)] = (one, mark)
+    return results
+
+
+def waits(tokens):
+    each = {id(t): t for t in (MARKS[id(one)][1] if id(one) in MARKS else one for one in tokens)}
+    return list(each.values())
+
+
+MARK_SPEC = pl.BlockSpec((8, LANES), lambda *index: (0, 0))
+MARK_SHAPE = jax.ShapeDtypeStruct((8, LANES), jnp.float32)
+
+
 def anywhere(count):
     return [pl.BlockSpec(memory_space=pl.ANY)] * count
 
 
-def cost(microseconds):
+def cost(microseconds=0):
     return pl.CostEstimate(flops=int(microseconds * 1e9), bytes_accessed=0, transcendentals=0)
+
+
+def hold(values, *tokens):
+    tokens = waits(tokens)
+
+    def nothing(*refs):
+        pass
+
+    return pl.pallas_call(
+        nothing,
+        in_specs=anywhere(len(values) + len(tokens)),
+        out_specs=anywhere(len(values)),
+        out_shape=[jax.ShapeDtypeStruct(a.shape, a.dtype) for a in values],
+        input_output_aliases={k: k for k in range(len(values))},
+        name="hold",
+    )(*values, *tokens)
 
 
 def lanes_of(rows):
@@ -71,29 +106,31 @@
     return values if shift == 0 else pltpu.roll(values, shift, 1)
 
 
-def coefficients(projected, means, rsqrts, param_ref, sums_ref, streams, uses, parts):
+def coefficients(projected, means, rsqrts, param_ref, sums_ref, streams, uses, parts, centred):
     rows = projected[0].shape[0]
     lane = lanes_of(rows)
     gathered = jnp.zeros((rows, LANES), jnp.float32)
+    sums = jnp.zeros((rows, LANES), jnp.float32)
     for j in range(streams):
-        total = projected[j]
-        for part in range(1, parts):
-            total = total + rolled(projected[j], -part * uses)
-        if sums_ref is not None:
+        total = joined(projected[j], parts)
+        if not centred:
             total = total - means[j] * sums_ref[0:1, :]
         total = total * rsqrts[j]
         inside = (lane >= j * uses) & (lane < (j + 1) * uses)
         gathered = jnp.where(inside, rolled(total, j * uses), gathered)
+        sums = jnp.where(inside, rolled(jnp.broadcast_to(sums_ref[0:1, :], (rows, LANES)), j * uses), sums)
     bent = jnp.tanh(gathered)
-    return gathered, bent, param_ref[0:1, :] + param_ref[1:2, :] * bent
-
-
-def pack_saved(coeffs, bent, gathered, means, rsqrts, mean_e, rsqrt_e, streams, uses):
+    return gathered, bent, param_ref[0:1, :] + param_ref[1:2, :] * bent, sums
+
+
+def pack_saved(coeffs, bent, gathered, sums, means, rsqrts, mean_e, rsqrt_e, streams, uses):
     lane = lanes_of(coeffs.shape[0])
     count = streams * uses
     saved = jnp.where(lane < count, coeffs, 0.0)
     saved = jnp.where((lane >= count) & (lane < 2 * count), rolled(bent, count), saved)
     saved = jnp.where((lane >= 2 * count) & (lane < 3 * count), rolled(gathered, 2 * count), saved)
+    first = 3 * count + 2 * streams + 2
+    saved = jnp.where((lane >= first) & (lane < first + count), rolled(sums, first), saved)
     return place(saved, [*means, *rsqrts, mean_e, rsqrt_e], 3 * count)
 
 
@@ -119,26 +156,35 @@
     return centre_stats(total, lambda start: entering_ref[rows, start : start + CHUNK], width)
 
 
-def weight_parts(w_ref, parts_ref, sums_ref, uses, parts):
+def weight_parts(w_ref, parts_ref, sums_ref, parts):
     @pl.when(pl.program_id(0) == 0)
     def _():
         rest = w_ref[...]
-        sums_ref[0:1, :] = jnp.sum(rest, axis=0, keepdims=True)
-        total = None
-        for part in range(parts):
-            one = rest.astype(jnp.bfloat16).astype(jnp.float32)
-            rest = rest - one
-            total = one if total is None else total + rolled(one, part * uses)
-        parts_ref[...] = total.astype(jnp.bfloat16)
+        rows, width = rest.shape
+        each = []
+        for _ in range(parts):
+            each.append(rest.astype(jnp.bfloat16).astype(jnp.float32))
+            rest = rest - each[-1]
+        each.append(jnp.zeros((LANES - parts * rows, width), jnp.float32))
+        parts_ref[...] = jnp.concatenate(each, axis=0).astype(jnp.bfloat16)
+        sums = times_transposed(jnp.ones((8, width), jnp.bfloat16), parts_ref[...])
+        sums_ref[...] = joined(sums, parts)
+
+
+def joined(values, parts):
+    total = values
+    for part in range(1, parts):
+        total = total + rolled(values, -8 * part)
+    return total
 
 
 def open_attention_kernel(
     streams, uses, width, x_ref, w_ref, param_ref, normed_ref, saved_ref, raw_ref, entering_ref, parts_ref, sums_ref
 ):
     block = x_ref.shape[0]
-    weight_parts(w_ref, parts_ref, sums_ref, uses, 3)
+    weight_parts(w_ref, parts_ref, sums_ref, 3)
     stacked = jnp.concatenate([x_ref[:, j * width : (j + 1) * width] for j in range(streams)], axis=0)
-    raw_ref[...] = jnp.dot(stacked, parts_ref[...], preferred_element_type=jnp.float32)
+    raw_ref[...] = times_transposed(stacked, parts_ref[...])
 
     def body(index, carry):
         first = pl.multiple_of(index * GROUP, GROUP)
@@ -157,26 +203,28 @@
             means.append(mean)
             rsqrts.append(rsqrt)
             projected.append(raw_ref[pl.ds(pl.multiple_of(j * block + first, GROUP), GROUP), :])
-        gathered, bent, coeffs = coefficients(projected, means, rsqrts, param_ref, sums_ref, streams, uses, 3)
+        gathered, bent, coeffs, sums = coefficients(
+            projected, means, rsqrts, param_ref, sums_ref, streams, uses, 3, False
+        )
         mean_e, rsqrt_e = entering_norm(read, coeffs, streams, uses, width, entering_ref, rows)
         for start in range(0, width, CHUNK):
             normed_ref[rows, start : start + CHUNK] = (
                 (entering_ref[rows, start : start + CHUNK] - mean_e) * rsqrt_e
             ).astype(jnp.bfloat16)
-        saved_ref[rows, :] = pack_saved(coeffs, bent, gathered, means, rsqrts, mean_e, rsqrt_e, streams, uses)
+        saved_ref[rows, :] = pack_saved(
+            coeffs, bent, gathered, sums, means, rsqrts, mean_e, rsqrt_e, streams, uses
+        )
         return carry
 
     lax.fori_loop(0, block // GROUP, body, 0)
 
 
-def open_feedforward_kernel(
-    streams, uses, width,
-    x_ref, saved_a_ref, arrived_ref, partial_ref, g_ref, valid_ref, w_ref, param_ref,
-    normed_ref, grad_ref, saved_ref, h_ref, out_ref,
-    high_ref, low_ref, raw_ref, entering_ref, stats_ref, parts_ref, sums_ref,
-):
+def open_feedforward_kernel(streams, uses, width, *refs):
+    x_ref, saved_a_ref, out_ref, g_ref, valid_ref, w_ref, param_ref = refs[:7]
+    normed_ref, grad_ref, saved_ref, h_ref = refs[7:11]
+    high_ref, low_ref, raw_ref, entering_ref, stats_ref, parts_ref, sums_ref = refs[11:]
     block = x_ref.shape[0]
-    weight_parts(w_ref, parts_ref, sums_ref, uses, 2)
+    weight_parts(w_ref, parts_ref, sums_ref, 2)
     count = streams * uses
 
     def first_pass(index, carry):
@@ -185,8 +233,7 @@
         coeffs = saved_a_ref[rows, :]
         totals = [None] * streams
         for start in range(0, width, CHUNK):
-            out = arrived_ref[rows, start : start + CHUNK].astype(jnp.float32) + partial_ref[rows, start : start + CHUNK]
-            out_ref[rows, start : start + CHUNK] = out
+            out = out_ref[rows, start : start + CHUNK]
             values = [
                 x_ref[rows, j * width + start : j * width + start + CHUNK].astype(jnp.float32)
                 for j in range(streams)
@@ -217,8 +264,8 @@
         return carry
 
     lax.fori_loop(0, block // GROUP, first_pass, 0)
-    raw_ref[...] = jnp.dot(high_ref[...], parts_ref[...], preferred_element_type=jnp.float32) + jnp.dot(
-        low_ref[...], parts_ref[...], preferred_element_type=jnp.float32
+    raw_ref[...] = times_transposed(high_ref[...], parts_ref[...]) + times_transposed(
+        low_ref[...], parts_ref[...]
     )
 
     def second_pass(index, carry):
@@ -228,7 +275,9 @@
         means = [column(stats, j) for j in range(streams)]
         rsqrts = [column(stats, streams + j) for j in range(streams)]
         projected = [raw_ref[pl.ds(pl.multiple_of(j * block + first, GROUP), GROUP), :] for j in range(streams)]
-        gathered, bent, coeffs = coefficients(projected, means, rsqrts, param_ref, None, streams, uses, 2)
+        gathered, bent, coeffs, sums = coefficients(
+            projected, means, rsqrts, param_ref, sums_ref, streams, uses, 2, True
+        )
 
         def read(j, start):
             return h_ref[rows, j * width + start : j * width + start + CHUNK]
@@ -244,13 +293,18 @@
                 term = branch[i] * g_ref[rows, i * width + start : i * width + start + CHUNK].astype(jnp.float32)
                 grad = term if grad is None else grad + term
             grad_ref[rows, start : start + CHUNK] = grad.astype(jnp.bfloat16)
-        saved_ref[rows, :] = pack_saved(coeffs, bent, gathered, means, rsqrts, mean_e, rsqrt_e, streams, uses)
+        saved_ref[rows, :] = pack_saved(
+            coeffs, bent, gathered, sums, means, rsqrts, mean_e, rsqrt_e, streams, uses
+        )
         return carry
 
     lax.fori_loop(0, block // GROUP, second_pass, 0)
 
 
-def finish_kernel(streams, uses, width, h_ref, saved_ref, arrived_ref, partial_ref, y_ref):
+def finish_kernel(streams, uses, width, h_ref, saved_ref, arrived_ref, partial_ref, *refs):
+    y_ref, mark_ref = refs[-2:]
+    mark_ref[...] = jnp.zeros_like(mark_ref)
+
     def body(index, carry):
         rows = pl.ds(pl.multiple_of(index * GROUP, GROUP), GROUP)
         coeffs = saved_ref[rows, :]
@@ -261,7 +315,7 @@
                 mixed = column(coeffs, i * uses + streams + 1) * out
                 for j in range(streams):
                     mixed = mixed + column(coeffs, j * uses + 1 + i) * values[j]
-                y_ref[rows, i * width + start : i * width + start + CHUNK] = mixed.astype(jnp.bfloat16)
+                y_ref[rows, i, start : start + CHUNK] = mixed.astype(jnp.bfloat16)
         return carry
 
     lax.fori_loop(0, h_ref.shape[0] // GROUP, body, 0)
@@ -272,11 +326,11 @@
     refs = refs[:inputs] + refs[inputs + kept :]
     if inner:
         (h_ref, saved_ref, g_ref, arrived_ref, partial_ref, arrived_f_ref, partial_f_ref, valid_ref, saved_a_ref,
-         out_a_ref, wt_ref, param_ref, grad_ref, below_ref, branch_ref, weight_ref, small_ref,
-         centre_ref, du_ref, left_ref, dl_ref, cols_ref, sums_ref) = refs
+         out_a_ref, wt_ref, param_ref, grad_ref, branch_ref, below_ref, weight_ref, small_ref,
+         centre_ref, du_ref, left_ref, dl_ref, cols_ref, sums_ref, parts_ref) = refs
     else:
         (h_ref, saved_ref, g_ref, arrived_ref, partial_ref, branch_in_ref, wt_ref, param_ref,
-         grad_ref, weight_ref, small_ref, centre_ref, du_ref, left_ref, dl_ref, cols_ref, sums_ref) = refs
+         grad_ref, weight_ref, small_ref, centre_ref, du_ref, left_ref, dl_ref, cols_ref, sums_ref, parts_ref) = refs
     block = h_ref.shape[0]
     count = streams * uses
     step = pl.program_id(0)
@@ -286,6 +340,10 @@
     @pl.when(step == 0)
     def _():
         sums_ref[...] = jnp.zeros_like(sums_ref)
+        weights = wt_ref[...]
+        high = weights.astype(jnp.bfloat16).astype(jnp.float32)
+        rest = jnp.zeros((LANES - 3 * weights.shape[0], width), jnp.float32)
+        parts_ref[...] = jnp.concatenate([high, high, weights - high, rest], axis=0).astype(jnp.bfloat16)
 
     def read_h(rows, j, start):
         return h_ref[rows, j * width + start : j * width + start + CHUNK].astype(jnp.float32)
@@ -354,7 +412,7 @@
         sums_ref[0] += d_coeffs
         sums_ref[1] += d_coeffs * bent
         du = d_coeffs * param_ref[1:2, :] * (1.0 - bent * bent)
-        with_mean = du * param_ref[3:4, :] * (1.0 / width)
+        with_mean = du * jnp.where(lane < count, rolled(saved, -(3 * count + 2 * streams + 2)), 0.0) * (1.0 / width)
         with_value = du * projected * (1.0 / width)
         shifts, slopes = [], []
         scaled = jnp.zeros((GROUP, LANES), jnp.float32)
@@ -366,19 +424,13 @@
             scaled = jnp.where(inside, du * rsqrts[j], scaled)
         high = scaled.astype(jnp.bfloat16).astype(jnp.float32)
         low = (scaled - high).astype(jnp.bfloat16).astype(jnp.float32)
-        spread = jnp.where(lane < count, high, 0.0)
-        spread = jnp.where((lane >= count) & (lane < 2 * count), rolled(low, count), spread)
-        spread = jnp.where((lane >= 2 * count) & (lane < 3 * count), rolled(high, 2 * count), spread)
         for j in range(streams):
-            mine = lane < 0
-            for part in range(3):
-                begin = part * count + j * uses
-                mine = mine | ((lane >= begin) & (lane < begin + uses))
-            left_ref[pl.ds(pl.multiple_of(j * block + first, GROUP), GROUP), :] = jnp.where(
-                mine, spread, 0.0
-            ).astype(jnp.bfloat16)
-            pair = jnp.where(lane < uses, rolled(high, -j * uses), 0.0)
-            pair = jnp.where((lane >= uses) & (lane < 2 * uses), rolled(low, uses - j * uses), pair)
+            own_high, own_low = rolled(high, -j * uses), rolled(low, -j * uses)
+            left = jnp.where(lane < uses, own_high, 0.0)
+            left = jnp.where((lane >= 8) & (lane < 8 + uses), rolled(own_low, 8), left)
+            left = jnp.where((lane >= 16) & (lane < 16 + uses), rolled(own_high, 16), left)
+            left_ref[pl.ds(pl.multiple_of(j * block + first, GROUP), GROUP), :] = left.astype(jnp.bfloat16)
+            pair = jnp.where(lane < 8 + uses, left, 0.0)
             du_ref[pl.ds(pl.multiple_of(j * all_rows + base + first, GROUP), GROUP), :] = pair.astype(jnp.bfloat16)
         cols_ref[rows, :] = place(
             jnp.zeros((GROUP, LANES), jnp.float32), [mean_dn, mean_dnn, *shifts, *slopes], 0
@@ -386,7 +438,7 @@
         return carry
 
     lax.fori_loop(0, block // GROUP, first_pass, 0)
-    dl_ref[...] = jnp.dot(left_ref[...], wt_ref[...], preferred_element_type=jnp.float32)
+    dl_ref[...] = jnp.dot(left_ref[...], parts_ref[...], preferred_element_type=jnp.float32)
 
     def second_pass(index, carry):
         first = pl.multiple_of(index * GROUP, GROUP)
@@ -413,7 +465,10 @@
                 grad = grad + dl_ref[pl.ds(pl.multiple_of(j * block + first, GROUP), GROUP), start : start + CHUNK]
                 for i in range(streams):
                     grad = grad + column(saved, j * uses + 1 + i) * gs[i]
-                grad_ref[rows, j * width + start : j * width + start + CHUNK] = grad.astype(grad_ref.dtype)
+                if inner:
+                    grad_ref[rows, j * width + start : j * width + start + CHUNK] = grad
+                else:
+                    grad_ref[rows, j, start : start + CHUNK] = grad.astype(jnp.bfloat16)
                 if inner:
                     part = fold(grad * out_a_ref[rows, start : start + CHUNK])
                     branch_sums[j] = part if branch_sums[j] is None else branch_sums[j] + part
@@ -444,37 +499,31 @@
 
 
 def specs_for(arrays, block, whole):
-    return [
-        pl.BlockSpec(a.shape, lambda i: (0, 0)) if k in whole else pl.BlockSpec((block, a.shape[1]), lambda i: (i, 0))
-        for k, a in enumerate(arrays)
-    ]
-
-
-def rounded(values):
-    return lax.reduce_precision(values, 8, 7)
+    specs = []
+    for k, entry in enumerate(arrays):
+        array, first = entry if isinstance(entry, tuple) else (entry, 0)
+        if k in whole:
+            specs.append(pl.BlockSpec(array.shape, lambda i: (0, 0)))
+        else:
+            specs.append(pl.BlockSpec((block, array.shape[1]), lambda i, first=first // block: (first + i, 0)))
+    return specs
+
+
+def plain(arrays):
+    return [entry[0] if isinstance(entry, tuple) else entry for entry in arrays]
 
 
 def mix_tables(static, weight, scale):
     streams, uses = static.shape
-    high = rounded(weight)
-    middle = rounded(weight - high)
-    forward = jnp.pad(weight, ((0, 0), (0, LANES - uses)))
-    tall = [jnp.tile(part.T, (streams, 1)) for part in (high, high, middle)]
-    backward = jnp.pad(jnp.concatenate(tall, axis=0), ((0, LANES - 3 * streams * uses), (0, 0))).astype(jnp.bfloat16)
     count = streams * uses
-
-    def row(values):
-        return jnp.pad(values, (0, LANES - values.shape[0]))[None]
-
-    constants = jnp.concatenate([row(static.reshape(count)), row(jnp.tile(scale, streams)), jnp.zeros((6, LANES), jnp.float32)])
-    with_sums = jnp.concatenate([constants[:3], row(jnp.tile(jnp.sum(weight, axis=0), streams)), constants[4:]])
-    return forward, backward, constants, with_sums
+    constants = jnp.stack([static.reshape(count), jnp.tile(scale, streams)])
+    return jnp.pad(weight.T, ((0, 8 - uses), (0, 0))), jnp.pad(constants, ((0, 6), (0, LANES - count)))
 
 
 def open_attention(x, tables, streams, uses):
     rows, width = x.shape[0], x.shape[1] // streams
     block = rows_block(rows)
-    arrays = [x, tables[0], tables[2]]
+    arrays = [x, *tables]
     return pl.pallas_call(
         functools.partial(open_attention_kernel, streams, uses, width),
         grid=(rows // block,),
@@ -484,19 +533,19 @@
         scratch_shapes=[
             pltpu.VMEM((streams * block, LANES), jnp.float32),
             pltpu.VMEM((block, width), jnp.float32),
-            pltpu.VMEM((width, LANES), jnp.bfloat16),
+            pltpu.VMEM((LANES, width), jnp.bfloat16),
             pltpu.VMEM((8, LANES), jnp.float32),
         ],
         compiler_params=PARAMS,
-        cost_estimate=cost(13),
+        cost_estimate=cost(),
         name="open_attention",
-    )(*arrays)
-
-
-def open_feedforward(x, saved_a, arrived, partial, g, valid, tables, streams, uses):
+    )(*plain(arrays))
+
+
+def open_feedforward(x, saved_a, out_a, g, valid, tables, streams, uses):
     rows, width = x.shape[0], x.shape[1] // streams
     block = rows_block(rows)
-    arrays = [x, saved_a, arrived, partial, g, valid, tables[0], tables[2]]
+    arrays = [x, saved_a, out_a, g, valid, *tables]
 
     def by_rows(columns):
         return pl.BlockSpec((block, columns), lambda i: (i, 0))
@@ -504,14 +553,13 @@
     return pl.pallas_call(
         functools.partial(open_feedforward_kernel, streams, uses, width),
         grid=(rows // block,),
-        in_specs=specs_for(arrays, block, {6, 7}),
-        out_specs=[by_rows(width), by_rows(width), by_rows(LANES), by_rows(streams * width), by_rows(width)],
+        in_specs=specs_for(arrays, block, {5, 6}),
+        out_specs=[by_rows(width), by_rows(width), by_rows(LANES), by_rows(streams * width)],
         out_shape=[
             jax.ShapeDtypeStruct((rows, width), jnp.bfloat16),
             jax.ShapeDtypeStruct((rows, width), jnp.bfloat16),
             jax.ShapeDtypeStruct((rows, LANES), jnp.float32),
             jax.ShapeDtypeStruct((rows, streams * width), jnp.float32),
-            jax.ShapeDtypeStruct((rows, width), jnp.float32),
         ],
         scratch_shapes=[
             pltpu.VMEM((streams * block, width), jnp.bfloat16),
@@ -519,51 +567,59 @@
             pltpu.VMEM((streams * block, LANES), jnp.float32),
             pltpu.VMEM((block, width), jnp.float32),
             pltpu.VMEM((block, LANES), jnp.float32),
-            pltpu.VMEM((width, LANES), jnp.bfloat16),
+            pltpu.VMEM((LANES, width), jnp.bfloat16),
             pltpu.VMEM((8, LANES), jnp.float32),
         ],
         compiler_params=PARAMS,
-        cost_estimate=cost(21),
+        cost_estimate=cost(),
         name="open_feedforward",
-    )(*arrays)
-
-
-def finish(h, saved, arrived, partial, streams, uses):
+    )(*plain(arrays))
+
+
+def finish(first, h, saved, arrived, partial, streams, uses, filled, tokens=()):
+    tokens = waits(tokens)
     rows, width = h.shape[0], h.shape[1] // streams
+    block = rows_block(arrived[2])
+    arrays = [(h, first), (saved, first), arrived[:2], (partial, first)]
+    result, mark = pl.pallas_call(
+        functools.partial(finish_kernel, streams, uses, width),
+        grid=(arrived[2] // block,),
+        in_specs=specs_for(arrays, block, set()) + anywhere(len(filled) + len(tokens)),
+        out_specs=[pl.BlockSpec((block, streams, width), lambda i: (first // block + i, 0, 0)), MARK_SPEC],
+        out_shape=[jax.ShapeDtypeStruct((rows, streams, width), jnp.bfloat16), MARK_SHAPE],
+        input_output_aliases={4 + k: k for k in range(len(filled))},
+        compiler_params=PARAMS,
+        cost_estimate=cost(),
+        name="finish",
+    )(*plain(arrays), *filled, *tokens)
+    return marked([result], mark)[0]
+
+
+def close_mix(inner, first, rows, arrays, tables, streams, uses, filled=(), tokens=()):
+    tokens = [*filled, *waits(tokens)]
+    h = arrays[0][0]
+    whole, width = h.shape[0], h.shape[1] // streams
     block = rows_block(rows)
-    arrays = [h, saved, arrived, partial]
-    return pl.pallas_call(
-        functools.partial(finish_kernel, streams, uses, width),
-        grid=(rows // block,),
-        in_specs=specs_for(arrays, block, set()),
-        out_specs=pl.BlockSpec((block, streams * width), lambda i: (i, 0)),
-        out_shape=jax.ShapeDtypeStruct((rows, streams * width), jnp.bfloat16),
-        compiler_params=PARAMS,
-        cost_estimate=cost(8),
-        name="finish",
-    )(*arrays)
-
-
-def close_mix(inner, arrays, tables, streams, uses, tokens=()):
-    h = arrays[0]
-    rows, width = h.shape[0], h.shape[1] // streams
-    block = rows_block(rows)
-    arrays = [*arrays, tables[1], tables[3]]
+    arrays = [*arrays, *tables]
     last = len(arrays)
 
     def by_rows(columns):
-        return pl.BlockSpec((block, columns), lambda i: (i, 0))
+        return pl.BlockSpec((block, columns), lambda i: (first // block + i, 0))
 
     def fixed(height, columns):
         return pl.BlockSpec((height, columns), lambda i: (0, 0))
 
-    out_specs = [by_rows(streams * width)]
-    out_shape = [jax.ShapeDtypeStruct((rows, streams * width), jnp.float32 if inner else jnp.bfloat16)]
     if inner:
-        out_specs += [by_rows(width), by_rows(LANES)]
+        out_specs = [by_rows(streams * width)]
+        out_shape = [jax.ShapeDtypeStruct((whole, streams * width), jnp.float32)]
+    else:
+        out_specs = [pl.BlockSpec((block, streams, width), lambda i: (i, 0, 0))]
+        out_shape = [jax.ShapeDtypeStruct((rows, streams, width), jnp.bfloat16)]
+    if inner:
+        out_specs += [by_rows(LANES), by_rows(width)]
         out_shape += [
-            jax.ShapeDtypeStruct((rows, width), jnp.bfloat16),
-            jax.ShapeDtypeStruct((rows, LANES), jnp.float32),
+            jax.ShapeDtypeStruct((whole, LANES), jnp.float32),
+            jax.ShapeDtypeStruct((whole, width), jnp.bfloat16),
         ]
     out_specs += [fixed(16, width), fixed(8, LANES)]
     out_shape += [jax.ShapeDtypeStruct((16, width), jnp.float32), jax.ShapeDtypeStruct((8, LANES), jnp.float32)]
@@ -580,20 +636,13 @@
             pltpu.VMEM((streams * block, width), jnp.float32),
             pltpu.VMEM((block, LANES), jnp.float32),
             pltpu.VMEM((2, GROUP, LANES), jnp.float32),
+            pltpu.VMEM((LANES, width), jnp.bfloat16),
         ],
+        input_output_aliases={len(arrays) + k: k for k in range(len(filled))},
         compiler_params=PARAMS,
-        cost_estimate=cost(30 if inner else 25),
+        cost_estimate=cost(30 if inner else 0),
         name="close_feedforward" if inner else "close_attention",
-    )(*arrays, *tokens)
-
-
-def mix_grads(weight_sum, small, streams, uses):
-    count = streams * uses
-    return (
-        small[0, :count].reshape(streams, uses),
-        (weight_sum[:uses] + weight_sum[uses : 2 * uses]).T,
-        jnp.sum(small[1, :count].reshape(streams, uses), axis=0),
-    )
+    )(*plain(arrays), *tokens)
 
 
 QUERY_ROWS = 256
@@ -713,12 +762,13 @@
         out_shape=[flat] * 4 + [jax.ShapeDtypeStruct(flat.shape, jnp.float32)],
         scratch_shapes=[pltpu.VMEM((total, HEAD_DIM), jnp.bfloat16)],
         compiler_params=PARAMS,
-        cost_estimate=cost(15),
+        cost_estimate=cost(),
         name="attend",
     )(mine, starts, cosine, sine, *[raw for raw in raw_blocks for _ in range(3)])
 
 
 def attend_back(heads_kept, grad_blocks, mine, starts, cosine, sine, tokens):
+    tokens = waits(tokens)
     size, block = len(grad_blocks), grad_blocks[0].shape[0]
     total, columns = heads_kept[0].shape
     heads = columns // HEAD_DIM
@@ -734,7 +784,7 @@
         out_shape=jax.ShapeDtypeStruct((total, 3 * columns), jnp.bfloat16),
         scratch_shapes=[pltpu.VMEM((total, HEAD_DIM), jnp.bfloat16)] + [pltpu.VMEM((total, HEAD_DIM), jnp.float32)] * 3,
         compiler_params=PARAMS,
-        cost_estimate=cost(18),
+        cost_estimate=cost(),
         name="attend_back",
     )(mine, starts, cosine, sine, *heads_kept, *grad_blocks, *tokens)
 
@@ -742,10 +792,11 @@
 UNIT_TILE = 512
 
 
-def forward_units_kernel(kept, *refs):
-    x_ref, gate_w_ref, up_w_ref, down_w_ref = refs[:4]
-    gate_ref, up_ref, partial_ref, rows_ref, hidden_ref = refs[4 + kept : 9 + kept]
-    x = x_ref[...]
+def forward_units_kernel(blocks, kept, *refs):
+    gate_w_ref, up_w_ref, down_w_ref = refs[blocks : blocks + 3]
+    gate_ref, up_ref, partial_ref, rows_ref, hidden_ref, mark_ref = refs[blocks + 3 + kept :]
+    mark_ref[...] = jnp.zeros_like(mark_ref)
+    x = jnp.concatenate([ref[...] for ref in refs[:blocks]], axis=0)
     gate, up = matmul(x, gate_w_ref[...]), matmul(x, up_w_ref[...])
     gate_ref[...] = gate
     up_ref[...] = up
@@ -764,9 +815,10 @@
 
 
 def backward_units_kernel(kept, *refs):
-    d_ref, gate_ref, up_ref, down_w_ref, gate_w_ref, up_w_ref = refs[:6]
-    partial_ref, rows_ref, d_gate_ref, d_up_ref = refs[6 + kept : 10 + kept]
-    d_out = d_ref[...]
+    first_ref, second_ref, gate_ref, up_ref, down_w_ref, gate_w_ref, up_w_ref = refs[:7]
+    partial_ref, rows_ref, d_gate_ref, d_up_ref, mark_ref = refs[7 + kept :]
+    mark_ref[...] = jnp.zeros_like(mark_ref)
+    d_out = jnp.concatenate([first_ref[...], second_ref[...]], axis=0)
     d_hidden = matmul(d_out, down_w_ref[...])
     gate = gate_ref[...]
     sigmoid = 1.0 / (1.0 + jnp.exp(-gate))
@@ -786,120 +838,425 @@
         partial_ref[...] += part
 
 
-def forward_units(step, size, x, gate_up, down, filled, passed, tokens):
-    rows, width = x.shape
+def forward_units(pair, size, blocks, gate_up, down, filled, tokens=()):
+    tokens = waits(tokens)
+    each, width = blocks[0].shape
+    count = len(blocks)
+    rows = each * count // 2
     units = down.shape[1]
     tile = min(UNIT_TILE, units)
     tiles = units // tile
     weight = functools.partial(pl.BlockSpec, (width, tile))
-    kept = len(filled) + len(passed) + len(tokens)
-    arrays = [x, gate_up, gate_up, down]
     outs = pl.pallas_call(
-        functools.partial(forward_units_kernel, kept),
+        functools.partial(forward_units_kernel, count, len(filled) + len(tokens)),
         grid=(tiles,),
-        in_specs=[
-            pl.BlockSpec((rows, width), lambda i: (0, 0)),
-            weight(lambda i: (0, i)),
-            weight(lambda i: (0, tiles + i)),
-            weight(lambda i: (0, i)),
-        ]
-        + anywhere(kept),
+        in_specs=[pl.BlockSpec((each, width), lambda i: (0, 0))] * count
+        + [weight(lambda i: (0, i)), weight(lambda i: (0, tiles + i)), weight(lambda i: (0, i))]
+        + anywhere(len(filled) + len(tokens)),
         out_specs=[
-            pl.BlockSpec((rows, tile), lambda i: (0, i)),
-            pl.BlockSpec((rows, tile), lambda i: (0, i)),
-            pl.BlockSpec((rows, width), lambda i: (0, 0)),
-            pl.BlockSpec((rows, width), lambda i: (step, 0)),
-            pl.BlockSpec((rows, tile), lambda i: (step, i)),
-        ]
-        + anywhere(len(passed)),
+            pl.BlockSpec((2 * rows, tile), lambda i: (0, i)),
+            pl.BlockSpec((2 * rows, tile), lambda i: (0, i)),
+            pl.BlockSpec((2 * rows, width), lambda i: (0, 0)),
+            pl.BlockSpec((2 * rows, width), lambda i: (pair, 0)),
+            pl.BlockSpec((2 * rows, tile), lambda i: (pair, i)),
+            MARK_SPEC,
+        ],
         out_shape=[
-            jax.ShapeDtypeStruct((rows, units), jnp.float32),
-            jax.ShapeDtypeStruct((rows, units), jnp.float32),
-            jax.ShapeDtypeStruct((rows, width), jnp.float32),
+            jax.ShapeDtypeStruct((2 * rows, units), jnp.float32),
+            jax.ShapeDtypeStruct((2 * rows, units), jnp.float32),
+            jax.ShapeDtypeStruct((2 * rows, width), jnp.float32),
             jax.ShapeDtypeStruct((size * rows, width), jnp.bfloat16),
             jax.ShapeDtypeStruct((size * rows, units), jnp.bfloat16),
-        ]
-        + [jax.ShapeDtypeStruct(a.shape, a.dtype) for a in passed],
-        input_output_aliases={
-            **{4 + k: 3 + k for k in range(len(filled))},
-            **{4 + len(filled) + k: 5 + k for k in range(len(passed))},
-        },
+            MARK_SHAPE,
+        ],
+        input_output_aliases={count + 3 + k: 3 + k for k in range(len(filled))},
         compiler_params=PARAMS,
-        cost_estimate=cost(9),
+        cost_estimate=cost(),
         name="forward_units",
-    )(*arrays, *filled, *passed, *tokens)
-    return outs[0], outs[1], outs[2], outs[3:5], outs[5:]
-
-
-def backward_units(step, size, d_out, gate, up, gate_up, down, filled, tokens):
-    rows, width = d_out.shape
+    )(*blocks, gate_up, gate_up, down, *filled, *tokens)
+    outs = marked(outs[:-1], outs[-1])
+    return outs[0], outs[1], outs[2], outs[3:]
+
+
+def backward_units(pair, size, blocks, gate, up, gate_up, down, filled, tokens=()):
+    tokens = waits(tokens)
+    rows, width = blocks[0].shape
     units = down.shape[1]
     tile = min(UNIT_TILE, units)
     tiles = units // tile
     weight = functools.partial(pl.BlockSpec, (width, tile))
-    kept = len(filled) + len(tokens)
-    by_tile = pl.BlockSpec((rows, tile), lambda i: (0, i))
+    by_tile = pl.BlockSpec((2 * rows, tile), lambda i: (0, i))
     outs = pl.pallas_call(
-        functools.partial(backward_units_kernel, kept),
+        functools.partial(backward_units_kernel, len(filled) + len(tokens)),
         grid=(tiles,),
-        in_specs=[
-            pl.BlockSpec((rows, width), lambda i: (0, 0)),
-            by_tile,
-            by_tile,
-            weight(lambda i: (0, i)),
-            weight(lambda i: (0, i)),
-            weight(lambda i: (0, tiles + i)),
-        ]
-        + anywhere(kept),
+        in_specs=[pl.BlockSpec((rows, width), lambda i: (0, 0))] * 2
+        + [by_tile, by_tile]
+        + [weight(lambda i: (0, i)), weight(lambda i: (0, i)), weight(lambda i: (0, tiles + i))]
+        + anywhere(len(filled) + len(tokens)),
         out_specs=[
-            pl.BlockSpec((rows, width), lambda i: (0, 0)),
-            pl.BlockSpec((rows, width), lambda i: (step, 0)),
-            pl.BlockSpec((rows, tile), lambda i: (step, i)),
-            pl.BlockSpec((rows, tile), lambda i: (step, i)),
+            pl.BlockSpec((2 * rows, width), lambda i: (0, 0)),
+            pl.BlockSpec((2 * rows, width), lambda i: (pair, 0)),
+            pl.BlockSpec((2 * rows, tile), lambda i: (pair, i)),
+            pl.BlockSpec((2 * rows, tile), lambda i: (pair, i)),
+            MARK_SPEC,
         ],
         out_shape=[
-            jax.ShapeDtypeStruct((rows, width), jnp.float32),
+            jax.ShapeDtypeStruct((2 * rows, width), jnp.float32),
             jax.ShapeDtypeStruct((size * rows, width), jnp.bfloat16),
             jax.ShapeDtypeStruct((size * rows, units), jnp.bfloat16),
             jax.ShapeDtypeStruct((size * rows, units), jnp.bfloat16),
+            MARK_SHAPE,
         ],
-        input_output_aliases={6 + k: 1 + k for k in range(len(filled))},
+        input_output_aliases={7 + k: 1 + k for k in range(len(filled))},
         compiler_params=PARAMS,
-        cost_estimate=cost(10),
+        cost_estimate=cost(),
         name="backward_units",
-    )(d_out, gate, up, down, gate_up, gate_up, *filled, *tokens)
+    )(*blocks, gate, up, down, gate_up, gate_up, *filled, *tokens)
+    outs = marked(outs[:-1], outs[-1])
     return outs[0], outs[1:]
 
 
-def assemble_kernel(count, pieces, table_ref, *refs):
-    out_ref = refs[-1]
+def assemble_kernel(count, pieces, kept, table_ref, *refs):
+    sources, outs, mark_ref = refs[:count], refs[count + kept : -1], refs[-1]
+    mark_ref[...] = jnp.zeros_like(mark_ref)
     for k in range(count):
 
         @pl.when(pl.program_id(0) // pieces == k)
         def _(k=k):
-            out_ref[...] = refs[k][...].astype(jnp.float32)
-
-
-def assemble(arrays, part, columns, table):
+            first = 0
+            for out_ref in outs:
+                columns = out_ref.shape[1]
+                out_ref[...] = sources[k][:, first : first + columns].astype(jnp.float32)
+                first += columns
+
+
+def assemble(arrays, widths, table, tokens=()):
+    tokens = waits(tokens)
     count = len(arrays)
-    pieces = table.shape[0] // count
-    rows = arrays[0].shape[0] // pieces
-    return pl.pallas_call(
-        functools.partial(assemble_kernel, count, pieces),
+    pieces = arrays[0][2]
+    rows, columns = arrays[0][3], arrays[0][0].shape[1]
+    *results, mark = pl.pallas_call(
+        functools.partial(assemble_kernel, count, pieces, len(tokens)),
         grid_spec=pltpu.PrefetchScalarGridSpec(
             num_scalar_prefetch=1,
             grid=(count * pieces,),
             in_specs=[
-                pl.BlockSpec((rows, columns), lambda i, t, k=k: (jnp.clip(i - k * pieces, 0, pieces - 1), part))
-                for k in range(count)
+                pl.BlockSpec(
+                    (rows, columns),
+                    lambda i, t, k=k, first=first: (first + jnp.clip(i - k * pieces, 0, pieces - 1), 0),
+                )
+                for k, (_, first, _, _) in enumerate(arrays)
+            ]
+            + anywhere(len(tokens)),
+            out_specs=[pl.BlockSpec((rows, width), lambda i, t: (t[i], 0)) for width in widths] + [MARK_SPEC],
+        ),
+        out_shape=[jax.ShapeDtypeStruct((count * pieces * rows, width), jnp.float32) for width in widths] + [MARK_SHAPE],
+        compiler_params=PARAMS,
+        cost_estimate=cost(),
+        name="assemble",
+    )(table, *(array for array, *_ in arrays), *tokens)
+    return marked(results, mark)
+
+
+PRODUCT_TILE = 1024
+
+
+def across_of(width, first):
+    if width <= 2 * PRODUCT_TILE and first % width == 0:
+        return width if width * 3 <= 5 * PRODUCT_TILE else width // 2
+    return math.gcd(PRODUCT_TILE, width, first or width)
+
+
+def joined_left(refs):
+    left = [ref[...] for ref in refs]
+    return left[0] if len(left) == 1 else jnp.concatenate(left, axis=0)
+
+
+def away_kernel(blocks, core_ref, *refs):
+    refs[-1][...] = jnp.zeros_like(refs[-1])
+    refs[-2][...] = transposed_times(joined_left(refs[:blocks]), refs[blocks][...]).astype(jnp.bfloat16)
+
+
+def own_kernel(blocks, scalars_ref, *refs):
+    away_ref, kept_ref, mark_ref = refs[-3:]
+    mark_ref[...] = jnp.zeros_like(mark_ref)
+    product = transposed_times(joined_left(refs[:blocks]), refs[blocks][...])
+    product = product + refs[blocks + 1][...].astype(jnp.float32)
+
+    @pl.when(pl.program_id(0) == 0)
+    def _():
+        away_ref[...] = product.astype(jnp.bfloat16)
+
+    @pl.when(pl.program_id(0) == 1)
+    def _():
+        kept_ref[...] = product
+
+
+def away_product(core, left, right, columns, first, filled, tokens=()):
+    tokens = waits(tokens)
+    half = left[0].shape[1] // 2
+    rows, width = right.shape
+    down, across = min(PRODUCT_TILE, half), across_of(width, first)
+    high, offset = half // down, first // across
+    result, mark = pl.pallas_call(
+        functools.partial(away_kernel, len(left)),
+        grid_spec=pltpu.PrefetchScalarGridSpec(
+            num_scalar_prefetch=1,
+            grid=(high, width // across),
+            in_specs=[
+                pl.BlockSpec((block.shape[0], down), lambda i, j, c: (0, (1 - c[0]) * high + i)) for block in left
+            ]
+            + [pl.BlockSpec((rows, across), lambda i, j, c: (0, j))]
+            + anywhere(len(filled) + len(tokens)),
+            out_specs=[pl.BlockSpec((down, across), lambda i, j, c: (i, offset + j)), MARK_SPEC],
+        ),
+        out_shape=[jax.ShapeDtypeStruct((half, columns), jnp.bfloat16), MARK_SHAPE],
+        input_output_aliases={2 + len(left): 0} if filled else {},
+        compiler_params=PARAMS,
+        cost_estimate=cost(),
+        name="away_product",
+    )(core, *left, right, *filled, *tokens)
+    return marked([result], mark)[0]
+
+
+def own_product(scalars, left, right, arrived, columns, first, rows_first, rows_here, filled, tokens=()):
+    tokens = waits(tokens)
+    half = left[0].shape[1] // 2
+    rows, width = right.shape
+    cut = rows_here // 2
+    down, across = min(PRODUCT_TILE, cut), across_of(width, first)
+    high, wide, offset = cut // down, width // across, first // across
+
+    def row(g, i, c):
+        return rows_first // down + jnp.where(g == 0, 1 - c[1], c[1]) * high + i
+
+    *results, mark = pl.pallas_call(
+        functools.partial(own_kernel, len(left)),
+        grid_spec=pltpu.PrefetchScalarGridSpec(
+            num_scalar_prefetch=1,
+            grid=(2, high, wide),
+            in_specs=[
+                pl.BlockSpec((block.shape[0], down), lambda g, i, j, c: (0, c[0] * (half // down) + row(g, i, c)))
+                for block in left
+            ]
+            + [
+                pl.BlockSpec((rows, across), lambda g, i, j, c: (0, j)),
+                pl.BlockSpec((down, across), lambda g, i, j, c: (row(g, i, c), offset + j)),
+            ]
+            + anywhere(len(filled) + len(tokens)),
+            out_specs=[
+                pl.BlockSpec(
+                    (down, across),
+                    lambda g, i, j, c: (jnp.where(g == 0, i, high - 1), offset + jnp.where(g == 0, j, wide - 1)),
+                ),
+                pl.BlockSpec(
+                    (down, across),
+                    lambda g, i, j, c: (jnp.where(g == 0, 0, i), offset + jnp.where(g == 0, 0, j)),
+                ),
+                MARK_SPEC,
             ],
-            out_specs=pl.BlockSpec((rows, columns), lambda i, t: (t[i], 0)),
         ),
-        out_shape=jax.ShapeDtypeStruct((count * arrays[0].shape[0], columns), jnp.float32),
+        out_shape=[
+            jax.ShapeDtypeStruct((cut, columns), jnp.bfloat16),
+            jax.ShapeDtypeStruct((cut, columns), jnp.float32),
+            MARK_SHAPE,
+        ],
+        input_output_aliases={3 + len(left) + k: k for k in range(len(filled))},
         compiler_params=PARAMS,
-        cost_estimate=cost(8 * columns / 2048),
-        name="assemble",
-    )(table, *arrays)
+        cost_estimate=cost(),
+        name="own_product",
+    )(scalars, *left, right, arrived, *filled, *tokens)
+    return marked(results, mark)
+
+
+def backproject_kernel(d_ref, w_ref, *refs):
+    refs[-1][...] = jnp.zeros_like(refs[-1])
+    refs[-2][...] = times_transposed(d_ref[...], w_ref[...]).astype(refs[-2].dtype)
+
+
+def backproject(rows_of, first, count, weight, kind, tokens=()):
+    tokens = waits(tokens)
+    array, rows = rows_of
+    width, columns = weight.shape
+    across = min(512, width)
+    result, mark = pl.pallas_call(
+        backproject_kernel,
+        grid=(width // across, count),
+        in_specs=[
+            pl.BlockSpec((rows, columns), lambda j, i: (first + i, 0)),
+            pl.BlockSpec((across, columns), lambda j, i: (j, 0)),
+        ]
+        + anywhere(len(tokens)),
+        out_specs=[pl.BlockSpec((rows, across), lambda j, i: (i, j)), MARK_SPEC],
+        out_shape=[jax.ShapeDtypeStruct((count * rows, width), kind), MARK_SHAPE],
+        compiler_params=PARAMS,
+        cost_estimate=cost(),
+        name="backproject",
+    )(array, weight, *tokens)
+    return marked([result], mark)[0]
+
+
+def project_kernel(count, *refs):
+    refs[-1][...] = matmul(jnp.concatenate([ref[...] for ref in refs[:count]], axis=0), refs[count][...]).astype(jnp.bfloat16)
+
+
+def project(blocks, weight, columns):
+    rows, width = blocks[0].shape
+    across = min(256, columns)
+    return pl.pallas_call(
+        functools.partial(project_kernel, len(blocks)),
+        grid=(columns // across,),
+        in_specs=[pl.BlockSpec((rows, width), lambda j: (0, 0))] * len(blocks)
+        + [pl.BlockSpec((width, across), lambda j: (0, j))],
+        out_specs=pl.BlockSpec((len(blocks) * rows, across), lambda j: (0, j)),
+        out_shape=jax.ShapeDtypeStruct((len(blocks) * rows, columns), jnp.bfloat16),
+        compiler_params=PARAMS,
+        cost_estimate=cost(),
+        name="project",
+    )(*blocks, weight)
+
+
+def out_project_kernel(count, *refs):
+    refs[-1][...] = times_transposed(jnp.concatenate([ref[...] for ref in refs[:count]], axis=1), refs[count][...])
+
+
+def out_project(blocks, weight):
+    rows = blocks[0].shape[0]
+    width, columns = weight.shape
+    across = min(512, width)
+    return pl.pallas_call(
+        functools.partial(out_project_kernel, len(blocks)),
+        grid=(width // across,),
+        in_specs=[pl.BlockSpec(block.shape, lambda j: (0, 0)) for block in blocks]
+        + [pl.BlockSpec((across, columns), lambda j: (j, 0))],
+        out_specs=pl.BlockSpec((rows, across), lambda j: (0, j)),
+        out_shape=jax.ShapeDtypeStruct((rows, width), jnp.float32),
+        compiler_params=PARAMS,
+        cost_estimate=cost(),
+        name="out_project",
+    )(*blocks, weight)
+
+
+SUM_ROWS = 256
+
+
+def halve_kernel(which_ref, own_ref, arrived_ref, *refs):
+    away_ref, kept_ref, mark_ref = refs[-3:]
+    mark_ref[...] = jnp.zeros_like(mark_ref)
+    total = own_ref[...] + arrived_ref[...].astype(jnp.float32)
+
+    @pl.when(pl.program_id(0) == 0)
+    def _():
+        away_ref[...] = total.astype(jnp.bfloat16)
+
+    @pl.when(pl.program_id(0) == 1)
+    def _():
+        kept_ref[...] = total
+
+
+def halve(own, arrived, which, tokens=()):
+    tokens = waits(tokens)
+    (own, own_first, rows), (arrived, arrived_first, _) = own, arrived
+    half, columns = rows // 2, own.shape[1]
+    tile = min(SUM_ROWS, half)
+    tiles = half // tile
+
+    def source(first):
+        return pl.BlockSpec(
+            (tile, columns), lambda g, t, w: (first // tile + jnp.where(g == 0, 1 - w[0], w[0]) * tiles + t, 0)
+        )
+
+    *results, mark = pl.pallas_call(
+        halve_kernel,
+        grid_spec=pltpu.PrefetchScalarGridSpec(
+            num_scalar_prefetch=1,
+            grid=(2, tiles),
+            in_specs=[source(own_first), source(arrived_first)] + anywhere(len(tokens)),
+            out_specs=[
+                pl.BlockSpec((tile, columns), lambda g, t, w: (jnp.where(g == 0, t, tiles - 1), 0)),
+                pl.BlockSpec((tile, columns), lambda g, t, w: (jnp.where(g == 0, 0, t), 0)),
+                MARK_SPEC,
+            ],
+        ),
+        out_shape=[
+            jax.ShapeDtypeStruct((half, columns), jnp.bfloat16),
+            jax.ShapeDtypeStruct((half, columns), jnp.float32),
+            MARK_SHAPE,
+        ],
+        compiler_params=PARAMS,
+        cost_estimate=cost(),
+        name="halve",
+    )(which, own, arrived, *tokens)
+    return marked(results, mark)
+
+
+def add_kernel(own, arrives, *refs):
+    out_ref, mark_ref = refs[-2:]
+    mark_ref[...] = jnp.zeros_like(mark_ref)
+    rows = out_ref.shape[0] // own
+    for k in range(own):
+        values = refs[k][...].astype(jnp.float32)
+        if arrives:
+            values = values + refs[own + k][...].astype(jnp.float32)
+        out_ref[k * rows : (k + 1) * rows, :] = values.astype(out_ref.dtype)
+
+
+def add_low(own, arrived=(), tokens=(), kind=jnp.bfloat16):
+    tokens = waits(tokens)
+    rows, columns = own[0][2], own[0][0].shape[1]
+    across = min(512, columns)
+    total = rows * len(own)
+    ranges = [*own, *arrived]
+    result, mark = pl.pallas_call(
+        functools.partial(add_kernel, len(own), bool(arrived)),
+        grid=(columns // across,),
+        in_specs=[
+            pl.BlockSpec((rows, across), lambda j, first=first // rows: (first, j)) for _, first, rows in ranges
+        ]
+        + anywhere(len(tokens)),
+        out_specs=[pl.BlockSpec((total, across), lambda j: (0, j)), MARK_SPEC],
+        out_shape=[jax.ShapeDtypeStruct((total, columns), kind), MARK_SHAPE],
+        compiler_params=PARAMS,
+        cost_estimate=cost(),
+        name="add_low",
+    )(*(array for array, _, _ in ranges), *tokens)
+    return marked([result], mark)[0]
+
+
+def whole_range(array):
+    return (array, 0, array.shape[0])
+
+
+def join_kernel(count, tiles, *refs):
+    out_ref, mark_ref = refs[-2:]
+    mark_ref[...] = jnp.zeros_like(mark_ref)
+    for k in range(count):
+
+        @pl.when(pl.program_id(0) // tiles == k)
+        def _(k=k):
+            out_ref[...] = refs[k][...]
+
+
+def join(arrays, tokens=()):
+    tokens = waits(tokens)
+    rows, columns = arrays[0].shape
+    tile = min(2 * SUM_ROWS, rows)
+    tiles = rows // tile
+    result, mark = pl.pallas_call(
+        functools.partial(join_kernel, len(arrays), tiles),
+        grid=(len(arrays) * tiles,),
+        in_specs=[
+            pl.BlockSpec((tile, columns), lambda i, k=k: (jnp.clip(i - k * tiles, 0, tiles - 1), 0))
+            for k in range(len(arrays))
+        ]
+        + anywhere(len(tokens)),
+        out_specs=[pl.BlockSpec((tile, columns), lambda i: (i, 0)), MARK_SPEC],
+        out_shape=[jax.ShapeDtypeStruct((len(arrays) * rows, columns), arrays[0].dtype), MARK_SHAPE],
+        compiler_params=PARAMS,
+        cost_estimate=cost(),
+        name="join",
+    )(*arrays, *tokens)
+    return marked([result], mark)[0]
 
 
 def ring_shift(block):
@@ -914,13 +1271,26 @@
     return blocks
 
 
-def ring_scatter(partials):
-    total = partials[1 % len(partials)]
-    for step in range(2, len(partials) + 1):
-        arrived = ring_shift(total.astype(jnp.bfloat16))
-        own = partials[step % len(partials)]
-        total = arrived.astype(jnp.float32) + own
-    return arrived, own
+def row_halves(ranges):
+    return [
+        [(array, first + k * (rows // 2), rows // 2) for array, first, rows in ranges] for k in range(2)
+    ]
+
+
+def ring_sums(step, size, ranges, arrived, tokens):
+    if step < size - 1:
+        return [add_low(ranges, arrived, tokens)]
+    arrived = row_halves(arrived) if arrived else ((), ())
+    return [add_low(own, other, tokens) for own, other in zip(row_halves(ranges), arrived)]
+
+
+def own_columns(attended):
+    blocks = jnp.split(attended, lax.axis_size("tensor"))
+    size = len(blocks)
+    return [blocks[0]] + [
+        lax.ppermute(blocks[size - step], "tensor", [(i, (i + step) % size) for i in range(size)])
+        for step in range(1, size)
+    ]
 
 
 def swap(values, axis, bit):
@@ -936,32 +1306,76 @@
     return list(range(1, bits)), list(range(bits - 1, 0, -1))
 
 
-def core_products(pairs):
-    half = pairs[0][0].shape[1] // 2
-    core = bit_of("dp", 0)
-
-    def products(which):
-        each = [
-            transposed_times(lax.dynamic_slice_in_dim(left, which * half, half, 1), right) for left, right in pairs
+class Butterfly:
+    def __init__(self, halved, orders):
+        self.orders, self.level, self.levels = orders, 0, len(orders[0])
+        self.ready, self.kept = [away for away, _ in halved], [kept for _, kept in halved]
+
+    def step(self, *after):
+        level, levels = self.level, self.levels
+        if level == 2 * levels:
+            return self
+        bits = [order[level] if level < levels else order[2 * levels - 1 - level] for order in self.orders]
+        arrived = [swap(away, "dp", bit) for away, bit in zip(self.ready, bits)]
+        self.level += 1
+        if self.level < levels:
+            halved = [
+                halve(
+                    (kept, 0, kept.shape[0]),
+                    (other, 0, kept.shape[0]),
+                    jnp.full((1,), bit_of("dp", order[self.level]), jnp.int32),
+                    after,
+                )
+                for kept, other, order in zip(self.kept, arrived, self.orders)
+            ]
+            self.ready, self.kept = [away for away, _ in halved], [kept for _, kept in halved]
+        elif self.level == levels:
+            self.ready = [
+                add_low([whole_range(kept)], [whole_range(other)], after) for kept, other in zip(self.kept, arrived)
+            ]
+        elif self.level < 2 * levels:
+            self.ready = [join(both, after) for both in zip(self.ready, arrived)]
+        else:
+            self.ready = [join([array for both in zip(self.ready, arrived) for array in both], after)]
+        return self
+
+    def gathered(self, *after):
+        while self.level < 2 * self.levels:
+            self.step(*after)
+        return self.ready[0]
+
+
+def own_scalars(order):
+    return jnp.stack([bit_of("dp", 0), bit_of("dp", order[0])]).astype(jnp.int32)
+
+
+def pieces_of(joined, parts, part=None):
+    count = parts << ((lax.axis_size("dp") - 1).bit_length() - 1)
+    rows = joined.shape[0] // count
+    each = count // parts
+    return [
+        (half, 0, count, rows) if part is None else (half, part * each, each, rows)
+        for half in (joined, swap(joined, "dp", 0))
+    ]
+
+
+class SumEverywhere:
+    def __init__(self, values):
+        self.values = values
+        self.left = [
+            (axis, bit) for axis in ("tensor", "dp") for bit in range((lax.axis_size(axis) - 1).bit_length())
         ]
-        return each[0] if len(each) == 1 else jnp.concatenate(each, axis=1)
-
-    arrived = swap(products(1 - core).astype(jnp.bfloat16), "dp", 0)
-    return products(core) + arrived.astype(jnp.float32)
-
-
-def butterfly(part, order):
-    marks = []
-    for bit in order:
-        rows, which = part.shape[0] // 2, bit_of("dp", bit)
-        away = lax.dynamic_slice_in_dim(part, (1 - which) * rows, rows).astype(jnp.bfloat16)
-        arrived = swap(away, "dp", bit)
-        marks += [away, arrived]
-        part = lax.dynamic_slice_in_dim(part, which * rows, rows) + arrived.astype(jnp.float32)
-    part = part.astype(jnp.bfloat16)
-    for bit in reversed(order):
-        part = jnp.concatenate([part, swap(part, "dp", bit)])
-    return part, marks
+
+    def step(self, *after):
+        axis, bit = self.left.pop(0)
+        arrived = swap(self.values, axis, bit)
+        self.values = add_low([whole_range(self.values)], [whole_range(arrived)], after, jnp.float32)
+        return self.values
+
+    def finished(self, last):
+        while len(self.left) > last:
+            self.step()
+        return self.values
 
 
 def piece_rows(orders):
@@ -977,17 +1391,6 @@
                     row = row * 2 + (bit_of("dp", bit) ^ digit)
                 entries.append((core * len(orders) + k) * (1 << levels) + row)
     return jnp.stack(entries).astype(jnp.int32)
-
-
-def with_partner(parts):
-    return [*parts, *(swap(part, "dp", 0) for part in parts)]
-
-
-def sum_everywhere(values):
-    for axis in ("dp", "tensor"):
-        for bit in range((lax.axis_size(axis) - 1).bit_length()):
-            values = values + swap(values, axis, bit)
-    return values
 
 
 def segments_from(slot_lengths, group_rows):
@@ -1036,8 +1439,8 @@
     mix_weight,
     mix_scale,
 ):
+    MARKS.clear()
     qkv_full = gather_rows(query_weight, key_weight, value_weight)
-    out_full = gather_rows(out_weight)
     gate_up_full = gather_rows(gate_weight, up_weight)
     down_full = gather_rows(down_weight)
     local_rows, count, width = streams.shape
@@ -1047,6 +1450,7 @@
     group_rows = local_rows * size
     mine = lax.axis_index("tensor")
     place_index = jnp.full((1,), mine, jnp.int32)
+    core = jnp.full((1,), bit_of("dp", 0), jnp.int32)
     units = gate_weight.shape[1]
     seq_count = permutation.shape[0] // lax.axis_size("dp")
 
@@ -1060,104 +1464,228 @@
     local_segment = lax.dynamic_slice_in_dim(segment, mine * local_rows, local_rows)
     valid = jnp.broadcast_to((local_segment < seq_count).astype(jnp.float32)[:, None], (local_rows, LANES))
 
+    others = [
+        lax.ppermute(out_weight, "tensor", [(i, (i + step) % size) for i in range(size)]) for step in range(1, size)
+    ]
     normed_a, saved_a = open_attention(inputs, tables_a, *sizes)
+    out_full = gather_rows(out_weight, *hold(others, normed_a))
     input_blocks = ring_gather(normed_a)
     query, key, value, attended, log_totals = attend(
         [matmul(block, qkv_full) for block in input_blocks], place_index, starts, cosine, sine
     )
-    arrived_a, own_a = ring_scatter([times_transposed(block, out_full) for block in jnp.split(attended, size)])
-    normed_f, d_out_f, saved_f, middle, out_a = open_feedforward(
-        inputs, saved_a, arrived_a, own_a, cotangents, valid, tables_f, *sizes
+    out_a = out_project(own_columns(attended), out_full)
+    half_rows = local_rows // 2
+    normed_f, d_out_f, saved_f, middle = open_feedforward(
+        inputs, saved_a, out_a, cotangents, valid, tables_f, *sizes
     )
-    feedforward_blocks = ring_gather(normed_f)
-    gates, ups, partials_f, filled = [], [], [], []
-    for step, block in enumerate(feedforward_blocks):
-        last = step == size - 1
-        passed = [d_out_f] if step == size - 2 else [partials_f[1].astype(jnp.bfloat16)] if last and step > 1 else []
-        gate, up, partial, filled, passed = forward_units(step, size, block, gate_up_full, down_full, filled, passed, [])
+    orders = axis_orders()
+    steps = 2 * len(orders[0])
+    whole_table, half_tables = piece_rows(orders), [piece_rows([order]) for order in orders]
+
+    def pair_of(arrays, pair):
+        return arrays[2 * pair : 2 * pair + 2]
+
+    blocks, gates, ups, partials_f, filled = [normed_f], [], [], [], []
+
+    def forward(pair, filled):
+        gate, up, partial, filled = forward_units(pair, size, pair_of(blocks, pair), gate_up_full, down_full, filled)
         gates.append(gate)
         ups.append(up)
         partials_f.append(partial)
-        if step == size - 2:
-            (d_out_f,) = passed
-        elif last and step > 1:
-            partials_f[1] = passed[0]
+        return filled
+
+    for step in range(1, size):
+        blocks.append(ring_shift(blocks[-1]))
+        if step % 2 == 0:
+            filled = forward(step // 2 - 1, filled)
+    last_pair = size // 2 - 1
+    grads, partials_n, filled_back = list(hold([d_out_f], blocks[-1], *partials_f)), [], []
+    for step in range(1, size):
+        arrived = ring_shift(grads[-1])
+        if step == 1:
+            filled = forward(last_pair, filled)
+            (arrived,) = hold([arrived], partials_f[-1])
+        elif step % 2 == 0:
+            pair = step // 2 - 1
+            partial, filled_back = backward_units(
+                pair, size, pair_of(grads, pair), gates[pair], ups[pair], gate_up_full, down_full, filled_back
+            )
+            partials_n.append(partial)
+            (arrived,) = hold([arrived], partial)
+        grads.append(arrived)
     feedforward_rows, hidden_rows = filled
-    partials_n, filled = [], []
-    for step, grad in enumerate(ring_gather(d_out_f)):
-        partial, filled = backward_units(step, size, grad, gates[step], ups[step], gate_up_full, down_full, filled, [])
-        partials_n.append(partial)
-    grad_rows, d_gate_rows, d_up_rows = filled
-    arrived_f, own_f = ring_scatter(partials_f)
-    out_streams = finish(middle, saved_f, arrived_f, own_f, *sizes)
-    arrived_n, own_n = ring_scatter(partials_n)
-
-    orders = axis_orders()
-    whole_table, half_tables = piece_rows(orders), [piece_rows([order]) for order in orders]
-    down_parts = [
-        butterfly(part, order) for part, order in zip(jnp.split(core_products([(grad_rows, hidden_rows)]), 2), orders)
-    ]
-    gate_up_parts = [
-        butterfly(core_products([(feedforward_rows, grads)]), order)
-        for grads, order in zip((d_gate_rows, d_up_rows), orders)
-    ]
-    middle_grad, d_out_a, d_branch_a, weight_sum_f, small_f = close_mix(
-        True,
-        [middle, saved_f, cotangents, arrived_n, own_n, arrived_f, own_f, valid, saved_a, out_a],
-        tables_f,
-        *sizes,
-        tokens=[marks[0] for _, marks in gate_up_parts],
+
+    def both_parts(index):
+        first = (index % 2) * local_rows
+        return [(partials_f[index // 2], first, local_rows), (partials_n[index // 2], first, local_rows)]
+
+    half = width // 2
+    totals = ring_sums(1, size, both_parts(1), (), [grads[-1]])
+    for step in range(2, size + 1):
+        arrived, total = [ring_shift(one) for one in totals], totals[0]
+        tokens = []
+        if step == 2:
+            partial, filled_back = backward_units(
+                last_pair,
+                size,
+                pair_of(grads, last_pair),
+                gates[last_pair],
+                ups[last_pair],
+                gate_up_full,
+                down_full,
+                filled_back,
+                [total],
+            )
+            partials_n.append(partial)
+            grad_rows, *unit_rows = filled_back
+            aways = [away_product(core, [feedforward_rows], rows, units, 0, []) for rows in unit_rows]
+            tokens = aways
+        elif step == 3:
+            others = [swap(away, "dp", 0) for away in hold(aways, total)]
+            down_away = away_product(core, [grad_rows], hidden_rows, units, 0, [], [total])
+            gate_up_sum = Butterfly(
+                [
+                    own_product(own_scalars(order), [feedforward_rows], rows, other, units, 0, 0, half, [], [down_away])
+                    for order, rows, other in zip(orders, unit_rows, others)
+                ],
+                orders,
+            )
+            tokens = [*gate_up_sum.ready, down_away]
+        elif step == 4:
+            down_other = swap(*hold([down_away], total), "dp", 0)
+            down_sum = Butterfly(
+                [
+                    own_product(
+                        own_scalars(order), [grad_rows], hidden_rows, down_other, units, 0, k * half // 2, half // 2, [], [total]
+                    )
+                    for k, order in enumerate(orders)
+                ],
+                orders,
+            )
+            tokens = down_sum.ready
+        if step < size:
+            here = [(arrived[0], 0, local_rows), (arrived[0], local_rows, local_rows)]
+            totals = ring_sums(step, size, both_parts(step), here, tokens)
+    filled, sums_f = [], []
+    for k, both in enumerate(arrived):
+        first = k * half_rows
+        own_f, own_n = (partials_f[0], first), (partials_n[0], first)
+        rest = [(a, first) for a in (valid, saved_a, out_a)]
+        arrays = [(a, first) for a in (middle, saved_f, cotangents)]
+        *filled, weight_sum, small = close_mix(
+            True,
+            first,
+            half_rows,
+            [*arrays, (both, half_rows), own_n, (both, 0), own_f, *rest],
+            tables_f,
+            *sizes,
+            filled,
+            tokens,
+        )
+        sums_f.append((weight_sum, small))
+        tokens = []
+    middle_grad, d_branch_a, d_out_a = filled
+
+    def finished(tokens):
+        filled = []
+        for k, both in enumerate(arrived_last):
+            filled = [finish(k * half_rows, middle, saved_f, (both, 0, half_rows), partials_f[0], *sizes, filled, tokens)]
+        return filled[0]
+
+    arrived_last = arrived
+
+    output_grads = [d_out_a]
+    for step in range(1, size):
+        arrived = ring_shift(output_grads[-1])
+        after = output_grads[-1]
+        tokens = []
+        if step == 1:
+            out_streams = finished([after])
+            tokens = [*gate_up_sum.step(after).ready, *down_sum.step(after).ready, out_streams]
+        elif step == 2:
+            tokens = gate_up_sum.step(after).ready
+        if tokens:
+            (arrived,) = hold([arrived], *tokens)
+        output_grads.append(arrived)
+        if step == 3:
+            tokens = gate_up_sum.step(after).ready
+    attended_grads = [project([block], out_full, attended.shape[1]) for block in output_grads]
+    output_rows = output_grads
+    d_qkv = attend_back(
+        [query, key, value, log_totals], attended_grads, place_index, starts, cosine, sine, tokens
     )
-    down_grad = assemble(with_partner([part for part, _ in down_parts]), 0, units, whole_table)
-    gate_grad, up_grad = (
-        assemble(with_partner([part]), 0, units, table) for (part, _), table in zip(gate_up_parts, half_tables)
-    )
-    output_grads = ring_gather(d_out_a)
-    attended_grads = [matmul(block, out_full).astype(jnp.bfloat16) for block in output_grads]
-    d_qkv = attend_back(
-        [query, key, value, log_totals],
-        attended_grads,
-        place_index,
-        starts,
-        cosine,
-        sine,
-        [marks[-1] for _, marks in [*gate_up_parts, *down_parts]],
-    )
-    arrived_i, own_i = ring_scatter([times_transposed(block, qkv_full) for block in jnp.split(d_qkv, size)])
-    attention_parts = [
-        butterfly(part, order)
-        for part, order in zip(
-            jnp.split(
-                core_products([(jnp.concatenate(output_grads), attended), (jnp.concatenate(input_blocks), d_qkv)]), 2
-            ),
-            orders,
-        )
-    ]
+    total = backproject((d_qkv, local_rows), 1, 1, qkv_full, jnp.bfloat16)
+    columns = attended.shape[1]
+    for step in range(2, size + 1):
+        arrived = ring_shift(total)
+        tokens = []
+        if step == 2:
+            away = away_product(core, input_blocks, d_qkv, 4 * columns, 0, [], [total])
+            away = away_product(core, output_rows, attended, 4 * columns, 3 * columns, [away])
+            own_partials = [backproject((d_qkv, local_rows), 2, 1, qkv_full, jnp.float32, [away])]
+            gate_up_joined = gate_up_sum.gathered(*own_partials)
+            tokens = [away, gate_up_joined, *down_sum.step(*own_partials).ready]
+        elif step == 3:
+            (away,) = hold([away], total)
+            other = swap(away, "dp", 0)
+            own_partials.append(backproject((d_qkv, local_rows), 3 % size, size - 3, qkv_full, jnp.float32, [total]))
+            halved = []
+            for k, order in enumerate(orders):
+                place = (4 * columns, 0, k * half // 2, half // 2)
+                scalars = own_scalars(order)
+                both = own_product(scalars, input_blocks, d_qkv, other, *place, [], [own_partials[-1]])
+                place = (4 * columns, 3 * columns, k * half // 2, half // 2)
+                halved.append(own_product(scalars, output_rows, attended, other, *place, both))
+            attention_sum = Butterfly(halved, orders)
+            tokens = [*attention_sum.ready, *down_sum.step(*attention_sum.ready).ready]
+        elif step == 4:
+            (gate_up_joined,) = hold([gate_up_joined], total)
+            gate_pieces, up_pieces = (pieces_of(gate_up_joined, 2, k) for k in range(2))
+            own_partial = backproject((d_qkv, local_rows), 0, 1, qkv_full, jnp.float32, [total])
+            (gate_grad,) = assemble(gate_pieces, [units], half_tables[0], [own_partial])
+            tokens = attention_sum.step(gate_grad).ready
+        if step < size:
+            place = (own_partials[0], 0) if step == 2 else (own_partials[1], (step - 3) * local_rows)
+            total = add_low([(*place, local_rows)], [whole_range(arrived)], tokens)
+    arrays = [(a, 0) for a in (inputs, saved_a, middle_grad, arrived, own_partial, d_branch_a)]
     input_grad, weight_sum_a, small_a = close_mix(
         False,
-        [inputs, saved_a, middle_grad, arrived_i, own_i, d_branch_a],
+        0,
+        local_rows,
+        arrays,
         tables_a,
         *sizes,
-        tokens=[marks[1] for _, marks in attention_parts] + [down_grad, gate_grad, up_grad],
-    )
-    attention_halves = with_partner([part for part, _ in attention_parts])
-    out_grad, query_grad, key_grad, value_grad = (
-        assemble(attention_halves, part, out_weight.shape[1], whole_table) for part in range(4)
+        tokens=tokens,
     )
     height = width // LANES
-    taken = 2 * uses * height
 
     def flat(weight_sum, small):
-        return jnp.concatenate([weight_sum.reshape(weight_sum.shape[0] * height, LANES)[:taken], small])
-
-    sums = sum_everywhere(jnp.concatenate([flat(weight_sum_a, small_a), flat(weight_sum_f, small_f)]))
-    (static_a, weight_a, scale_a), (static_f, weight_f, scale_f) = (
-        mix_grads(part[:taken].reshape(2 * uses, width), part[taken:], *sizes) for part in jnp.split(sums, 2)
+        summed = weight_sum[:uses] + weight_sum[8 : 8 + uses]
+        return jnp.concatenate([summed.reshape(uses * height, LANES), small])
+
+    def unpacked(sums):
+        constants = sums[uses * height : uses * height + 2, : count * uses].reshape(2, count, uses)
+        return constants[0], sums[: uses * height].reshape(uses, width).T, jnp.sum(constants[1], axis=0)
+
+    weight_sum_f, small_f = (one + other for one, other in zip(*sums_f))
+    sums = SumEverywhere(jnp.concatenate([flat(weight_sum_f, small_f), flat(weight_sum_a, small_a)]))
+    attention_sum.step(small_a)
+    (up_grad,) = assemble(up_pieces, [units], half_tables[1], [sums.values, *attention_sum.ready])
+    attention_sum.step(sums.step(up_grad))
+    down_joined = down_sum.gathered(*attention_sum.ready)
+    after = sums.step(down_joined)
+    (down_grad,) = assemble(pieces_of(down_joined, 2), [units], whole_table, [after])
+    attention_joined = attention_sum.gathered(sums.step(down_grad))
+    after = sums.step(attention_joined)
+    query_grad, key_grad, value_grad, out_grad = assemble(
+        pieces_of(attention_joined, 2), [columns] * 4, whole_table, [sums.finished(0)]
     )
-    shape = streams.shape
+    (static_f, weight_f, scale_f), (static_a, weight_a, scale_a) = (
+        unpacked(part) for part in jnp.split(sums.finished(0), 2)
+    )
     return (
-        out_streams.reshape(shape),
-        input_grad.reshape(shape),
+        out_streams,
+        input_grad,
         query_grad,
         key_grad,
         value_grad,

time: 983 us -> 896 us (0.911)
  Pallas kernels: 327 us -> 486 us
  matrix products: 106 us -> 16 us
  waiting for transfers between devices: 324 us -> 236 us
  other arithmetic: 58.8 us -> 11.8 us
  local copies, waits for them, and re-layouts: 99.7 us -> 62.8 us
  starting transfers between devices: 41.1 us -> 58.9 us
    pallas_call x15 -> x72, Pallas kernels: 198 us -> 347 us  [the longest x8 58.2 us: own_product(): pl.pallas_call(functools.partial(own_kernel, len(left)), grid_spec=pltpu....]
    dot_general x18 -> x0, matrix products: 83.9 us -> none  [the longest x10 60.2 us: transposed_times(): lax.dot_general(left, right, (((0,), (0,)), ((), ())), preferred_element_...]
    ppermute x39 -> x36, waiting for transfers between devices: 90.3 us -> 24.4 us  [swap(): lax.ppermute(values, axis, [(i, i ^ 1 << bit) for i in range(lax.axis_siz...]
    ppermute x24 -> x19, waiting for transfers between devices: 233 us -> 182 us  [ring_shift(): lax.ppermute(block, 'tensor', [(i, (i + 1) % size) for i in range(size)])]
    concatenate x17 -> x1, other arithmetic: 27.2 us -> 0.01 us  [per_device(): jnp.concatenate([flat(weight_sum_f, small_f), flat(weight_sum_a, small_a)])]
    all_gather x4, waiting for transfers between devices: 0.06 us -> 22.1 us  [gather_rows(): lax.all_gather(jnp.concatenate(weights, axis=1), 'dp', axis=0, tiled=True)]
    another operation x29 -> x7, local copies, waits for them, and re-layouts: 18.3 us -> 0.34 us  [mix_tables(): constants = jnp.stack([static.reshape(count), jnp.tile(scale, streams)])]
    unnamed x162 -> x221, local copies, waits for them, and re-layouts: 41.8 us -> 59.3 us
  transfers between devices with their start and end apart: 67 -> 65, of which waited for: 29 -> 27; matrix products, arithmetic and copies ran while one was open for 25% -> 5% of each run, Pallas kernels for 29% -> 50%
where the time goes in v3:
time: 896 us; the launch traced here: 887 us
  Pallas kernels  486 us (54%)
  waiting for transfers between devices  236 us (26%)
  local copies, waits for them, and re-layouts  62.8 us (7%)
  starting transfers between devices  58.9 us (7%)
  matrix products  16 us (2%)
  between operations  15.2 us (2%)
  other arithmetic  11.8 us (1%)
    ppermute x19, waiting for transfers between devices, ring_shift(): lax.ppermute(block, 'tensor', [(i, (i + 1) % size) for i in range(size)])  182 us
    pallas_call x3, Pallas kernels, close_mix(): pl.pallas_call(functools.partial(close_kernel, streams, uses, width, inne...  61.2 us
    unnamed x221, local copies, waits for them, and re-layouts  59.3 us
    pallas_call x8, Pallas kernels, own_product(): pl.pallas_call(functools.partial(own_kernel, len(left)), grid_spec=pltpu....  58.2 us
    pallas_call x4, Pallas kernels, assemble(): pl.pallas_call(functools.partial(assemble_kernel, count, pieces, len(toke...  52 us
    pallas_call x2, Pallas kernels, backward_units(): pl.pallas_call(functools.partial(backward_units_kernel, len(filled) + len...  46.7 us
    pallas_call x2, Pallas kernels, forward_units(): pl.pallas_call(functools.partial(forward_units_kernel, count, len(filled)...  44.4 us
    pallas_call x5, Pallas kernels, away_product(): pl.pallas_call(functools.partial(away_kernel, len(left)), grid_spec=pltpu...  35.9 us
  transfers between devices with their start and end apart: 65, of which 27 were waited for; matrix products, arithmetic and copies ran while one was open for 5% of the time, Pallas kernels for 50%

profile of v3, /device:TPU:0, one launch (start us, length us, event | category | flops | bytes accessed | tf_op | source)
XLA Modules:
  0.0 886.8 jit_solution(755832332192829541)
XLA Ops:
  16.4 8.6 copy.63
  25.4 12.9 %open_attention.1 = (bf16[256,2048]{1,0:T(8,128)(2,1)S(1)}, f32[256,128]{1,0:T(8,128)S(1)}) custom-call(bf16[256,8192]{1,0:T(8,128)(2,1)} %bitcast.72, f32[8,2048]{1,0:T(8,128)S(1)} %pad.14.w_ref.refs_6_, f32[8,128]{1,0:T(8,128)S(1)} %select_maximum_fusion.1.param_ref.refs_7_), custom_call_target="tpu_custom_call" | custom-call | tf_op jit(solution)/shard_map/open_attention/pallas_call | solution.py:527
  45.9 24.7 %collective-permute-done.refs_1_ = bf16[256,2048]{1,0:T(8,128)(2,1)S(1)} collective-permute-done((bf16[256,2048]{1,0:T(8,128)(2,1)S(1)}, bf16[256,2048]{1,0:T(8,128)(2,1)S(1)}, u32[]{:S(2)}, u32[]{:S(2)}) %collective-permute-start) | collective-permute-done | bytes 1048608 | tf_op jit(solution)/shard_map/ppermute | solution.py:1264
  74.2 21.4 %collective-permute-done.1.refs_2_ = bf16[256,2048]{1,0:T(8,128)(2,1)S(1)} collective-permute-done((bf16[256,2048]{1,0:T(8,128)(2,1)S(1)}, bf16[256,2048]{1,0:T(8,128)(2,1)S(1)}, u32[]{:S(2)}, u32[]{:S(2)}) %collective-permute-start.1) | collective-permute-done | bytes 1048608 | tf_op jit(solution)/shard_map/ppermute | solution.py:1264
  107.7 12.2 %collective-permute-done.2.refs_3_ = bf16[256,2048]{1,0:T(8,128)(2,1)} collective-permute-done((bf16[256,2048]{1,0:T(8,128)(2,1)S(1)}, bf16[256,2048]{1,0:T(8,128)(2,1)}, u32[]{:S(2)}, u32[]{:S(2)}) %collective-permute-start.2) | collective-permute-done | bytes 1048608 | tf_op jit(solution)/shard_map/ppermute | solution.py:1264
  124.3 14.9 %attend.1 = (bf16[1024,512]{1,0:T(8,128)(2,1)S(1)}, bf16[1024,512]{1,0:T(8,128)(2,1)S(1)}, bf16[1024,512]{1,0:T(8,128)(2,1)}, bf16[1024,512]{1,0:T(8,128)(2,1)}, f32[1024,512]{1,0:T(8,128)}) custom-call(s32[1]{0:T(128)} %bitcast.3.refs_0_, s32[1024,128]{1,0:T(8,128)S(1)} %broadcast_in_dim.37.refs_1_, f32[1024,128]{1,0:T(8,128)S(1)} %copy-done.16, ...), custom_call_target="tpu_custom_call" | custom-call | tf_op jit(solution)/shard_map/attend/pallas_call | solution.py:755
  167.2 21.0 %open_feedforward.1 = (bf16[256,2048]{1,0:T(8,128)(2,1)S(1)}, bf16[256,2048]{1,0:T(8,128)(2,1)S(1)}, f32[256,128]{1,0:T(8,128)S(1)}, f32[256,8192]{1,0:T(8,128)}) custom-call(bf16[256,8192]{1,0:T(8,128)(2,1)} %bitcast.73, f32[256,128]{1,0:T(8,128)S(1)} %get-tuple-element.182.refs_1_.refs_8_, f32[256,2048]{1,0:T(8,128)} %copy-done.15, ...), custom_call_target="tpu_custom_call" | custom-call | tf_op jit(solution)/shard_map/open_feedforward/pallas_call | solution.py:553
  194.3 21.9 %collective-permute-done.9.refs_1_ = bf16[256,2048]{1,0:T(8,128)(2,1)S(1)} collective-permute-done((bf16[256,2048]{1,0:T(8,128)(2,1)S(1)}, bf16[256,2048]{1,0:T(8,128)(2,1)S(1)}, u32[]{:S(2)}, u32[]{:S(2)}) %collective-permute-start.9) | collective-permute-done | bytes 1048608 | tf_op jit(solution)/shard_map/ppermute | solution.py:1264
  219.7 21.9 %collective-permute-done.10.refs_0_ = bf16[256,2048]{1,0:T(8,128)(2,1)S(1)} collective-permute-done((bf16[256,2048]{1,0:T(8,128)(2,1)S(1)}, bf16[256,2048]{1,0:T(8,128)(2,1)S(1)}, u32[]{:S(2)}, u32[]{:S(2)}) %collective-permute-start.10) | collective-permute-done | bytes 1048608 | tf_op jit(solution)/shard_map/ppermute | solution.py:1264
  242.2 22.1 %all-gather.9.cloned.1.call-done.refs_2_.refs_3_.refs_5_.refs_6_ = bf16[2048,4096]{1,0:T(8,128)(2,1)} async-done(((bf16[256,4096]{1,0:T(8,128)(2,1)}), bf16[2048,4096]{1,0:T(8,128)(2,1)}) %all-gather.9.cloned.1.call-update) | async-done | bytes 16777232 | tf_op jit(solution)/shard_map/all_gather | solution.py:1423
  265.6 22.2 %forward_units.2 = (f32[512,2048]{1,0:T(8,128)}, f32[512,2048]{1,0:T(8,128)}, f32[512,2048]{1,0:T(8,128)}, bf16[1024,2048]{1,0:T(8,128)(2,1)}, bf16[1024,2048]{1,0:T(8,128)(2,1)}, /*index=5*/f32[8,128]{1,0:T(8,128)S(1)}) custom-call(bf16[256,2048]{1,0:T(8,128)(2,1)S(1)} %get-tuple-element.190.refs_0_, bf16[256,2048]{1,0:T(8,128)(2,1)S(1)} %copy-done.41, ...), custom_call_target="tpu_custom_call" | custom-call | tf_op jit(solution)/shard_map/forward_units/pallas_call | solution.py:850
  293.7 22.3 %forward_units.3 = (f32[512,2048]{1,0:T(8,128)}, f32[512,2048]{1,0:T(8,128)}, f32[512,2048]{1,0:T(8,128)}, bf16[1024,2048]{1,0:T(8,128)(2,1)}, bf16[1024,2048]{1,0:T(8,128)(2,1)}, /*index=5*/f32[8,128]{1,0:T(8,128)S(1)}) custom-call(bf16[256,2048]{1,0:T(8,128)(2,1)S(1)} %copy-done.39, ...), custom_call_target="tpu_custom_call", output_to_operand_aliasing={{3}: (5, {}), {4}: (6, {})} | custom-call | tf_op jit(solution)/shard_map/forward_units/pallas_call | solution.py:850
  320.3 23.3 %backward_units.2 = (f32[512,2048]{1,0:T(8,128)}, bf16[1024,2048]{1,0:T(8,128)(2,1)}, bf16[1024,2048]{1,0:T(8,128)(2,1)}, bf16[1024,2048]{1,0:T(8,128)(2,1)}, f32[8,128]{1,0:T(8,128)S(1)}) custom-call(bf16[256,2048]{1,0:T(8,128)(2,1)S(1)} %copy-done.25, bf16[256,2048]{1,0:T(8,128)(2,1)S(1)} %copy-done.29, f32[512,2048]{1,0:T(8,128)} %get-tuple-element.197.refs_2_, ...), custom_call_target="tpu_custom_call" | custom-call | tf_op jit(solution)/shard_map/backward_units/pallas_call | solution.py:889
  346.6 25.3 %collective-permute-done.14.refs_2_.refs_1_ = bf16[256,2048]{1,0:T(8,128)(2,1)S(1)} collective-permute-done((bf16[256,2048]{1,0:T(8,128)(2,1)}, bf16[256,2048]{1,0:T(8,128)(2,1)S(1)}, u32[]{:S(2)}, u32[]{:S(2)}) %collective-permute-start.14) | collective-permute-done | bytes 1048608 | tf_op jit(solution)/shard_map/ppermute | solution.py:1264
  376.4 23.4 %backward_units.3 = (f32[512,2048]{1,0:T(8,128)}, bf16[1024,2048]{1,0:T(8,128)(2,1)}, bf16[1024,2048]{1,0:T(8,128)(2,1)}, bf16[1024,2048]{1,0:T(8,128)(2,1)}, f32[8,128]{1,0:T(8,128)}) custom-call(bf16[256,2048]{1,0:T(8,128)(2,1)S(1)} %copy-done.23, ...), custom_call_target="tpu_custom_call", output_to_operand_aliasing={{1}: (7, {}), {2}: (8, {}), {3}: (9, {})} | custom-call | tf_op jit(solution)/shard_map/backward_units/pallas_call | solution.py:889
  399.8 8.3 away_product.5
  408.1 8.3 away_product.6
  416.4 7.9 collective-permute-done.15.refs_2_.refs_3_
  430.6 8.3 away_product.7
  438.9 11.3 %own_product.8 = (bf16[512,2048]{1,0:T(8,128)(2,1)}, f32[512,2048]{1,0:T(8,128)}, f32[8,128]{1,0:T(8,128)S(1)}) custom-call(s32[2]{0:T(128)S(1)} %pad_add_fusion.1.scalars_ref, bf16[1024,2048]{1,0:T(8,128)(2,1)} %get-tuple-element.210.refs_0_, bf16[1024,2048]{1,0:T(8,128)(2,1)} %get-tuple-element.211.refs_1_, ...), custom_call_target="tpu_custom_call" | custom-call | tf_op jit(solution)/shard_map/own_product/pallas_call | solution.py:1033
  450.2 10.7 %own_product.9 = (bf16[512,2048]{1,0:T(8,128)(2,1)S(1)}, f32[512,2048]{1,0:T(8,128)}, f32[8,128]{1,0:T(8,128)S(1)}) custom-call(s32[2]{0:T(128)S(1)} %pad_add_fusion.2.scalars_ref, bf16[1024,2048]{1,0:T(8,128)(2,1)} %get-tuple-element.210.refs_0_, bf16[1024,2048]{1,0:T(8,128)(2,1)} %get-tuple-element.213.refs_1_, ...), custom_call_target="tpu_custom_call" | custom-call | tf_op jit(solution)/shard_map/own_product/pallas_call | solution.py:1033
  462.2 17.7 %collective-permute-done.16.refs_2_.refs_3_ = bf16[512,2048]{1,0:T(8,128)(2,1)S(1)} collective-permute-done((bf16[512,2048]{1,0:T(8,128)(2,1)}, bf16[512,2048]{1,0:T(8,128)(2,1)S(1)}, u32[]{:S(2)}, u32[]{:S(2)}) %collective-permute-start.16) | collective-permute-done | bytes 2097184 | tf_op jit(solution)/shard_map/ppermute | solution.py:1264
  491.4 7.8 own_product.10
  512.7 16.5 %close_feedforward.2 = (f32[256,8192]{1,0:T(8,128)}, f32[256,128]{1,0:T(8,128)S(1)}, bf16[256,2048]{1,0:T(8,128)(2,1)S(1)}, f32[16,2048]{1,0:T(8,128)S(1)}, f32[8,128]{1,0:T(8,128)S(1)}) custom-call(f32[256,8192]{1,0:T(8,128)} %get-tuple-element.188.refs_0_.h_ref, f32[256,128]{1,0:T(8,128)S(1)} %get-tuple-element.189.refs_1_.saved_ref, ...), custom_call_target="tpu_custom_call" | custom-call | flops 30000001024 | tf_op jit(solution)/shard_map/close_feedforward/pallas_call | solution.py:626
  534.0 16.5 %close_feedforward.3 = (f32[256,8192]{1,0:T(8,128)}, f32[256,128]{1,0:T(8,128)S(1)}, bf16[256,2048]{1,0:T(8,128)(2,1)S(1)}, f32[16,2048]{1,0:T(8,128)S(1)}, f32[8,128]{1,0:T(8,128)S(1)}) custom-call(f32[256,8192]{1,0:T(8,128)} %get-tuple-element.188.refs_0_.h_ref, ...), custom_call_target="tpu_custom_call", output_to_operand_aliasing={{0}: (12, {}), {1}: (13, {}), {2}: (14, {})} | custom-call | flops 30000001024 | tf_op jit(solution)/shard_map/close_feedforward/pallas_call | solution.py:626
  595.2 14.4 %collective-permute-done.27.refs_0_ = bf16[256,2048]{1,0:T(8,128)(2,1)S(1)} collective-permute-done((bf16[256,2048]{1,0:T(8,128)(2,1)}, bf16[256,2048]{1,0:T(8,128)(2,1)S(1)}, u32[]{:S(2)}, u32[]{:S(2)}) %collective-permute-start.27) | collective-permute-done | bytes 1048608 | tf_op jit(solution)/shard_map/ppermute | solution.py:1264
  638.8 17.2 %attend_back.1.d_ref.refs_4_ = bf16[1024,1536]{1,0:T(8,128)(2,1)} custom-call(s32[1]{0:T(128)} %bitcast.3.refs_0_, s32[1024,128]{1,0:T(8,128)S(1)} %copy-done.21, f32[1024,128]{1,0:T(8,128)S(1)} %copy-done.17, f32[1024,128]{1,0:T(8,128)S(1)} %copy-done.19, bf16[1024,512]{1,0:T(8,128)(2,1)S(1)} %copy-done.36, bf16[1024,512]{1,0:T(8,128)(2,1)} %copy-done.37, ...), custom_call_target="tpu_custom_call" | custom-call | tf_op jit(solution)/shard_map/attend_back/pallas_call | solution.py:775
  744.3 11.5 %assemble.4 = (f32[2048,2048]{1,0:T(8,128)}, f32[8,128]{1,0:T(8,128)S(1)}) custom-call(s32[8]{0:T(128)S(1)} %stack.172.table_ref, bf16[2048,2048]{1,0:T(8,128)(2,1)} %hold.19.refs_0_, bf16[2048,2048]{1,0:T(8,128)(2,1)} %collective-permute-done.44.refs_1_, f32[8,128]{1,0:T(8,128)S(1)} %get-tuple-element.303.refs_2_), custom_call_target="tpu_custom_call" | custom-call | tf_op jit(solution)/shard_map/assemble/pallas_call | solution.py:938
  770.0 28.2 %close_attention.1 = (bf16[256,4,2048]{2,1,0:T(4,128)(2,1)}, f32[16,2048]{1,0:T(8,128)S(1)}, f32[8,128]{1,0:T(8,128)S(1)}) custom-call(bf16[256,8192]{1,0:T(8,128)(2,1)} %bitcast.74, f32[256,128]{1,0:T(8,128)S(1)} %get-tuple-element.182.refs_1_.refs_8_, f32[256,8192]{1,0:T(8,128)} %get-tuple-element.238.refs_2_, ...), custom_call_target="tpu_custom_call" | custom-call | tf_op jit(solution)/shard_map/close_attention/pallas_call | solution.py:626
  806.1 11.5 %assemble.5 = (f32[2048,2048]{1,0:T(8,128)}, f32[8,128]{1,0:T(8,128)S(1)}) custom-call(s32[8]{0:T(128)S(1)} %stack.198.table_ref, bf16[2048,2048]{1,0:T(8,128)(2,1)} %hold.19.refs_0_, bf16[2048,2048]{1,0:T(8,128)(2,1)} %collective-permute-done.44.refs_1_, f32[208,128]{1,0:T(8,128)S(1)} %pad_maximum_fusion.6.refs_2_.refs_0_, ...), custom_call_target="tpu_custom_call" | custom-call | tf_op jit(solution)/shard_map/assemble/pallas_call | solution.py:938
  833.1 14.4 %assemble.6 = (f32[2048,2048]{1,0:T(8,128)}, f32[8,128]{1,0:T(8,128)S(1)}) custom-call(s32[16]{0:T(128)S(1)} %stack.189.table_ref, bf16[1024,2048]{1,0:T(8,128)(2,1)} %get-tuple-element.335.refs_0_, bf16[1024,2048]{1,0:T(8,128)(2,1)} %collective-permute-done.57.refs_1_, f32[8,128]{1,0:T(8,128)S(1)} %get-tuple-element.336.refs_2_), custom_call_target="tpu_custom_call" | custom-call | tf_op jit(solution)/shard_map/assemble/pallas_call | solution.py:938
  865.4 14.6 %assemble.7 = (f32[2048,512]{1,0:T(8,128)}, f32[2048,512]{1,0:T(8,128)}, f32[2048,512]{1,0:T(8,128)}, f32[2048,512]{1,0:T(8,128)}, f32[8,128]{1,0:T(8,128)}) custom-call(s32[16]{0:T(128)S(1)} %stack.189.table_ref, bf16[1024,2048]{1,0:T(8,128)(2,1)} %get-tuple-element.339.refs_0_, bf16[1024,2048]{1,0:T(8,128)(2,1)} %collective-permute-done.58.refs_1_, ...), custom_call_target="tpu_custom_call" | custom-call | tf_op jit(solution)/shard_map/assemble/pallas_call | solution.py:938
  (463 shorter events, 348.3 us)
Async XLA Ops:
  7.2 88.7 %all-gather.5.cloned.1.call-start = ((), (), s32[]{:S(2)}) async-start(), calls=%async_computation | async-start | bytes 7077888 | tf_op jit(solution)/shard_map/all_gather | solution.py:1423
  9.3 150.7 %all-gather.7.cloned.1.call-start = ((), (), s32[]{:S(2)}) async-start(), calls=%async_computation.1 | async-start | bytes 9437184 | tf_op jit(solution)/shard_map/all_gather | solution.py:1423
  9.3 29.9 %collective-permute-start.6 = (bf16[256,512]{1,0:T(8,128)(2,1)}, bf16[256,512]{1,0:T(8,128)(2,1)S(1)}, u32[]{:S(2)}, u32[]{:S(2)}) collective-permute-start(bf16[256,512]{1,0:T(8,128)(2,1)} %param.21), channel_id=1, source_target_pairs={{0,1},{1,2},{2,3},{3,0},{4,5},{5,6},{6,7},{7,4},{8,9},{9,10},{10,1... | collective-permute-start | bytes 786440 | tf_op jit(solution)/shard_map/ppermute | solution.py:1468
  12.4 26.9 %collective-permute-start.7 = (bf16[256,512]{1,0:T(8,128)(2,1)}, bf16[256,512]{1,0:T(8,128)(2,1)S(1)}, u32[]{:S(2)}, u32[]{:S(2)}) collective-permute-start(bf16[256,512]{1,0:T(8,128)(2,1)} %param.21), channel_id=1, source_target_pairs={{0,2},{1,3},{2,0},{3,1},{4,6},{5,7},{6,4},{7,5},{8,10},{9,11},{10,... | collective-permute-start | bytes 786440 | tf_op jit(solution)/shard_map/ppermute | solution.py:1468
  42.5 199.8 %all-gather.11.cloned.1.call-start = ((), (), s32[]{:S(2)}) async-start(), calls=%async_computation.3 | async-start | bytes 9437184 | tf_op jit(solution)/shard_map/all_gather | solution.py:1423
  43.2 221.2 %all-gather.9.cloned.1.call-start = ((), (), s32[]{:S(2)}) async-start(), calls=%async_computation.2 | async-start | bytes 18874368 | tf_op jit(solution)/shard_map/all_gather | solution.py:1423
  189.2 27.1 %collective-permute-start.9 = (bf16[256,2048]{1,0:T(8,128)(2,1)S(1)}, bf16[256,2048]{1,0:T(8,128)(2,1)S(1)}, u32[]{:S(2)}, u32[]{:S(2)}) collective-permute-start(bf16[256,2048]{1,0:T(8,128)(2,1)S(1)} %get-tuple-element.190.refs_0_), channel_id=1, source_target_pairs={{0,1},{1,2},{2,3},{3,0},{4,5},{5,6},{6,7},{7,4},{8,9},{9,10},{10,1... | collective-permute-start | bytes 3145736 | tf_op jit(solution)/shard_map/ppermute | solution.py:1264
  241.6 46.8 %collective-permute-start.11 = (bf16[256,2048]{1,0:T(8,128)(2,1)S(1)}, bf16[256,2048]{1,0:T(8,128)(2,1)S(1)}, u32[]{:S(2)}, u32[]{:S(2)}) collective-permute-start(bf16[256,2048]{1,0:T(8,128)(2,1)S(1)} %collective-permute-done.10.refs_0_), channel_id=1, source_target_pairs={{0,1},{1,2},{2,3},{3,0},{4,5},{5,6},{6,7},{7,4},{8,9},{9,10},{10,1... | collective-permute-start | bytes 3145736 | tf_op jit(solution)/shard_map/ppermute | solution.py:1264
  289.3 27.8 %collective-permute-start.12 = (bf16[256,2048]{1,0:T(8,128)(2,1)}, bf16[256,2048]{1,0:T(8,128)(2,1)S(1)}, u32[]{:S(2)}, u32[]{:S(2)}) collective-permute-start(bf16[256,2048]{1,0:T(8,128)(2,1)} %hold.11.refs_0_), channel_id=1, source_target_pairs={{0,1},{1,2},{2,3},{3,0},{4,5},{5,6},{6,7},{7,4},{8,9},{9,10},{10,1... | collective-permute-start | bytes 3145736 | tf_op jit(solution)/shard_map/ppermute | solution.py:1264
  376.2 48.2 %collective-permute-start.15 = (bf16[512,2048]{1,0:T(8,128)(2,1)}, bf16[512,2048]{1,0:T(8,128)(2,1)}, u32[]{:S(2)}, u32[]{:S(2)}) collective-permute-start(bf16[512,2048]{1,0:T(8,128)(2,1)} %get-tuple-element.209), channel_id=1, source_target_pairs={{0,1},{1,2},{2,3},{3,0},{4,5},{5,6},{6,7},{7,4},{8,9},{9,10},{10,1... | collective-permute-start | bytes 6291464 | tf_op jit(solution)/shard_map/ppermute | solution.py:1264
  430.4 49.5 %collective-permute-start.16 = (bf16[512,2048]{1,0:T(8,128)(2,1)}, bf16[512,2048]{1,0:T(8,128)(2,1)S(1)}, u32[]{:S(2)}, u32[]{:S(2)}) collective-permute-start(bf16[512,2048]{1,0:T(8,128)(2,1)} %copy-done.88), channel_id=1, source_target_pairs={{0,1},{1,2},{2,3},{3,0},{4,5},{5,6},{6,7},{7,4},{8,9},{9,10},{10,1... | collective-permute-start | bytes 6291464 | tf_op jit(solution)/shard_map/ppermute | solution.py:1264
  484.0 28.0 %collective-permute-start.20 = (bf16[256,2048]{1,0:T(8,128)(2,1)}, bf16[256,2048]{1,0:T(8,128)(2,1)S(1)}, u32[]{:S(2)}, u32[]{:S(2)}) collective-permute-start(bf16[256,2048]{1,0:T(8,128)(2,1)} %copy-done.90), channel_id=1, source_target_pairs={{0,1},{1,2},{2,3},{3,0},{4,5},{5,6},{6,7},{7,4},{8,9},{9,10},{10,1... | collective-permute-start | bytes 3145736 | tf_op jit(solution)/shard_map/ppermute | solution.py:1264
  487.9 46.1 %collective-permute-start.19 = (bf16[256,2048]{1,0:T(8,128)(2,1)}, bf16[256,2048]{1,0:T(8,128)(2,1)S(1)}, u32[]{:S(2)}, u32[]{:S(2)}) collective-permute-start(bf16[256,2048]{1,0:T(8,128)(2,1)} %get-tuple-element.226), channel_id=1, source_target_pairs={{0,1},{1,2},{2,3},{3,0},{4,5},{5,6},{6,7},{7,4},{8,9},{9,10},{10,1... | collective-permute-start | bytes 3145736 | tf_op jit(solution)/shard_map/ppermute | solution.py:1264
  488.1 62.5 %collective-permute-start.23 = (bf16[512,2048]{1,0:T(8,128)(2,1)}, bf16[512,2048]{1,0:T(8,128)(2,1)}, u32[]{:S(2)}, u32[]{:S(2)}) collective-permute-start(bf16[512,2048]{1,0:T(8,128)(2,1)} %get-tuple-element.244), channel_id=1, source_target_pairs={{0,8},{4,12},{8,0},{12,4},{16,24},{20,28},{24,16},{28,20},{1,9},{5... | collective-permute-start | bytes 6291464 | tf_op jit(solution)/shard_map/ppermute | solution.py:1297
  489.6 67.2 %collective-permute-start.24 = (bf16[512,2048]{1,0:T(8,128)(2,1)S(1)}, bf16[512,2048]{1,0:T(8,128)(2,1)}, u32[]{:S(2)}, u32[]{:S(2)}) collective-permute-start(bf16[512,2048]{1,0:T(8,128)(2,1)S(1)} %copy-done.87), channel_id=1, source_target_pairs={{0,16},{4,20},{8,24},{12,28},{16,0},{20,4},{24,8},{28,12},{1,17},{... | collective-permute-start | bytes 6291464 | tf_op jit(solution)/shard_map/ppermute | solution.py:1297
  500.6 74.7 %collective-permute-start.25 = (bf16[256,2048]{1,0:T(8,128)(2,1)}, bf16[256,2048]{1,0:T(8,128)(2,1)S(1)}, u32[]{:S(2)}, u32[]{:S(2)}) collective-permute-start(bf16[256,2048]{1,0:T(8,128)(2,1)} %get-tuple-element.250), channel_id=1, source_target_pairs={{0,8},{4,12},{8,0},{12,4},{16,24},{20,28},{24,16},{28,20},{1,9},{5... | collective-permute-start | bytes 3145736 | tf_op jit(solution)/shard_map/ppermute | solution.py:1297
  512.0 65.7 %collective-permute-start.26 = (bf16[256,2048]{1,0:T(8,128)(2,1)S(1)}, bf16[256,2048]{1,0:T(8,128)(2,1)S(1)}, u32[]{:S(2)}, u32[]{:S(2)}) collective-permute-start(bf16[256,2048]{1,0:T(8,128)(2,1)S(1)} %get-tuple-element.253), channel_id=1, source_target_pairs={{0,16},{4,20},{8,24},{12,28},{16,0},{20,4},{24,8},{28,12},{1,17},{... | collective-permute-start | bytes 3145736 | tf_op jit(solution)/shard_map/ppermute | solution.py:1297
  550.5 31.9 %collective-permute-start.22 = (bf16[256,2048]{1,0:T(8,128)(2,1)S(1)}, bf16[256,2048]{1,0:T(8,128)(2,1)S(1)}, u32[]{:S(2)}, u32[]{:S(2)}) collective-permute-start(bf16[256,2048]{1,0:T(8,128)(2,1)S(1)} %get-tuple-element.235.refs_0_.refs_1_), channel_id=1, source_target_pairs={{0,1},{1,2},{2,3},{3,0},{4,5},{5,6},{6,7},{7,4},{8,9},{9,10},{10,1... | collective-permute-start | bytes 3145736 | tf_op jit(solution)/shard_map/ppermute | solution.py:1264
  556.1 27.3 %collective-permute-start.28 = (bf16[256,2048]{1,0:T(8,128)(2,1)}, bf16[256,2048]{1,0:T(8,128)(2,1)S(1)}, u32[]{:S(2)}, u32[]{:S(2)}) collective-permute-start(bf16[256,2048]{1,0:T(8,128)(2,1)} %get-tuple-element.257), channel_id=1, source_target_pairs={{0,16},{4,20},{8,24},{12,28},{16,0},{20,4},{24,8},{28,12},{1,17},{... | collective-permute-start | bytes 3145736 | tf_op jit(solution)/shard_map/ppermute | solution.py:1297
  561.8 29.1 %collective-permute-start.29 = (bf16[256,2048]{1,0:T(8,128)(2,1)}, bf16[256,2048]{1,0:T(8,128)(2,1)}, u32[]{:S(2)}, u32[]{:S(2)}) collective-permute-start(bf16[256,2048]{1,0:T(8,128)(2,1)} %get-tuple-element.260), channel_id=1, source_target_pairs={{0,8},{4,12},{8,0},{12,4},{16,24},{20,28},{24,16},{28,20},{1,9},{5... | collective-permute-start | bytes 3145736 | tf_op jit(solution)/shard_map/ppermute | solution.py:1297
  617.5 64.2 %collective-permute-start.34 = (bf16[512,2048]{1,0:T(8,128)(2,1)}, bf16[512,2048]{1,0:T(8,128)(2,1)}, u32[]{:S(2)}, u32[]{:S(2)}) collective-permute-start(bf16[512,2048]{1,0:T(8,128)(2,1)} %get-tuple-element.271.refs_0_), channel_id=1, source_target_pairs={{0,8},{4,12},{8,0},{12,4},{16,24},{20,28},{24,16},{28,20},{1,9},{5... | collective-permute-start | bytes 6291464 | tf_op jit(solution)/shard_map/ppermute | solution.py:1297
  622.0 59.7 %collective-permute-start.35 = (bf16[512,2048]{1,0:T(8,128)(2,1)}, bf16[512,2048]{1,0:T(8,128)(2,1)}, u32[]{:S(2)}, u32[]{:S(2)}) collective-permute-start(bf16[512,2048]{1,0:T(8,128)(2,1)} %get-tuple-element.272.refs_2_), channel_id=1, source_target_pairs={{0,16},{4,20},{8,24},{12,28},{16,0},{20,4},{24,8},{28,12},{1,17},{... | collective-permute-start | bytes 6291464 | tf_op jit(solution)/shard_map/ppermute | solution.py:1297
  661.2 27.1 %collective-permute-start.33 = (bf16[256,2048]{1,0:T(8,128)(2,1)S(1)}, bf16[256,2048]{1,0:T(8,128)(2,1)S(1)}, u32[]{:S(2)}, u32[]{:S(2)}) collective-permute-start(bf16[256,2048]{1,0:T(8,128)(2,1)S(1)} %get-tuple-element.270), channel_id=1, source_target_pairs={{0,1},{1,2},{2,3},{3,0},{4,5},{5,6},{6,7},{7,4},{8,9},{9,10},{10,1... | collective-permute-start | bytes 3145736 | tf_op jit(solution)/shard_map/ppermute | solution.py:1264
  692.4 34.1 %collective-permute-start.38 = (bf16[256,2048]{1,0:T(8,128)(2,1)}, bf16[256,2048]{1,0:T(8,128)(2,1)S(1)}, u32[]{:S(2)}, u32[]{:S(2)}) collective-permute-start(bf16[256,2048]{1,0:T(8,128)(2,1)} %copy-done.89), channel_id=1, source_target_pairs={{0,1},{1,2},{2,3},{3,0},{4,5},{5,6},{6,7},{7,4},{8,9},{9,10},{10,1... | collective-permute-start | bytes 3145736 | tf_op jit(solution)/shard_map/ppermute | solution.py:1264
  692.5 31.9 %collective-permute-start.40 = (bf16[128,2048]{1,0:T(8,128)(2,1)}, bf16[128,2048]{1,0:T(8,128)(2,1)S(1)}, u32[]{:S(2)}, u32[]{:S(2)}) collective-permute-start(bf16[128,2048]{1,0:T(8,128)(2,1)} %copy-done.56), channel_id=1, source_target_pairs={{0,16},{4,20},{8,24},{12,28},{16,0},{20,4},{24,8},{28,12},{1,17},{... | collective-permute-start | bytes 1572872 | tf_op jit(solution)/shard_map/ppermute | solution.py:1297
  693.3 32.1 %collective-permute-start.41 = (bf16[128,2048]{1,0:T(8,128)(2,1)}, bf16[128,2048]{1,0:T(8,128)(2,1)S(1)}, u32[]{:S(2)}, u32[]{:S(2)}) collective-permute-start(bf16[128,2048]{1,0:T(8,128)(2,1)} %copy-done.58), channel_id=1, source_target_pairs={{0,8},{4,12},{8,0},{12,4},{16,24},{20,28},{24,16},{28,20},{1,9},{5... | collective-permute-start | bytes 1572872 | tf_op jit(solution)/shard_map/ppermute | solution.py:1297
  731.5 30.4 %collective-permute-start.45 = (bf16[256,2048]{1,0:T(8,128)(2,1)}, bf16[256,2048]{1,0:T(8,128)(2,1)}, u32[]{:S(2)}, u32[]{:S(2)}) collective-permute-start(bf16[256,2048]{1,0:T(8,128)(2,1)} %get-tuple-element.307), channel_id=1, source_target_pairs={{0,16},{4,20},{8,24},{12,28},{16,0},{20,4},{24,8},{28,12},{1,17},{... | collective-permute-start | bytes 3145736 | tf_op jit(solution)/shard_map/ppermute | solution.py:1297
  732.8 37.1 %collective-permute-start.42 = (bf16[256,2048]{1,0:T(8,128)(2,1)}, bf16[256,2048]{1,0:T(8,128)(2,1)S(1)}, u32[]{:S(2)}, u32[]{:S(2)}) collective-permute-start(bf16[256,2048]{1,0:T(8,128)(2,1)} %get-tuple-element.296), channel_id=1, source_target_pairs={{0,1},{1,2},{2,3},{3,0},{4,5},{5,6},{6,7},{7,4},{8,9},{9,10},{10,1... | collective-permute-start | bytes 3145736 | tf_op jit(solution)/shard_map/ppermute | solution.py:1264
  760.5 37.7 %collective-permute-start.46 = (bf16[128,2048]{1,0:T(8,128)(2,1)}, bf16[128,2048]{1,0:T(8,128)(2,1)}, u32[]{:S(2)}, u32[]{:S(2)}) collective-permute-start(bf16[128,2048]{1,0:T(8,128)(2,1)} %get-tuple-element.311), channel_id=1, source_target_pairs={{0,16},{4,20},{8,24},{12,28},{16,0},{20,4},{24,8},{28,12},{1,17},{... | collective-permute-start | bytes 1572872 | tf_op jit(solution)/shard_map/ppermute | solution.py:1297
  765.8 36.0 %collective-permute-start.49 = (bf16[128,2048]{1,0:T(8,128)(2,1)}, bf16[128,2048]{1,0:T(8,128)(2,1)}, u32[]{:S(2)}, u32[]{:S(2)}) collective-permute-start(bf16[128,2048]{1,0:T(8,128)(2,1)} %get-tuple-element.321), channel_id=1, source_target_pairs={{0,8},{4,12},{8,0},{12,4},{16,24},{20,28},{24,16},{28,20},{1,9},{5... | collective-permute-start | bytes 1572872 | tf_op jit(solution)/shard_map/ppermute | solution.py:1297
  766.3 51.6 %collective-permute-start.54 = (bf16[256,2048]{1,0:T(8,128)(2,1)}, bf16[256,2048]{1,0:T(8,128)(2,1)}, u32[]{:S(2)}, u32[]{:S(2)}) collective-permute-start(bf16[256,2048]{1,0:T(8,128)(2,1)} %get-tuple-element.329.refs_0_), channel_id=1, source_target_pairs={{0,8},{4,12},{8,0},{12,4},{16,24},{20,28},{24,16},{28,20},{1,9},{5... | collective-permute-start | bytes 3145736 | tf_op jit(solution)/shard_map/ppermute | solution.py:1297
  767.9 50.0 %collective-permute-start.55 = (bf16[256,2048]{1,0:T(8,128)(2,1)}, bf16[256,2048]{1,0:T(8,128)(2,1)}, u32[]{:S(2)}, u32[]{:S(2)}) collective-permute-start(bf16[256,2048]{1,0:T(8,128)(2,1)} %get-tuple-element.330.refs_2_), channel_id=1, source_target_pairs={{0,16},{4,20},{8,24},{12,28},{16,0},{20,4},{24,8},{28,12},{1,17},{... | collective-permute-start | bytes 3145736 | tf_op jit(solution)/shard_map/ppermute | solution.py:1297
  (141 other events, 1352.9 us)
Sparse Core Ops, SparseCore 0:
  10.5 48.2 all-gather.4
  61.2 54.3 all-gather.6
  117.5 54.4 all-gather.10
  174.3 90.0 all-gather.8

commit v4 on v3

--- a/solution.py
+++ b/solution.py
@@ -793,25 +793,18 @@
 
 
 def forward_units_kernel(blocks, kept, *refs):
-    gate_w_ref, up_w_ref, down_w_ref = refs[blocks : blocks + 3]
-    gate_ref, up_ref, partial_ref, rows_ref, hidden_ref, mark_ref = refs[blocks + 3 + kept :]
+    gate_w_ref, up_w_ref = refs[blocks : blocks + 2]
+    gate_ref, up_ref, rows_ref, hidden_ref, mark_ref = refs[blocks + 2 + kept :]
     mark_ref[...] = jnp.zeros_like(mark_ref)
     x = jnp.concatenate([ref[...] for ref in refs[:blocks]], axis=0)
     gate, up = matmul(x, gate_w_ref[...]), matmul(x, up_w_ref[...])
     gate_ref[...] = gate
     up_ref[...] = up
-    hidden = (gate / (1.0 + jnp.exp(-gate)) * up).astype(jnp.bfloat16)
-    hidden_ref[...] = hidden
-    part = times_transposed(hidden, down_w_ref[...])
+    hidden_ref[...] = (gate / (1.0 + jnp.exp(-gate)) * up).astype(jnp.bfloat16)
 
     @pl.when(pl.program_id(0) == 0)
     def _():
-        partial_ref[...] = part
         rows_ref[...] = x
-
-    @pl.when(pl.program_id(0) > 0)
-    def _():
-        partial_ref[...] += part
 
 
 def backward_units_kernel(kept, *refs):
@@ -838,12 +831,12 @@
         partial_ref[...] += part
 
 
-def forward_units(pair, size, blocks, gate_up, down, filled, tokens=()):
+def forward_units(pair, size, blocks, gate_up, filled, tokens=()):
     tokens = waits(tokens)
     each, width = blocks[0].shape
     count = len(blocks)
     rows = each * count // 2
-    units = down.shape[1]
+    units = gate_up.shape[1] // 2
     tile = min(UNIT_TILE, units)
     tiles = units // tile
     weight = functools.partial(pl.BlockSpec, (width, tile))
@@ -851,12 +844,11 @@
         functools.partial(forward_units_kernel, count, len(filled) + len(tokens)),
         grid=(tiles,),
         in_specs=[pl.BlockSpec((each, width), lambda i: (0, 0))] * count
-        + [weight(lambda i: (0, i)), weight(lambda i: (0, tiles + i)), weight(lambda i: (0, i))]
+        + [weight(lambda i: (0, i)), weight(lambda i: (0, tiles + i))]
         + anywhere(len(filled) + len(tokens)),
         out_specs=[
             pl.BlockSpec((2 * rows, tile), lambda i: (0, i)),
             pl.BlockSpec((2 * rows, tile), lambda i: (0, i)),
-            pl.BlockSpec((2 * rows, width), lambda i: (0, 0)),
             pl.BlockSpec((2 * rows, width), lambda i: (pair, 0)),
             pl.BlockSpec((2 * rows, tile), lambda i: (pair, i)),
             MARK_SPEC,
@@ -864,18 +856,17 @@
         out_shape=[
             jax.ShapeDtypeStruct((2 * rows, units), jnp.float32),
             jax.ShapeDtypeStruct((2 * rows, units), jnp.float32),
-            jax.ShapeDtypeStruct((2 * rows, width), jnp.float32),
             jax.ShapeDtypeStruct((size * rows, width), jnp.bfloat16),
             jax.ShapeDtypeStruct((size * rows, units), jnp.bfloat16),
             MARK_SHAPE,
         ],
-        input_output_aliases={count + 3 + k: 3 + k for k in range(len(filled))},
+        input_output_aliases={count + 2 + k: 2 + k for k in range(len(filled))},
         compiler_params=PARAMS,
         cost_estimate=cost(),
         name="forward_units",
-    )(*blocks, gate_up, gate_up, down, *filled, *tokens)
+    )(*blocks, gate_up, gate_up, *filled, *tokens)
     outs = marked(outs[:-1], outs[-1])
-    return outs[0], outs[1], outs[2], outs[3:]
+    return outs[0], outs[1], outs[2:]
 
 
 def backward_units(pair, size, blocks, gate, up, gate_up, down, filled, tokens=()):
@@ -1485,13 +1476,12 @@
     def pair_of(arrays, pair):
         return arrays[2 * pair : 2 * pair + 2]
 
-    blocks, gates, ups, partials_f, filled = [normed_f], [], [], [], []
+    blocks, gates, ups, filled = [normed_f], [], [], []
 
     def forward(pair, filled):
-        gate, up, partial, filled = forward_units(pair, size, pair_of(blocks, pair), gate_up_full, down_full, filled)
+        gate, up, filled = forward_units(pair, size, pair_of(blocks, pair), gate_up_full, filled)
         gates.append(gate)
         ups.append(up)
-        partials_f.append(partial)
         return filled
 
     for step in range(1, size):
@@ -1499,12 +1489,12 @@
         if step % 2 == 0:
             filled = forward(step // 2 - 1, filled)
     last_pair = size // 2 - 1
-    grads, partials_n, filled_back = list(hold([d_out_f], blocks[-1], *partials_f)), [], []
+    grads, partials_n, filled_back = list(hold([d_out_f], blocks[-1], *gates)), [], []
     for step in range(1, size):
         arrived = ring_shift(grads[-1])
         if step == 1:
             filled = forward(last_pair, filled)
-            (arrived,) = hold([arrived], partials_f[-1])
+            (arrived,) = hold([arrived], gates[-1])
         elif step % 2 == 0:
             pair = step // 2 - 1
             partial, filled_back = backward_units(
@@ -1514,10 +1504,11 @@
             (arrived,) = hold([arrived], partial)
         grads.append(arrived)
     feedforward_rows, hidden_rows = filled
+    partials_f = backproject((hidden_rows, local_rows), 0, size, down_full, jnp.float32, partials_n)
 
     def both_parts(index):
         first = (index % 2) * local_rows
-        return [(partials_f[index // 2], first, local_rows), (partials_n[index // 2], first, local_rows)]
+        return [(partials_f, index * local_rows, local_rows), (partials_n[index // 2], first, local_rows)]
 
     half = width // 2
     totals = ring_sums(1, size, both_parts(1), (), [grads[-1]])
@@ -1569,7 +1560,7 @@
     filled, sums_f = [], []
     for k, both in enumerate(arrived):
         first = k * half_rows
-        own_f, own_n = (partials_f[0], first), (partials_n[0], first)
+        own_f, own_n = (partials_f, first), (partials_n[0], first)
         rest = [(a, first) for a in (valid, saved_a, out_a)]
         arrays = [(a, first) for a in (middle, saved_f, cotangents)]
         *filled, weight_sum, small = close_mix(
@@ -1589,7 +1580,7 @@
     def finished(tokens):
         filled = []
         for k, both in enumerate(arrived_last):
-            filled = [finish(k * half_rows, middle, saved_f, (both, 0, half_rows), partials_f[0], *sizes, filled, tokens)]
+            filled = [finish(k * half_rows, middle, saved_f, (both, 0, half_rows), partials_f, *sizes, filled, tokens)]
         return filled[0]
 
     arrived_last = arrived
@@ -1600,10 +1591,10 @@
         after = output_grads[-1]
         tokens = []
         if step == 1:
-            out_streams = finished([after])
-            tokens = [*gate_up_sum.step(after).ready, *down_sum.step(after).ready, out_streams]
+            tokens = [*gate_up_sum.step(after).ready, *down_sum.step(after).ready]
         elif step == 2:
-            tokens = gate_up_sum.step(after).ready
+            out_streams = finished(gate_up_sum.step(after).ready)
+            tokens = [*gate_up_sum.ready, out_streams]
         if tokens:
             (arrived,) = hold([arrived], *tokens)
         output_grads.append(arrived)

time: 896 us -> 860 us (0.960)
  waiting for transfers between devices: 236 us -> 190 us
  Pallas kernels: 486 us -> 496 us
    ppermute x19, waiting for transfers between devices: 182 us -> 152 us  [ring_shift(): lax.ppermute(block, 'tensor', [(i, (i + 1) % size) for i in range(size)])]
    pallas_call x4 -> x5, Pallas kernels: 20.6 us -> 42.7 us  [backproject(): pl.pallas_call(backproject_kernel, grid=(width // across, count), in_spec...]
    all_gather x4, waiting for transfers between devices: 22.1 us -> 0.04 us  [gather_rows(): lax.all_gather(jnp.concatenate(weights, axis=1), 'dp', axis=0, tiled=True)]
    pallas_call x2, Pallas kernels: 44.4 us -> 30.4 us  [forward_units(): pl.pallas_call(functools.partial(forward_units_kernel, count, len(filled)...]
    unnamed x221 -> x227, local copies, waits for them, and re-layouts: 59.3 us -> 60.3 us
  transfers between devices with their start and end apart: 65 -> 65, of which waited for: 27 -> 26; matrix products, arithmetic and copies ran while one was open for 5% -> 5% of each run, Pallas kernels for 50% -> 54%
where the time goes in v4:
time: 860 us; the launch traced here: 850 us
  Pallas kernels  496 us (58%)
  waiting for transfers between devices  190 us (22%)
  local copies, waits for them, and re-layouts  63.8 us (7%)
  starting transfers between devices  56.8 us (7%)
  matrix products  16.1 us (2%)
  between operations  15.2 us (2%)
  other arithmetic  11.8 us (1%)
    ppermute x19, waiting for transfers between devices, ring_shift(): lax.ppermute(block, 'tensor', [(i, (i + 1) % size) for i in range(size)])  152 us
    pallas_call x3, Pallas kernels, close_mix(): pl.pallas_call(functools.partial(close_kernel, streams, uses, width, inne...  61.5 us
    unnamed x227, local copies, waits for them, and re-layouts  60.3 us
    pallas_call x8, Pallas kernels, own_product(): pl.pallas_call(functools.partial(own_kernel, len(left)), grid_spec=pltpu....  57.6 us
    pallas_call x4, Pallas kernels, assemble(): pl.pallas_call(functools.partial(assemble_kernel, count, pieces, len(toke...  52 us
    pallas_call x2, Pallas kernels, backward_units(): pl.pallas_call(functools.partial(backward_units_kernel, len(filled) + len...  46.6 us
    pallas_call x5, Pallas kernels, backproject(): pl.pallas_call(backproject_kernel, grid=(width // across, count), in_spec...  42.7 us
    pallas_call x5, Pallas kernels, away_product(): pl.pallas_call(functools.partial(away_kernel, len(left)), grid_spec=pltpu...  35.9 us
  transfers between devices with their start and end apart: 65, of which 26 were waited for; matrix products, arithmetic and copies ran while one was open for 5% of the time, Pallas kernels for 54%

profile of v4, /device:TPU:0, one launch (start us, length us, event | category | flops | bytes accessed | tf_op | source)
XLA Modules:
  0.0 849.7 jit_solution(17588490467522080457)
XLA Ops:
  16.4 8.6 %copy.63 = bf16[32,8,4,2048]{3,1,2,0:T(8,128)(2,1)} copy(bf16[32,8,4,2048]{3,2,1,0:T(4,128)(2,1)} %bitcast.78) | data formatting | bytes 8388608
  25.4 12.9 %open_attention.1 = (bf16[256,2048]{1,0:T(8,128)(2,1)S(1)}, f32[256,128]{1,0:T(8,128)S(1)}) custom-call(bf16[256,8192]{1,0:T(8,128)(2,1)} %bitcast.72, f32[8,2048]{1,0:T(8,128)S(1)} %pad.14.w_ref.refs_6_, f32[8,128]{1,0:T(8,128)S(1)} %select_maximum_fusion.1.param_ref.refs_7_), custom_call_target="tpu_custom_call" | custom-call | tf_op jit(solution)/shard_map/open_attention/pallas_call | solution.py:527
  45.8 24.7 %collective-permute-done.refs_1_ = bf16[256,2048]{1,0:T(8,128)(2,1)S(1)} collective-permute-done((bf16[256,2048]{1,0:T(8,128)(2,1)S(1)}, bf16[256,2048]{1,0:T(8,128)(2,1)S(1)}, u32[]{:S(2)}, u32[]{:S(2)}) %collective-permute-start) | collective-permute-done | bytes 1048608 | tf_op jit(solution)/shard_map/ppermute | solution.py:1255
  74.0 21.4 %collective-permute-done.1.refs_2_ = bf16[256,2048]{1,0:T(8,128)(2,1)S(1)} collective-permute-done((bf16[256,2048]{1,0:T(8,128)(2,1)S(1)}, bf16[256,2048]{1,0:T(8,128)(2,1)S(1)}, u32[]{:S(2)}, u32[]{:S(2)}) %collective-permute-start.1) | collective-permute-done | bytes 1048608 | tf_op jit(solution)/shard_map/ppermute | solution.py:1255
  107.6 12.1 %collective-permute-done.2.refs_3_ = bf16[256,2048]{1,0:T(8,128)(2,1)} collective-permute-done((bf16[256,2048]{1,0:T(8,128)(2,1)S(1)}, bf16[256,2048]{1,0:T(8,128)(2,1)}, u32[]{:S(2)}, u32[]{:S(2)}) %collective-permute-start.2) | collective-permute-done | bytes 1048608 | tf_op jit(solution)/shard_map/ppermute | solution.py:1255
  124.1 14.9 %attend.1 = (bf16[1024,512]{1,0:T(8,128)(2,1)S(1)}, bf16[1024,512]{1,0:T(8,128)(2,1)S(1)}, bf16[1024,512]{1,0:T(8,128)(2,1)}, bf16[1024,512]{1,0:T(8,128)(2,1)}, f32[1024,512]{1,0:T(8,128)}) custom-call(s32[1]{0:T(128)} %bitcast.3.refs_0_, s32[1024,128]{1,0:T(8,128)S(1)} %broadcast_in_dim.37.refs_1_, f32[1024,128]{1,0:T(8,128)S(1)} %copy-done.16, ...), custom_call_target="tpu_custom_call" | custom-call | tf_op jit(solution)/shard_map/attend/pallas_call | solution.py:755
  167.5 20.9 %open_feedforward.1 = (bf16[256,2048]{1,0:T(8,128)(2,1)S(1)}, bf16[256,2048]{1,0:T(8,128)(2,1)S(1)}, f32[256,128]{1,0:T(8,128)S(1)}, f32[256,8192]{1,0:T(8,128)}) custom-call(bf16[256,8192]{1,0:T(8,128)(2,1)} %bitcast.73, f32[256,128]{1,0:T(8,128)S(1)} %get-tuple-element.181.refs_1_.refs_8_, f32[256,2048]{1,0:T(8,128)} %copy-done.15, ...), custom_call_target="tpu_custom_call" | custom-call | tf_op jit(solution)/shard_map/open_feedforward/pallas_call | solution.py:553
  194.1 21.8 %collective-permute-done.9.refs_1_ = bf16[256,2048]{1,0:T(8,128)(2,1)S(1)} collective-permute-done((bf16[256,2048]{1,0:T(8,128)(2,1)S(1)}, bf16[256,2048]{1,0:T(8,128)(2,1)S(1)}, u32[]{:S(2)}, u32[]{:S(2)}) %collective-permute-start.9) | collective-permute-done | bytes 1048608 | tf_op jit(solution)/shard_map/ppermute | solution.py:1255
  219.3 21.8 %collective-permute-done.10.refs_0_ = bf16[256,2048]{1,0:T(8,128)(2,1)S(1)} collective-permute-done((bf16[256,2048]{1,0:T(8,128)(2,1)S(1)}, bf16[256,2048]{1,0:T(8,128)(2,1)S(1)}, u32[]{:S(2)}, u32[]{:S(2)}) %collective-permute-start.10) | collective-permute-done | bytes 1048608 | tf_op jit(solution)/shard_map/ppermute | solution.py:1255
  242.9 15.2 %forward_units.2 = (f32[512,2048]{1,0:T(8,128)}, f32[512,2048]{1,0:T(8,128)}, bf16[1024,2048]{1,0:T(8,128)(2,1)}, bf16[1024,2048]{1,0:T(8,128)(2,1)}, f32[8,128]{1,0:T(8,128)S(1)}) custom-call(bf16[256,2048]{1,0:T(8,128)(2,1)S(1)} %get-tuple-element.189.refs_0_, bf16[256,2048]{1,0:T(8,128)(2,1)S(1)} %copy-done.43, ...), custom_call_target="tpu_custom_call" | custom-call | tf_op jit(solution)/shard_map/forward_units/pallas_call | solution.py:843
  258.7 6.6 collective-permute-done.11.refs_1_
  268.8 15.1 %forward_units.3 = (f32[512,2048]{1,0:T(8,128)}, f32[512,2048]{1,0:T(8,128)}, bf16[1024,2048]{1,0:T(8,128)(2,1)}, bf16[1024,2048]{1,0:T(8,128)(2,1)}, f32[8,128]{1,0:T(8,128)S(1)}) custom-call(bf16[256,2048]{1,0:T(8,128)(2,1)S(1)} %copy-done.41, bf16[256,2048]{1,0:T(8,128)(2,1)S(1)} %copy-done.27, ...), custom_call_target="tpu_custom_call", output_to_operand_aliasing={{2}: (4, {}), {3}: (5, {})} | custom-call | tf_op jit(solution)/shard_map/forward_units/pallas_call | solution.py:843
  292.6 23.2 %backward_units.2 = (f32[512,2048]{1,0:T(8,128)}, bf16[1024,2048]{1,0:T(8,128)(2,1)}, bf16[1024,2048]{1,0:T(8,128)(2,1)}, bf16[1024,2048]{1,0:T(8,128)(2,1)}, f32[8,128]{1,0:T(8,128)S(1)}) custom-call(bf16[256,2048]{1,0:T(8,128)(2,1)S(1)} %copy-done.25, bf16[256,2048]{1,0:T(8,128)(2,1)S(1)} %copy-done.29, f32[512,2048]{1,0:T(8,128)} %get-tuple-element.196.refs_2_, ...), custom_call_target="tpu_custom_call" | custom-call | tf_op jit(solution)/shard_map/backward_units/pallas_call | solution.py:880
  318.1 22.2 %backproject.5 = (f32[1024,2048]{1,0:T(8,128)}, f32[8,128]{1,0:T(8,128)}) custom-call(bf16[1024,2048]{1,0:T(8,128)(2,1)} %get-tuple-element.192.d_ref.refs_1_, bf16[2048,2048]{1,0:T(8,128)(2,1)} %all-gather.11.cloned.1.call-done.refs_4_.w_ref, f32[8,128]{1,0:T(8,128)S(1)} %copy-done.79), custom_call_target="tpu_custom_call" | custom-call | tf_op jit(solution)/shard_map/backproject/pallas_call | solution.py:1073
  345.4 23.4 %backward_units.3 = (f32[512,2048]{1,0:T(8,128)}, bf16[1024,2048]{1,0:T(8,128)(2,1)}, bf16[1024,2048]{1,0:T(8,128)(2,1)}, bf16[1024,2048]{1,0:T(8,128)(2,1)}, f32[8,128]{1,0:T(8,128)}) custom-call(bf16[256,2048]{1,0:T(8,128)(2,1)S(1)} %copy-done.23, ...), custom_call_target="tpu_custom_call", output_to_operand_aliasing={{1}: (7, {}), {2}: (8, {}), {3}: (9, {})} | custom-call | tf_op jit(solution)/shard_map/backward_units/pallas_call | solution.py:880
  368.7 8.3 away_product.5
  377.0 8.3 away_product.6
  396.9 8.3 away_product.7
  405.3 10.7 %own_product.8 = (bf16[512,2048]{1,0:T(8,128)(2,1)S(1)}, f32[512,2048]{1,0:T(8,128)}, f32[8,128]{1,0:T(8,128)S(1)}) custom-call(s32[2]{0:T(128)S(1)} %pad_add_fusion.1.scalars_ref, bf16[1024,2048]{1,0:T(8,128)(2,1)} %get-tuple-element.209.refs_0_, bf16[1024,2048]{1,0:T(8,128)(2,1)} %get-tuple-element.210.refs_1_, ...), custom_call_target="tpu_custom_call" | custom-call | tf_op jit(solution)/shard_map/own_product/pallas_call | solution.py:1024
  417.3 10.7 %own_product.9 = (bf16[512,2048]{1,0:T(8,128)(2,1)S(1)}, f32[512,2048]{1,0:T(8,128)}, f32[8,128]{1,0:T(8,128)S(1)}) custom-call(s32[2]{0:T(128)S(1)} %pad_add_fusion.2.scalars_ref, bf16[1024,2048]{1,0:T(8,128)(2,1)} %get-tuple-element.209.refs_0_, bf16[1024,2048]{1,0:T(8,128)(2,1)} %get-tuple-element.212.refs_1_, ...), custom_call_target="tpu_custom_call" | custom-call | tf_op jit(solution)/shard_map/own_product/pallas_call | solution.py:1024
  429.3 16.2 %collective-permute-done.16.refs_2_.refs_3_ = bf16[512,2048]{1,0:T(8,128)(2,1)S(1)} collective-permute-done((bf16[512,2048]{1,0:T(8,128)(2,1)}, bf16[512,2048]{1,0:T(8,128)(2,1)S(1)}, u32[]{:S(2)}, u32[]{:S(2)}) %collective-permute-start.16) | collective-permute-done | bytes 2097184 | tf_op jit(solution)/shard_map/ppermute | solution.py:1255
  457.1 7.9 own_product.10
  467.5 7.1 own_product.11
  478.6 16.5 %close_feedforward.2 = (f32[256,8192]{1,0:T(8,128)}, f32[256,128]{1,0:T(8,128)S(1)}, bf16[256,2048]{1,0:T(8,128)(2,1)S(1)}, f32[16,2048]{1,0:T(8,128)S(1)}, f32[8,128]{1,0:T(8,128)S(1)}) custom-call(f32[256,8192]{1,0:T(8,128)} %get-tuple-element.187.refs_0_.h_ref, f32[256,128]{1,0:T(8,128)S(1)} %get-tuple-element.188.refs_1_.saved_ref, ...), custom_call_target="tpu_custom_call" | custom-call | flops 30000001024 | tf_op jit(solution)/shard_map/close_feedforward/pallas_call | solution.py:626
  499.6 16.8 %close_feedforward.3 = (f32[256,8192]{1,0:T(8,128)}, f32[256,128]{1,0:T(8,128)S(1)}, bf16[256,2048]{1,0:T(8,128)(2,1)S(1)}, f32[16,2048]{1,0:T(8,128)S(1)}, f32[8,128]{1,0:T(8,128)S(1)}) custom-call(f32[256,8192]{1,0:T(8,128)} %get-tuple-element.187.refs_0_.h_ref, ...), custom_call_target="tpu_custom_call", output_to_operand_aliasing={{0}: (12, {}), {1}: (13, {}), {2}: (14, {})} | custom-call | flops 30000001024 | tf_op jit(solution)/shard_map/close_feedforward/pallas_call | solution.py:626
  600.4 17.2 %attend_back.1.d_ref.refs_4_ = bf16[1024,1536]{1,0:T(8,128)(2,1)} custom-call(s32[1]{0:T(128)} %bitcast.3.refs_0_, s32[1024,128]{1,0:T(8,128)S(1)} %copy-done.21, f32[1024,128]{1,0:T(8,128)S(1)} %copy-done.17, f32[1024,128]{1,0:T(8,128)S(1)} %copy-done.19, bf16[1024,512]{1,0:T(8,128)(2,1)S(1)} %copy-done.36, bf16[1024,512]{1,0:T(8,128)(2,1)} %copy-done.37, ...), custom_call_target="tpu_custom_call" | custom-call | tf_op jit(solution)/shard_map/attend_back/pallas_call | solution.py:775
  625.2 7.3 away_product.8
  707.4 11.5 %assemble.4 = (f32[2048,2048]{1,0:T(8,128)}, f32[8,128]{1,0:T(8,128)S(1)}) custom-call(s32[8]{0:T(128)S(1)} %stack.172.table_ref, bf16[2048,2048]{1,0:T(8,128)(2,1)} %hold.19.refs_0_, bf16[2048,2048]{1,0:T(8,128)(2,1)} %collective-permute-done.44.refs_1_, f32[8,128]{1,0:T(8,128)S(1)} %get-tuple-element.301.refs_2_), custom_call_target="tpu_custom_call" | custom-call | tf_op jit(solution)/shard_map/assemble/pallas_call | solution.py:929
  733.2 28.2 %close_attention.1 = (bf16[256,4,2048]{2,1,0:T(4,128)(2,1)}, f32[16,2048]{1,0:T(8,128)S(1)}, f32[8,128]{1,0:T(8,128)S(1)}) custom-call(bf16[256,8192]{1,0:T(8,128)(2,1)} %bitcast.74, f32[256,128]{1,0:T(8,128)S(1)} %get-tuple-element.181.refs_1_.refs_8_, f32[256,8192]{1,0:T(8,128)} %get-tuple-element.254.refs_2_, ...), custom_call_target="tpu_custom_call" | custom-call | tf_op jit(solution)/shard_map/close_attention/pallas_call | solution.py:626
  768.5 11.5 %assemble.5 = (f32[2048,2048]{1,0:T(8,128)}, f32[8,128]{1,0:T(8,128)S(1)}) custom-call(s32[8]{0:T(128)S(1)} %stack.198.table_ref, bf16[2048,2048]{1,0:T(8,128)(2,1)} %hold.19.refs_0_, bf16[2048,2048]{1,0:T(8,128)(2,1)} %collective-permute-done.44.refs_1_, f32[208,128]{1,0:T(8,128)S(1)} %pad_maximum_fusion.6.refs_2_.refs_0_, ...), custom_call_target="tpu_custom_call" | custom-call | tf_op jit(solution)/shard_map/assemble/pallas_call | solution.py:929
  795.8 14.4 %assemble.6 = (f32[2048,2048]{1,0:T(8,128)}, f32[8,128]{1,0:T(8,128)S(1)}) custom-call(s32[16]{0:T(128)S(1)} %stack.189.table_ref, bf16[1024,2048]{1,0:T(8,128)(2,1)} %get-tuple-element.333.refs_0_, bf16[1024,2048]{1,0:T(8,128)(2,1)} %collective-permute-done.57.refs_1_, f32[8,128]{1,0:T(8,128)S(1)} %get-tuple-element.334.refs_2_), custom_call_target="tpu_custom_call" | custom-call | tf_op jit(solution)/shard_map/assemble/pallas_call | solution.py:929
  828.3 14.6 %assemble.7 = (f32[2048,512]{1,0:T(8,128)}, f32[2048,512]{1,0:T(8,128)}, f32[2048,512]{1,0:T(8,128)}, f32[2048,512]{1,0:T(8,128)}, f32[8,128]{1,0:T(8,128)}) custom-call(s32[16]{0:T(128)S(1)} %stack.189.table_ref, bf16[1024,2048]{1,0:T(8,128)(2,1)} %get-tuple-element.337.refs_0_, bf16[1024,2048]{1,0:T(8,128)(2,1)} %collective-permute-done.58.refs_1_, ...), custom_call_target="tpu_custom_call" | custom-call | tf_op jit(solution)/shard_map/assemble/pallas_call | solution.py:929
  (470 shorter events, 354.0 us)
Async XLA Ops:
  7.2 88.4 %all-gather.5.cloned.1.call-start = ((), (), s32[]{:S(2)}) async-start(), calls=%async_computation | async-start | bytes 7077888 | tf_op jit(solution)/shard_map/all_gather | solution.py:1414
  9.3 150.4 %all-gather.7.cloned.1.call-start = ((), (), s32[]{:S(2)}) async-start(), calls=%async_computation.1 | async-start | bytes 9437184 | tf_op jit(solution)/shard_map/all_gather | solution.py:1414
  9.3 29.9 %collective-permute-start.6 = (bf16[256,512]{1,0:T(8,128)(2,1)}, bf16[256,512]{1,0:T(8,128)(2,1)S(1)}, u32[]{:S(2)}, u32[]{:S(2)}) collective-permute-start(bf16[256,512]{1,0:T(8,128)(2,1)} %param.21), channel_id=1, source_target_pairs={{0,1},{1,2},{2,3},{3,0},{4,5},{5,6},{6,7},{7,4},{8,9},{9,10},{10,1... | collective-permute-start | bytes 786440 | tf_op jit(solution)/shard_map/ppermute | solution.py:1459
  12.4 26.9 %collective-permute-start.7 = (bf16[256,512]{1,0:T(8,128)(2,1)}, bf16[256,512]{1,0:T(8,128)(2,1)S(1)}, u32[]{:S(2)}, u32[]{:S(2)}) collective-permute-start(bf16[256,512]{1,0:T(8,128)(2,1)} %param.21), channel_id=1, source_target_pairs={{0,2},{1,3},{2,0},{3,1},{4,6},{5,7},{6,4},{7,5},{8,10},{9,11},{10,... | collective-permute-start | bytes 786440 | tf_op jit(solution)/shard_map/ppermute | solution.py:1459
  42.4 199.2 %all-gather.9.cloned.1.call-start = ((), (), s32[]{:S(2)}) async-start(), calls=%async_computation.2 | async-start | bytes 18874368 | tf_op jit(solution)/shard_map/all_gather | solution.py:1414
  44.0 247.3 %all-gather.11.cloned.1.call-start = ((), (), s32[]{:S(2)}) async-start(), calls=%async_computation.3 | async-start | bytes 9437184 | tf_op jit(solution)/shard_map/all_gather | solution.py:1414
  44.6 25.9 %collective-permute-start = (bf16[256,2048]{1,0:T(8,128)(2,1)S(1)}, bf16[256,2048]{1,0:T(8,128)(2,1)S(1)}, u32[]{:S(2)}, u32[]{:S(2)}) collective-permute-start(bf16[256,2048]{1,0:T(8,128)(2,1)S(1)} %copy-done.8), channel_id=1, source_target_pairs={{0,1},{1,2},{2,3},{3,0},{4,5},{5,6},{6,7},{7,4},{8,9},{9,10},{10,1... | collective-permute-start | bytes 3145736 | tf_op jit(solution)/shard_map/ppermute | solution.py:1255
  189.4 26.4 %collective-permute-start.9 = (bf16[256,2048]{1,0:T(8,128)(2,1)S(1)}, bf16[256,2048]{1,0:T(8,128)(2,1)S(1)}, u32[]{:S(2)}, u32[]{:S(2)}) collective-permute-start(bf16[256,2048]{1,0:T(8,128)(2,1)S(1)} %get-tuple-element.189.refs_0_), channel_id=1, source_target_pairs={{0,1},{1,2},{2,3},{3,0},{4,5},{5,6},{6,7},{7,4},{8,9},{9,10},{10,1... | collective-permute-start | bytes 3145736 | tf_op jit(solution)/shard_map/ppermute | solution.py:1255
  344.6 45.2 %collective-permute-start.15 = (bf16[512,2048]{1,0:T(8,128)(2,1)}, bf16[512,2048]{1,0:T(8,128)(2,1)}, u32[]{:S(2)}, u32[]{:S(2)}) collective-permute-start(bf16[512,2048]{1,0:T(8,128)(2,1)} %get-tuple-element.208), channel_id=1, source_target_pairs={{0,1},{1,2},{2,3},{3,0},{4,5},{5,6},{6,7},{7,4},{8,9},{9,10},{10,1... | collective-permute-start | bytes 6291464 | tf_op jit(solution)/shard_map/ppermute | solution.py:1255
  395.9 49.7 %collective-permute-start.16 = (bf16[512,2048]{1,0:T(8,128)(2,1)}, bf16[512,2048]{1,0:T(8,128)(2,1)S(1)}, u32[]{:S(2)}, u32[]{:S(2)}) collective-permute-start(bf16[512,2048]{1,0:T(8,128)(2,1)} %copy-done.91), channel_id=1, source_target_pairs={{0,1},{1,2},{2,3},{3,0},{4,5},{5,6},{6,7},{7,4},{8,9},{9,10},{10,1... | collective-permute-start | bytes 6291464 | tf_op jit(solution)/shard_map/ppermute | solution.py:1255
  449.6 28.0 %collective-permute-start.20 = (bf16[256,2048]{1,0:T(8,128)(2,1)}, bf16[256,2048]{1,0:T(8,128)(2,1)S(1)}, u32[]{:S(2)}, u32[]{:S(2)}) collective-permute-start(bf16[256,2048]{1,0:T(8,128)(2,1)} %copy-done.93), channel_id=1, source_target_pairs={{0,1},{1,2},{2,3},{3,0},{4,5},{5,6},{6,7},{7,4},{8,9},{9,10},{10,1... | collective-permute-start | bytes 3145736 | tf_op jit(solution)/shard_map/ppermute | solution.py:1255
  453.4 46.2 %collective-permute-start.19 = (bf16[256,2048]{1,0:T(8,128)(2,1)}, bf16[256,2048]{1,0:T(8,128)(2,1)S(1)}, u32[]{:S(2)}, u32[]{:S(2)}) collective-permute-start(bf16[256,2048]{1,0:T(8,128)(2,1)} %get-tuple-element.224), channel_id=1, source_target_pairs={{0,1},{1,2},{2,3},{3,0},{4,5},{5,6},{6,7},{7,4},{8,9},{9,10},{10,1... | collective-permute-start | bytes 3145736 | tf_op jit(solution)/shard_map/ppermute | solution.py:1255
  454.0 62.8 %collective-permute-start.21 = (bf16[512,2048]{1,0:T(8,128)(2,1)S(1)}, bf16[512,2048]{1,0:T(8,128)(2,1)}, u32[]{:S(2)}, u32[]{:S(2)}) collective-permute-start(bf16[512,2048]{1,0:T(8,128)(2,1)S(1)} %copy-done.90), channel_id=1, source_target_pairs={{0,8},{4,12},{8,0},{12,4},{16,24},{20,28},{24,16},{28,20},{1,9},{5... | collective-permute-start | bytes 6291464 | tf_op jit(solution)/shard_map/ppermute | solution.py:1288
  455.2 68.0 %collective-permute-start.25 = (bf16[512,2048]{1,0:T(8,128)(2,1)S(1)}, bf16[512,2048]{1,0:T(8,128)(2,1)}, u32[]{:S(2)}, u32[]{:S(2)}) collective-permute-start(bf16[512,2048]{1,0:T(8,128)(2,1)S(1)} %copy-done.88), channel_id=1, source_target_pairs={{0,16},{4,20},{8,24},{12,28},{16,0},{20,4},{24,8},{28,12},{1,17},{... | collective-permute-start | bytes 6291464 | tf_op jit(solution)/shard_map/ppermute | solution.py:1288
  466.2 63.6 %collective-permute-start.26 = (bf16[256,2048]{1,0:T(8,128)(2,1)}, bf16[256,2048]{1,0:T(8,128)(2,1)S(1)}, u32[]{:S(2)}, u32[]{:S(2)}) collective-permute-start(bf16[256,2048]{1,0:T(8,128)(2,1)} %get-tuple-element.243), channel_id=1, source_target_pairs={{0,8},{4,12},{8,0},{12,4},{16,24},{20,28},{24,16},{28,20},{1,9},{5... | collective-permute-start | bytes 3145736 | tf_op jit(solution)/shard_map/ppermute | solution.py:1288
  477.6 54.6 %collective-permute-start.27 = (bf16[256,2048]{1,0:T(8,128)(2,1)S(1)}, bf16[256,2048]{1,0:T(8,128)(2,1)S(1)}, u32[]{:S(2)}, u32[]{:S(2)}) collective-permute-start(bf16[256,2048]{1,0:T(8,128)(2,1)S(1)} %get-tuple-element.246), channel_id=1, source_target_pairs={{0,16},{4,20},{8,24},{12,28},{16,0},{20,4},{24,8},{28,12},{1,17},{... | collective-permute-start | bytes 3145736 | tf_op jit(solution)/shard_map/ppermute | solution.py:1288
  516.5 26.8 %collective-permute-start.24 = (bf16[256,2048]{1,0:T(8,128)(2,1)S(1)}, bf16[256,2048]{1,0:T(8,128)(2,1)S(1)}, u32[]{:S(2)}, u32[]{:S(2)}) collective-permute-start(bf16[256,2048]{1,0:T(8,128)(2,1)S(1)} %get-tuple-element.235.refs_0_), channel_id=1, source_target_pairs={{0,1},{1,2},{2,3},{3,0},{4,5},{5,6},{6,7},{7,4},{8,9},{9,10},{10,1... | collective-permute-start | bytes 3145736 | tf_op jit(solution)/shard_map/ppermute | solution.py:1255
  528.2 25.7 %collective-permute-start.28 = (bf16[256,2048]{1,0:T(8,128)(2,1)}, bf16[256,2048]{1,0:T(8,128)(2,1)}, u32[]{:S(2)}, u32[]{:S(2)}) collective-permute-start(bf16[256,2048]{1,0:T(8,128)(2,1)} %get-tuple-element.250), channel_id=1, source_target_pairs={{0,8},{4,12},{8,0},{12,4},{16,24},{20,28},{24,16},{28,20},{1,9},{5... | collective-permute-start | bytes 3145736 | tf_op jit(solution)/shard_map/ppermute | solution.py:1288
  544.2 27.3 %collective-permute-start.29 = (bf16[256,2048]{1,0:T(8,128)(2,1)}, bf16[256,2048]{1,0:T(8,128)(2,1)S(1)}, u32[]{:S(2)}, u32[]{:S(2)}) collective-permute-start(bf16[256,2048]{1,0:T(8,128)(2,1)} %hold.16.refs_2_.refs_0_.refs_1_), channel_id=1, source_target_pairs={{0,1},{1,2},{2,3},{3,0},{4,5},{5,6},{6,7},{7,4},{8,9},{9,10},{10,1... | collective-permute-start | bytes 3145736 | tf_op jit(solution)/shard_map/ppermute | solution.py:1255
  580.9 62.5 %collective-permute-start.34 = (bf16[512,2048]{1,0:T(8,128)(2,1)}, bf16[512,2048]{1,0:T(8,128)(2,1)}, u32[]{:S(2)}, u32[]{:S(2)}) collective-permute-start(bf16[512,2048]{1,0:T(8,128)(2,1)} %get-tuple-element.269.refs_0_), channel_id=1, source_target_pairs={{0,8},{4,12},{8,0},{12,4},{16,24},{20,28},{24,16},{28,20},{1,9},{5... | collective-permute-start | bytes 6291464 | tf_op jit(solution)/shard_map/ppermute | solution.py:1288
  585.1 58.4 %collective-permute-start.35 = (bf16[512,2048]{1,0:T(8,128)(2,1)}, bf16[512,2048]{1,0:T(8,128)(2,1)}, u32[]{:S(2)}, u32[]{:S(2)}) collective-permute-start(bf16[512,2048]{1,0:T(8,128)(2,1)} %get-tuple-element.270.refs_2_), channel_id=1, source_target_pairs={{0,16},{4,20},{8,24},{12,28},{16,0},{20,4},{24,8},{28,12},{1,17},{... | collective-permute-start | bytes 6291464 | tf_op jit(solution)/shard_map/ppermute | solution.py:1288
  622.8 27.3 %collective-permute-start.33 = (bf16[256,2048]{1,0:T(8,128)(2,1)S(1)}, bf16[256,2048]{1,0:T(8,128)(2,1)S(1)}, u32[]{:S(2)}, u32[]{:S(2)}) collective-permute-start(bf16[256,2048]{1,0:T(8,128)(2,1)S(1)} %get-tuple-element.268), channel_id=1, source_target_pairs={{0,1},{1,2},{2,3},{3,0},{4,5},{5,6},{6,7},{7,4},{8,9},{9,10},{10,1... | collective-permute-start | bytes 3145736 | tf_op jit(solution)/shard_map/ppermute | solution.py:1255
  654.1 35.5 %collective-permute-start.38 = (bf16[256,2048]{1,0:T(8,128)(2,1)}, bf16[256,2048]{1,0:T(8,128)(2,1)S(1)}, u32[]{:S(2)}, u32[]{:S(2)}) collective-permute-start(bf16[256,2048]{1,0:T(8,128)(2,1)} %copy-done.92), channel_id=1, source_target_pairs={{0,1},{1,2},{2,3},{3,0},{4,5},{5,6},{6,7},{7,4},{8,9},{9,10},{10,1... | collective-permute-start | bytes 3145736 | tf_op jit(solution)/shard_map/ppermute | solution.py:1255
  656.2 31.4 %collective-permute-start.40 = (bf16[128,2048]{1,0:T(8,128)(2,1)}, bf16[128,2048]{1,0:T(8,128)(2,1)S(1)}, u32[]{:S(2)}, u32[]{:S(2)}) collective-permute-start(bf16[128,2048]{1,0:T(8,128)(2,1)} %copy-done.56), channel_id=1, source_target_pairs={{0,16},{4,20},{8,24},{12,28},{16,0},{20,4},{24,8},{28,12},{1,17},{... | collective-permute-start | bytes 1572872 | tf_op jit(solution)/shard_map/ppermute | solution.py:1288
  657.5 31.1 %collective-permute-start.41 = (bf16[128,2048]{1,0:T(8,128)(2,1)}, bf16[128,2048]{1,0:T(8,128)(2,1)S(1)}, u32[]{:S(2)}, u32[]{:S(2)}) collective-permute-start(bf16[128,2048]{1,0:T(8,128)(2,1)} %copy-done.58), channel_id=1, source_target_pairs={{0,8},{4,12},{8,0},{12,4},{16,24},{20,28},{24,16},{28,20},{1,9},{5... | collective-permute-start | bytes 1572872 | tf_op jit(solution)/shard_map/ppermute | solution.py:1288
  693.9 25.9 %collective-permute-start.43 = (bf16[256,2048]{1,0:T(8,128)(2,1)}, bf16[256,2048]{1,0:T(8,128)(2,1)}, u32[]{:S(2)}, u32[]{:S(2)}) collective-permute-start(bf16[256,2048]{1,0:T(8,128)(2,1)} %get-tuple-element.299), channel_id=1, source_target_pairs={{0,8},{4,12},{8,0},{12,4},{16,24},{20,28},{24,16},{28,20},{1,9},{5... | collective-permute-start | bytes 3145736 | tf_op jit(solution)/shard_map/ppermute | solution.py:1288
  695.5 29.2 %collective-permute-start.45 = (bf16[256,2048]{1,0:T(8,128)(2,1)}, bf16[256,2048]{1,0:T(8,128)(2,1)}, u32[]{:S(2)}, u32[]{:S(2)}) collective-permute-start(bf16[256,2048]{1,0:T(8,128)(2,1)} %get-tuple-element.305), channel_id=1, source_target_pairs={{0,16},{4,20},{8,24},{12,28},{16,0},{20,4},{24,8},{28,12},{1,17},{... | collective-permute-start | bytes 3145736 | tf_op jit(solution)/shard_map/ppermute | solution.py:1288
  696.2 37.0 %collective-permute-start.42 = (bf16[256,2048]{1,0:T(8,128)(2,1)}, bf16[256,2048]{1,0:T(8,128)(2,1)S(1)}, u32[]{:S(2)}, u32[]{:S(2)}) collective-permute-start(bf16[256,2048]{1,0:T(8,128)(2,1)} %get-tuple-element.294), channel_id=1, source_target_pairs={{0,1},{1,2},{2,3},{3,0},{4,5},{5,6},{6,7},{7,4},{8,9},{9,10},{10,1... | collective-permute-start | bytes 3145736 | tf_op jit(solution)/shard_map/ppermute | solution.py:1255
  723.7 37.8 %collective-permute-start.46 = (bf16[128,2048]{1,0:T(8,128)(2,1)}, bf16[128,2048]{1,0:T(8,128)(2,1)}, u32[]{:S(2)}, u32[]{:S(2)}) collective-permute-start(bf16[128,2048]{1,0:T(8,128)(2,1)} %get-tuple-element.309), channel_id=1, source_target_pairs={{0,16},{4,20},{8,24},{12,28},{16,0},{20,4},{24,8},{28,12},{1,17},{... | collective-permute-start | bytes 1572872 | tf_op jit(solution)/shard_map/ppermute | solution.py:1288
  728.6 36.0 %collective-permute-start.49 = (bf16[128,2048]{1,0:T(8,128)(2,1)}, bf16[128,2048]{1,0:T(8,128)(2,1)}, u32[]{:S(2)}, u32[]{:S(2)}) collective-permute-start(bf16[128,2048]{1,0:T(8,128)(2,1)} %get-tuple-element.319), channel_id=1, source_target_pairs={{0,8},{4,12},{8,0},{12,4},{16,24},{20,28},{24,16},{28,20},{1,9},{5... | collective-permute-start | bytes 1572872 | tf_op jit(solution)/shard_map/ppermute | solution.py:1288
  729.8 50.5 %collective-permute-start.54 = (bf16[256,2048]{1,0:T(8,128)(2,1)}, bf16[256,2048]{1,0:T(8,128)(2,1)}, u32[]{:S(2)}, u32[]{:S(2)}) collective-permute-start(bf16[256,2048]{1,0:T(8,128)(2,1)} %get-tuple-element.327.refs_0_), channel_id=1, source_target_pairs={{0,8},{4,12},{8,0},{12,4},{16,24},{20,28},{24,16},{28,20},{1,9},{5... | collective-permute-start | bytes 3145736 | tf_op jit(solution)/shard_map/ppermute | solution.py:1288
  730.7 49.6 %collective-permute-start.55 = (bf16[256,2048]{1,0:T(8,128)(2,1)}, bf16[256,2048]{1,0:T(8,128)(2,1)}, u32[]{:S(2)}, u32[]{:S(2)}) collective-permute-start(bf16[256,2048]{1,0:T(8,128)(2,1)} %get-tuple-element.328.refs_2_), channel_id=1, source_target_pairs={{0,16},{4,20},{8,24},{12,28},{16,0},{20,4},{24,8},{28,12},{1,17},{... | collective-permute-start | bytes 3145736 | tf_op jit(solution)/shard_map/ppermute | solution.py:1288
  (144 other events, 1322.8 us)
Sparse Core Ops, SparseCore 0:
  10.5 48.2 all-gather.4
  61.2 54.3 all-gather.6
  118.1 89.8 all-gather.8
  209.7 54.3 all-gather.10

commit v5 on v4

--- a/solution.py
+++ b/solution.py
@@ -14,7 +14,7 @@
 LANES = 128
 GROUP = 16
 CHUNK = 512
-PARAMS = pltpu.CompilerParams(vmem_limit_bytes=50 * 1024 * 1024)
+PARAMS = pltpu.CompilerParams(vmem_limit_bytes=58 * 1024 * 1024)
 
 
 def matmul(left, right):

time: 860 us -> 905 us (1.052)
  Pallas kernels: 496 us -> 548 us
    pallas_call x17, Pallas kernels: 33.1 us -> 53.3 us  [add_low(): pl.pallas_call(functools.partial(add_kernel, len(own), bool(arrived)), gr...]
    unnamed x227 -> x131, local copies, waits for them, and re-layouts: 60.3 us -> 48 us
  transfers between devices with their start and end apart: 65 -> 65, of which waited for: 26 -> 25; matrix products, arithmetic and copies ran while one was open for 5% -> 6% of each run, Pallas kernels for 54% -> 56%
where the time goes in v5:
time: 905 us; the launch traced here: 894 us
  Pallas kernels  548 us (61%)
  waiting for transfers between devices  183 us (20%)
  starting transfers between devices  59 us (7%)
  local copies, waits for them, and re-layouts  57.4 us (6%)
  matrix products  16.1 us (2%)
  other arithmetic  15 us (2%)
  between operations  14.9 us (2%)
    ppermute x19, waiting for transfers between devices, ring_shift(): lax.ppermute(block, 'tensor', [(i, (i + 1) % size) for i in range(size)])  151 us
    pallas_call x3, Pallas kernels, close_mix(): pl.pallas_call(functools.partial(close_kernel, streams, uses, width, inne...  62.8 us
    pallas_call x8, Pallas kernels, own_product(): pl.pallas_call(functools.partial(own_kernel, len(left)), grid_spec=pltpu....  61.8 us
    pallas_call x17, Pallas kernels, add_low(): pl.pallas_call(functools.partial(add_kernel, len(own), bool(arrived)), gr...  53.3 us
    pallas_call x4, Pallas kernels, assemble(): pl.pallas_call(functools.partial(assemble_kernel, count, pieces, len(toke...  52.5 us
    pallas_call x2, Pallas kernels, backward_units(): pl.pallas_call(functools.partial(backward_units_kernel, len(filled) + len...  49.7 us
    unnamed x131, local copies, waits for them, and re-layouts  48 us
    pallas_call x5, Pallas kernels, backproject(): pl.pallas_call(backproject_kernel, grid=(width // across, count), in_spec...  46 us
  transfers between devices with their start and end apart: 65, of which 25 were waited for; matrix products, arithmetic and copies ran while one was open for 6% of the time, Pallas kernels for 56%

profile of v5, /device:TPU:0, one launch (start us, length us, event | category | flops | bytes accessed | tf_op | source)
XLA Modules:
  0.0 893.8 jit_solution(2461638461536981627)
XLA Ops:
  16.4 8.6 copy.63
  26.5 13.6 %open_attention.1 = (bf16[256,2048]{1,0:T(8,128)(2,1)}, f32[256,128]{1,0:T(8,128)}) custom-call(bf16[256,8192]{1,0:T(8,128)(2,1)} %bitcast.72, f32[8,2048]{1,0:T(8,128)} %pad.14.w_ref.refs_6_, f32[8,128]{1,0:T(8,128)} %select_maximum_fusion.1.param_ref.refs_7_), custom_call_target="tpu_custom_call" | custom-call | tf_op jit(solution)/shard_map/open_attention/pallas_call | solution.py:527
  46.6 24.7 %collective-permute-done.refs_1_ = bf16[256,2048]{1,0:T(8,128)(2,1)S(1)} collective-permute-done((bf16[256,2048]{1,0:T(8,128)(2,1)S(1)}, bf16[256,2048]{1,0:T(8,128)(2,1)S(1)}, u32[]{:S(2)}, u32[]{:S(2)}) %collective-permute-start) | collective-permute-done | bytes 1048608 | tf_op jit(solution)/shard_map/ppermute | solution.py:1255
  74.9 21.3 %collective-permute-done.1.refs_2_ = bf16[256,2048]{1,0:T(8,128)(2,1)S(1)} collective-permute-done((bf16[256,2048]{1,0:T(8,128)(2,1)S(1)}, bf16[256,2048]{1,0:T(8,128)(2,1)S(1)}, u32[]{:S(2)}, u32[]{:S(2)}) %collective-permute-start.1) | collective-permute-done | bytes 1048608 | tf_op jit(solution)/shard_map/ppermute | solution.py:1255
  108.4 12.1 %collective-permute-done.2.refs_3_ = bf16[256,2048]{1,0:T(8,128)(2,1)} collective-permute-done((bf16[256,2048]{1,0:T(8,128)(2,1)S(1)}, bf16[256,2048]{1,0:T(8,128)(2,1)}, u32[]{:S(2)}, u32[]{:S(2)}) %collective-permute-start.2) | collective-permute-done | bytes 1048608 | tf_op jit(solution)/shard_map/ppermute | solution.py:1255
  125.7 15.6 %attend.1 = (bf16[1024,512]{1,0:T(8,128)(2,1)}, bf16[1024,512]{1,0:T(8,128)(2,1)}, bf16[1024,512]{1,0:T(8,128)(2,1)}, bf16[1024,512]{1,0:T(8,128)(2,1)}, f32[1024,512]{1,0:T(8,128)}) custom-call(s32[1]{0:T(128)} %bitcast.3.refs_0_, s32[1024,128]{1,0:T(8,128)} %broadcast_in_dim.37.refs_1_, f32[1024,128]{1,0:T(8,128)} %get-tuple-element.393.refs_2_, ...), custom_call_target="tpu_custom_call" | custom-call | tf_op jit(solution)/shard_map/attend/pallas_call | solution.py:755
  168.7 21.4 %open_feedforward.1 = (bf16[256,2048]{1,0:T(8,128)(2,1)}, bf16[256,2048]{1,0:T(8,128)(2,1)}, f32[256,128]{1,0:T(8,128)}, f32[256,8192]{1,0:T(8,128)}) custom-call(bf16[256,8192]{1,0:T(8,128)(2,1)} %bitcast.73, f32[256,128]{1,0:T(8,128)} %get-tuple-element.181.refs_1_.refs_8_, f32[256,2048]{1,0:T(8,128)} %out_project.1.refs_2_.refs_9_, ...), custom_call_target="tpu_custom_call" | custom-call | tf_op jit(solution)/shard_map/open_feedforward/pallas_call | solution.py:553
  195.3 22.1 %collective-permute-done.9.refs_1_ = bf16[256,2048]{1,0:T(8,128)(2,1)S(1)} collective-permute-done((bf16[256,2048]{1,0:T(8,128)(2,1)}, bf16[256,2048]{1,0:T(8,128)(2,1)S(1)}, u32[]{:S(2)}, u32[]{:S(2)}) %collective-permute-start.9) | collective-permute-done | bytes 1048608 | tf_op jit(solution)/shard_map/ppermute | solution.py:1255
  219.8 22.8 %collective-permute-done.10.refs_0_ = bf16[256,2048]{1,0:T(8,128)(2,1)S(1)} collective-permute-done((bf16[256,2048]{1,0:T(8,128)(2,1)S(1)}, bf16[256,2048]{1,0:T(8,128)(2,1)S(1)}, u32[]{:S(2)}, u32[]{:S(2)}) %collective-permute-start.10) | collective-permute-done | bytes 1048608 | tf_op jit(solution)/shard_map/ppermute | solution.py:1255
  243.2 15.7 %forward_units.2 = (f32[512,2048]{1,0:T(8,128)}, f32[512,2048]{1,0:T(8,128)}, bf16[1024,2048]{1,0:T(8,128)(2,1)}, bf16[1024,2048]{1,0:T(8,128)(2,1)}, f32[8,128]{1,0:T(8,128)}) custom-call(bf16[256,2048]{1,0:T(8,128)(2,1)} %get-tuple-element.189.refs_0_, bf16[256,2048]{1,0:T(8,128)(2,1)} %copy-done.29, ...), custom_call_target="tpu_custom_call" | custom-call | tf_op jit(solution)/shard_map/forward_units/pallas_call | solution.py:843
  258.9 7.9 collective-permute-done.11.refs_1_
  267.8 15.7 %forward_units.3 = (f32[512,2048]{1,0:T(8,128)}, f32[512,2048]{1,0:T(8,128)}, bf16[1024,2048]{1,0:T(8,128)(2,1)}, bf16[1024,2048]{1,0:T(8,128)(2,1)}, f32[8,128]{1,0:T(8,128)}) custom-call(bf16[256,2048]{1,0:T(8,128)(2,1)} %copy-done.27, bf16[256,2048]{1,0:T(8,128)(2,1)} %copy-done.13, ...), custom_call_target="tpu_custom_call", output_to_operand_aliasing={{2}: (4, {}), {3}: (5, {})} | custom-call | tf_op jit(solution)/shard_map/forward_units/pallas_call | solution.py:843
  283.5 7.9 collective-permute-done.12.refs_0_
  292.7 24.8 %backward_units.2 = (f32[512,2048]{1,0:T(8,128)}, bf16[1024,2048]{1,0:T(8,128)(2,1)}, bf16[1024,2048]{1,0:T(8,128)(2,1)}, bf16[1024,2048]{1,0:T(8,128)(2,1)}, f32[8,128]{1,0:T(8,128)}) custom-call(bf16[256,2048]{1,0:T(8,128)(2,1)} %hold.11.refs_0_, bf16[256,2048]{1,0:T(8,128)(2,1)} %hold.12.refs_1_, f32[512,2048]{1,0:T(8,128)} %get-tuple-element.196.refs_2_, ...), custom_call_target="tpu_custom_call" | custom-call | tf_op jit(solution)/shard_map/backward_units/pallas_call | solution.py:880
  318.5 22.2 %backproject.5 = (f32[1024,2048]{1,0:T(8,128)}, f32[8,128]{1,0:T(8,128)}) custom-call(bf16[1024,2048]{1,0:T(8,128)(2,1)} %get-tuple-element.192.d_ref.refs_1_, bf16[2048,2048]{1,0:T(8,128)(2,1)} %all-gather.11.cloned.1.call-done.refs_4_.w_ref, f32[8,128]{1,0:T(8,128)} %get-tuple-element.198.refs_0_.refs_1_), custom_call_target="tpu_custom_call" | custom-call | tf_op jit(solution)/shard_map/backproject/pallas_call | solution.py:1073
  346.6 24.9 %backward_units.3 = (f32[512,2048]{1,0:T(8,128)}, bf16[1024,2048]{1,0:T(8,128)(2,1)}, bf16[1024,2048]{1,0:T(8,128)(2,1)}, bf16[1024,2048]{1,0:T(8,128)(2,1)}, f32[8,128]{1,0:T(8,128)}) custom-call(bf16[256,2048]{1,0:T(8,128)(2,1)} %hold.13.refs_0_, bf16[256,2048]{1,0:T(8,128)(2,1)} %copy-done.12, ...), custom_call_target="tpu_custom_call", output_to_operand_aliasing={{1}: (7, {}), {2}: (8, {}), {3}: (9, {})} | custom-call | tf_op jit(solution)/shard_map/backward_units/pallas_call | solution.py:880
  371.6 8.3 away_product.5
  379.9 8.3 away_product.6
  400.3 8.3 away_product.7
  408.7 11.4 %own_product.8 = (bf16[512,2048]{1,0:T(8,128)(2,1)}, f32[512,2048]{1,0:T(8,128)}, f32[8,128]{1,0:T(8,128)}) custom-call(s32[2]{0:T(128)} %pad_add_fusion.1.scalars_ref, bf16[1024,2048]{1,0:T(8,128)(2,1)} %get-tuple-element.209.refs_0_, bf16[1024,2048]{1,0:T(8,128)(2,1)} %get-tuple-element.210.refs_1_, bf16[1024,2048]{1,0:T(8,128)(2,1)} %collective-permute-done.17.refs_2_, ...), custom_call_target="tpu_custom_call" | custom-call | tf_op jit(solution)/shard_map/own_product/pallas_call | solution.py:1024
  420.1 11.4 %own_product.9 = (bf16[512,2048]{1,0:T(8,128)(2,1)}, f32[512,2048]{1,0:T(8,128)}, f32[8,128]{1,0:T(8,128)}) custom-call(s32[2]{0:T(128)} %pad_add_fusion.2.scalars_ref, bf16[1024,2048]{1,0:T(8,128)(2,1)} %get-tuple-element.209.refs_0_, bf16[1024,2048]{1,0:T(8,128)(2,1)} %get-tuple-element.212.refs_1_, bf16[1024,2048]{1,0:T(8,128)(2,1)} %collective-permute-done.18.refs_2_, ...), custom_call_target="tpu_custom_call" | custom-call | tf_op jit(solution)/shard_map/own_product/pallas_call | solution.py:1024
  431.5 15.8 %collective-permute-done.16.refs_2_.refs_3_ = bf16[512,2048]{1,0:T(8,128)(2,1)S(1)} collective-permute-done((bf16[512,2048]{1,0:T(8,128)(2,1)}, bf16[512,2048]{1,0:T(8,128)(2,1)S(1)}, u32[]{:S(2)}, u32[]{:S(2)}) %collective-permute-start.16) | collective-permute-done | bytes 2097184 | tf_op jit(solution)/shard_map/ppermute | solution.py:1255
  461.8 8.3 own_product.10
  471.5 8.4 own_product.11
  481.5 17.0 %close_feedforward.2 = (f32[256,8192]{1,0:T(8,128)}, f32[256,128]{1,0:T(8,128)}, bf16[256,2048]{1,0:T(8,128)(2,1)}, f32[16,2048]{1,0:T(8,128)}, f32[8,128]{1,0:T(8,128)}) custom-call(f32[256,8192]{1,0:T(8,128)} %get-tuple-element.187.refs_0_.h_ref, f32[256,128]{1,0:T(8,128)} %get-tuple-element.188.refs_1_.saved_ref, bf16[256,8192]{1,0:T(8,128)(2,1)} %bitcast.76, ...), custom_call_target="tpu_custom_call" | custom-call | flops 30000001024 | tf_op jit(solution)/shard_map/close_feedforward/pallas_call | solution.py:626
  502.6 17.1 %close_feedforward.3 = (f32[256,8192]{1,0:T(8,128)}, f32[256,128]{1,0:T(8,128)}, bf16[256,2048]{1,0:T(8,128)(2,1)}, f32[16,2048]{1,0:T(8,128)}, f32[8,128]{1,0:T(8,128)}) custom-call(f32[256,8192]{1,0:T(8,128)} %get-tuple-element.187.refs_0_.h_ref, ...), custom_call_target="tpu_custom_call", output_to_operand_aliasing={{0}: (12, {}), {1}: (13, {}), {2}: (14, {})} | custom-call | flops 30000001024 | tf_op jit(solution)/shard_map/close_feedforward/pallas_call | solution.py:626
  603.6 17.9 %attend_back.1.d_ref.refs_4_ = bf16[1024,1536]{1,0:T(8,128)(2,1)} custom-call(s32[1]{0:T(128)} %bitcast.3.refs_0_, s32[1024,128]{1,0:T(8,128)} %broadcast_in_dim.37.refs_1_, f32[1024,128]{1,0:T(8,128)} %get-tuple-element.393.refs_2_, f32[1024,128]{1,0:T(8,128)} %get-tuple-element.394.refs_3_, bf16[1024,512]{1,0:T(8,128)(2,1)} %get-tuple-element.255.refs_4_, ...), custom_call_target="tpu_custom_call" | custom-call | tf_op jit(solution)/shard_map/attend_back/pallas_call | solution.py:775
  726.9 11.6 %assemble.4 = (f32[2048,2048]{1,0:T(8,128)}, f32[8,128]{1,0:T(8,128)}) custom-call(s32[8]{0:T(128)} %stack.172.table_ref, bf16[2048,2048]{1,0:T(8,128)(2,1)} %hold.19.refs_0_, bf16[2048,2048]{1,0:T(8,128)(2,1)} %collective-permute-done.44.refs_1_, f32[8,128]{1,0:T(8,128)} %get-tuple-element.301.refs_2_), custom_call_target="tpu_custom_call" | custom-call | tf_op jit(solution)/shard_map/assemble/pallas_call | solution.py:929
  751.0 28.7 %close_attention.1 = (bf16[256,4,2048]{2,1,0:T(4,128)(2,1)}, f32[16,2048]{1,0:T(8,128)}, f32[8,128]{1,0:T(8,128)}) custom-call(bf16[256,8192]{1,0:T(8,128)(2,1)} %bitcast.74, f32[256,128]{1,0:T(8,128)} %get-tuple-element.181.refs_1_.refs_8_, f32[256,8192]{1,0:T(8,128)} %get-tuple-element.254.refs_2_, bf16[256,2048]{1,0:T(8,128)(2,1)} %copy-done.22, ...), custom_call_target="tpu_custom_call" | custom-call | tf_op jit(solution)/shard_map/close_attention/pallas_call | solution.py:626
  792.5 11.6 %assemble.5 = (f32[2048,2048]{1,0:T(8,128)}, f32[8,128]{1,0:T(8,128)}) custom-call(s32[8]{0:T(128)} %stack.198.table_ref, bf16[2048,2048]{1,0:T(8,128)(2,1)} %hold.19.refs_0_, bf16[2048,2048]{1,0:T(8,128)(2,1)} %collective-permute-done.44.refs_1_, f32[208,128]{1,0:T(8,128)} %copy-done.37, f32[8,128]{1,0:T(8,128)} %get-tuple-element.317.refs_3_, ...), custom_call_target="tpu_custom_call" | custom-call | tf_op jit(solution)/shard_map/assemble/pallas_call | solution.py:929
  830.8 14.5 %assemble.6 = (f32[2048,2048]{1,0:T(8,128)}, f32[8,128]{1,0:T(8,128)}) custom-call(s32[16]{0:T(128)} %stack.189.table_ref, bf16[1024,2048]{1,0:T(8,128)(2,1)} %get-tuple-element.333.refs_0_, bf16[1024,2048]{1,0:T(8,128)(2,1)} %collective-permute-done.57.refs_1_, f32[8,128]{1,0:T(8,128)} %get-tuple-element.334.refs_2_), custom_call_target="tpu_custom_call" | custom-call | tf_op jit(solution)/shard_map/assemble/pallas_call | solution.py:929
  872.0 14.7 %assemble.7 = (f32[2048,512]{1,0:T(8,128)}, f32[2048,512]{1,0:T(8,128)}, f32[2048,512]{1,0:T(8,128)}, f32[2048,512]{1,0:T(8,128)}, f32[8,128]{1,0:T(8,128)}) custom-call(s32[16]{0:T(128)} %stack.189.table_ref, bf16[1024,2048]{1,0:T(8,128)(2,1)} %get-tuple-element.337.refs_0_, bf16[1024,2048]{1,0:T(8,128)(2,1)} %collective-permute-done.58.refs_1_, ...), custom_call_target="tpu_custom_call" | custom-call | tf_op jit(solution)/shard_map/assemble/pallas_call | solution.py:929
  (374 shorter events, 384.0 us)
Async XLA Ops:
  7.2 89.3 %all-gather.5.cloned.1.call-start = ((), (), s32[]{:S(2)}) async-start(), calls=%async_computation | async-start | bytes 7077888 | tf_op jit(solution)/shard_map/all_gather | solution.py:1414
  9.3 151.0 %all-gather.7.cloned.1.call-start = ((), (), s32[]{:S(2)}) async-start(), calls=%async_computation.1 | async-start | bytes 9437184 | tf_op jit(solution)/shard_map/all_gather | solution.py:1414
  9.3 30.8 %collective-permute-start.6 = (bf16[256,512]{1,0:T(8,128)(2,1)}, bf16[256,512]{1,0:T(8,128)(2,1)S(1)}, u32[]{:S(2)}, u32[]{:S(2)}) collective-permute-start(bf16[256,512]{1,0:T(8,128)(2,1)} %param.21), channel_id=1, source_target_pairs={{0,1},{1,2},{2,3},{3,0},{4,5},{5,6},{6,7},{7,4},{8,9},{9,10},{10,1... | collective-permute-start | bytes 786440 | tf_op jit(solution)/shard_map/ppermute | solution.py:1459
  12.4 27.8 %collective-permute-start.7 = (bf16[256,512]{1,0:T(8,128)(2,1)}, bf16[256,512]{1,0:T(8,128)(2,1)S(1)}, u32[]{:S(2)}, u32[]{:S(2)}) collective-permute-start(bf16[256,512]{1,0:T(8,128)(2,1)} %param.21), channel_id=1, source_target_pairs={{0,2},{1,3},{2,0},{3,1},{4,6},{5,7},{6,4},{7,5},{8,10},{9,11},{10,... | collective-permute-start | bytes 786440 | tf_op jit(solution)/shard_map/ppermute | solution.py:1459
  43.3 199.9 %all-gather.9.cloned.1.call-start = ((), (), s32[]{:S(2)}) async-start(), calls=%async_computation.2 | async-start | bytes 18874368 | tf_op jit(solution)/shard_map/all_gather | solution.py:1414
  44.8 247.9 %all-gather.11.cloned.1.call-start = ((), (), s32[]{:S(2)}) async-start(), calls=%async_computation.3 | async-start | bytes 9437184 | tf_op jit(solution)/shard_map/all_gather | solution.py:1414
  45.4 25.9 %collective-permute-start = (bf16[256,2048]{1,0:T(8,128)(2,1)S(1)}, bf16[256,2048]{1,0:T(8,128)(2,1)S(1)}, u32[]{:S(2)}, u32[]{:S(2)}) collective-permute-start(bf16[256,2048]{1,0:T(8,128)(2,1)S(1)} %copy-done.7), channel_id=1, source_target_pairs={{0,1},{1,2},{2,3},{3,0},{4,5},{5,6},{6,7},{7,4},{8,9},{9,10},{10,1... | collective-permute-start | bytes 3145736 | tf_op jit(solution)/shard_map/ppermute | solution.py:1255
  190.0 27.4 %collective-permute-start.9 = (bf16[256,2048]{1,0:T(8,128)(2,1)}, bf16[256,2048]{1,0:T(8,128)(2,1)S(1)}, u32[]{:S(2)}, u32[]{:S(2)}) collective-permute-start(bf16[256,2048]{1,0:T(8,128)(2,1)} %get-tuple-element.189.refs_0_), channel_id=1, source_target_pairs={{0,1},{1,2},{2,3},{3,0},{4,5},{5,6},{6,7},{7,4},{8,9},{9,10},{10,1... | collective-permute-start | bytes 3145736 | tf_op jit(solution)/shard_map/ppermute | solution.py:1255
  346.4 44.6 %collective-permute-start.15 = (bf16[512,2048]{1,0:T(8,128)(2,1)}, bf16[512,2048]{1,0:T(8,128)(2,1)S(1)}, u32[]{:S(2)}, u32[]{:S(2)}) collective-permute-start(bf16[512,2048]{1,0:T(8,128)(2,1)} %get-tuple-element.208), channel_id=1, source_target_pairs={{0,1},{1,2},{2,3},{3,0},{4,5},{5,6},{6,7},{7,4},{8,9},{9,10},{10,1... | collective-permute-start | bytes 6291464 | tf_op jit(solution)/shard_map/ppermute | solution.py:1255
  397.6 49.8 %collective-permute-start.16 = (bf16[512,2048]{1,0:T(8,128)(2,1)}, bf16[512,2048]{1,0:T(8,128)(2,1)S(1)}, u32[]{:S(2)}, u32[]{:S(2)}) collective-permute-start(bf16[512,2048]{1,0:T(8,128)(2,1)} %get-tuple-element.214), channel_id=1, source_target_pairs={{0,1},{1,2},{2,3},{3,0},{4,5},{5,6},{6,7},{7,4},{8,9},{9,10},{10,1... | collective-permute-start | bytes 6291464 | tf_op jit(solution)/shard_map/ppermute | solution.py:1255
  452.5 28.0 %collective-permute-start.20 = (bf16[256,2048]{1,0:T(8,128)(2,1)}, bf16[256,2048]{1,0:T(8,128)(2,1)S(1)}, u32[]{:S(2)}, u32[]{:S(2)}) collective-permute-start(bf16[256,2048]{1,0:T(8,128)(2,1)} %get-tuple-element.225), channel_id=1, source_target_pairs={{0,1},{1,2},{2,3},{3,0},{4,5},{5,6},{6,7},{7,4},{8,9},{9,10},{10,1... | collective-permute-start | bytes 3145736 | tf_op jit(solution)/shard_map/ppermute | solution.py:1255
  456.4 46.2 %collective-permute-start.19 = (bf16[256,2048]{1,0:T(8,128)(2,1)}, bf16[256,2048]{1,0:T(8,128)(2,1)}, u32[]{:S(2)}, u32[]{:S(2)}) collective-permute-start(bf16[256,2048]{1,0:T(8,128)(2,1)} %get-tuple-element.224), channel_id=1, source_target_pairs={{0,1},{1,2},{2,3},{3,0},{4,5},{5,6},{6,7},{7,4},{8,9},{9,10},{10,1... | collective-permute-start | bytes 3145736 | tf_op jit(solution)/shard_map/ppermute | solution.py:1255
  457.1 62.8 %collective-permute-start.21 = (bf16[512,2048]{1,0:T(8,128)(2,1)}, bf16[512,2048]{1,0:T(8,128)(2,1)}, u32[]{:S(2)}, u32[]{:S(2)}) collective-permute-start(bf16[512,2048]{1,0:T(8,128)(2,1)} %get-tuple-element.227), channel_id=1, source_target_pairs={{0,8},{4,12},{8,0},{12,4},{16,24},{20,28},{24,16},{28,20},{1,9},{5... | collective-permute-start | bytes 6291464 | tf_op jit(solution)/shard_map/ppermute | solution.py:1288
  458.5 67.4 %collective-permute-start.25 = (bf16[512,2048]{1,0:T(8,128)(2,1)}, bf16[512,2048]{1,0:T(8,128)(2,1)}, u32[]{:S(2)}, u32[]{:S(2)}) collective-permute-start(bf16[512,2048]{1,0:T(8,128)(2,1)} %get-tuple-element.240), channel_id=1, source_target_pairs={{0,16},{4,20},{8,24},{12,28},{16,0},{20,4},{24,8},{28,12},{1,17},{... | collective-permute-start | bytes 6291464 | tf_op jit(solution)/shard_map/ppermute | solution.py:1288
  470.1 62.1 %collective-permute-start.26 = (bf16[256,2048]{1,0:T(8,128)(2,1)}, bf16[256,2048]{1,0:T(8,128)(2,1)S(1)}, u32[]{:S(2)}, u32[]{:S(2)}) collective-permute-start(bf16[256,2048]{1,0:T(8,128)(2,1)} %get-tuple-element.243), channel_id=1, source_target_pairs={{0,8},{4,12},{8,0},{12,4},{16,24},{20,28},{24,16},{28,20},{1,9},{5... | collective-permute-start | bytes 3145736 | tf_op jit(solution)/shard_map/ppermute | solution.py:1288
  480.5 56.0 %collective-permute-start.27 = (bf16[256,2048]{1,0:T(8,128)(2,1)}, bf16[256,2048]{1,0:T(8,128)(2,1)S(1)}, u32[]{:S(2)}, u32[]{:S(2)}) collective-permute-start(bf16[256,2048]{1,0:T(8,128)(2,1)} %get-tuple-element.246), channel_id=1, source_target_pairs={{0,16},{4,20},{8,24},{12,28},{16,0},{20,4},{24,8},{28,12},{1,17},{... | collective-permute-start | bytes 3145736 | tf_op jit(solution)/shard_map/ppermute | solution.py:1288
  519.7 27.0 %collective-permute-start.24 = (bf16[256,2048]{1,0:T(8,128)(2,1)}, bf16[256,2048]{1,0:T(8,128)(2,1)S(1)}, u32[]{:S(2)}, u32[]{:S(2)}) collective-permute-start(bf16[256,2048]{1,0:T(8,128)(2,1)} %get-tuple-element.235.refs_0_), channel_id=1, source_target_pairs={{0,1},{1,2},{2,3},{3,0},{4,5},{5,6},{6,7},{7,4},{8,9},{9,10},{10,1... | collective-permute-start | bytes 3145736 | tf_op jit(solution)/shard_map/ppermute | solution.py:1255
  524.9 26.0 %collective-permute-start.23 = (bf16[256,2048]{1,0:T(8,128)(2,1)}, bf16[256,2048]{1,0:T(8,128)(2,1)}, u32[]{:S(2)}, u32[]{:S(2)}) collective-permute-start(bf16[256,2048]{1,0:T(8,128)(2,1)} %get-tuple-element.237), channel_id=1, source_target_pairs={{0,16},{4,20},{8,24},{12,28},{16,0},{20,4},{24,8},{28,12},{1,17},{... | collective-permute-start | bytes 3145736 | tf_op jit(solution)/shard_map/ppermute | solution.py:1288
  582.2 73.2 %collective-permute-start.34 = (bf16[512,2048]{1,0:T(8,128)(2,1)}, bf16[512,2048]{1,0:T(8,128)(2,1)S(1)}, u32[]{:S(2)}, u32[]{:S(2)}) collective-permute-start(bf16[512,2048]{1,0:T(8,128)(2,1)} %get-tuple-element.269.refs_0_), channel_id=1, source_target_pairs={{0,8},{4,12},{8,0},{12,4},{16,24},{20,28},{24,16},{28,20},{1,9},{5... | collective-permute-start | bytes 6291464 | tf_op jit(solution)/shard_map/ppermute | solution.py:1288
  587.0 68.5 %collective-permute-start.35 = (bf16[512,2048]{1,0:T(8,128)(2,1)}, bf16[512,2048]{1,0:T(8,128)(2,1)S(1)}, u32[]{:S(2)}, u32[]{:S(2)}) collective-permute-start(bf16[512,2048]{1,0:T(8,128)(2,1)} %get-tuple-element.270.refs_2_), channel_id=1, source_target_pairs={{0,16},{4,20},{8,24},{12,28},{16,0},{20,4},{24,8},{28,12},{1,17},{... | collective-permute-start | bytes 6291464 | tf_op jit(solution)/shard_map/ppermute | solution.py:1288
  627.4 37.8 %collective-permute-start.33 = (bf16[256,2048]{1,0:T(8,128)(2,1)}, bf16[256,2048]{1,0:T(8,128)(2,1)S(1)}, u32[]{:S(2)}, u32[]{:S(2)}) collective-permute-start(bf16[256,2048]{1,0:T(8,128)(2,1)} %get-tuple-element.268), channel_id=1, source_target_pairs={{0,1},{1,2},{2,3},{3,0},{4,5},{5,6},{6,7},{7,4},{8,9},{9,10},{10,1... | collective-permute-start | bytes 3145736 | tf_op jit(solution)/shard_map/ppermute | solution.py:1255
  670.0 38.6 %collective-permute-start.38 = (bf16[256,2048]{1,0:T(8,128)(2,1)}, bf16[256,2048]{1,0:T(8,128)(2,1)S(1)}, u32[]{:S(2)}, u32[]{:S(2)}) collective-permute-start(bf16[256,2048]{1,0:T(8,128)(2,1)} %get-tuple-element.281), channel_id=1, source_target_pairs={{0,1},{1,2},{2,3},{3,0},{4,5},{5,6},{6,7},{7,4},{8,9},{9,10},{10,1... | collective-permute-start | bytes 3145736 | tf_op jit(solution)/shard_map/ppermute | solution.py:1255
  671.7 32.4 %collective-permute-start.40 = (bf16[128,2048]{1,0:T(8,128)(2,1)S(1)}, bf16[128,2048]{1,0:T(8,128)(2,1)}, u32[]{:S(2)}, u32[]{:S(2)}) collective-permute-start(bf16[128,2048]{1,0:T(8,128)(2,1)S(1)} %copy-done.40), channel_id=1, source_target_pairs={{0,16},{4,20},{8,24},{12,28},{16,0},{20,4},{24,8},{28,12},{1,17},{... | collective-permute-start | bytes 1572872 | tf_op jit(solution)/shard_map/ppermute | solution.py:1288
  672.7 33.6 %collective-permute-start.41 = (bf16[128,2048]{1,0:T(8,128)(2,1)}, bf16[128,2048]{1,0:T(8,128)(2,1)}, u32[]{:S(2)}, u32[]{:S(2)}) collective-permute-start(bf16[128,2048]{1,0:T(8,128)(2,1)} %get-tuple-element.292.refs_0_), channel_id=1, source_target_pairs={{0,8},{4,12},{8,0},{12,4},{16,24},{20,28},{24,16},{28,20},{1,9},{5... | collective-permute-start | bytes 1572872 | tf_op jit(solution)/shard_map/ppermute | solution.py:1288
  715.6 28.0 %collective-permute-start.45 = (bf16[256,2048]{1,0:T(8,128)(2,1)S(1)}, bf16[256,2048]{1,0:T(8,128)(2,1)}, u32[]{:S(2)}, u32[]{:S(2)}) collective-permute-start(bf16[256,2048]{1,0:T(8,128)(2,1)S(1)} %copy-done.28), channel_id=1, source_target_pairs={{0,16},{4,20},{8,24},{12,28},{16,0},{20,4},{24,8},{28,12},{1,17},{... | collective-permute-start | bytes 3145736 | tf_op jit(solution)/shard_map/ppermute | solution.py:1288
  716.6 33.4 %collective-permute-start.42 = (bf16[256,2048]{1,0:T(8,128)(2,1)}, bf16[256,2048]{1,0:T(8,128)(2,1)S(1)}, u32[]{:S(2)}, u32[]{:S(2)}) collective-permute-start(bf16[256,2048]{1,0:T(8,128)(2,1)} %get-tuple-element.294), channel_id=1, source_target_pairs={{0,1},{1,2},{2,3},{3,0},{4,5},{5,6},{6,7},{7,4},{8,9},{9,10},{10,1... | collective-permute-start | bytes 3145736 | tf_op jit(solution)/shard_map/ppermute | solution.py:1255
  742.6 37.1 %collective-permute-start.46 = (bf16[128,2048]{1,0:T(8,128)(2,1)}, bf16[128,2048]{1,0:T(8,128)(2,1)}, u32[]{:S(2)}, u32[]{:S(2)}) collective-permute-start(bf16[128,2048]{1,0:T(8,128)(2,1)} %get-tuple-element.309), channel_id=1, source_target_pairs={{0,16},{4,20},{8,24},{12,28},{16,0},{20,4},{24,8},{28,12},{1,17},{... | collective-permute-start | bytes 1572872 | tf_op jit(solution)/shard_map/ppermute | solution.py:1288
  746.9 37.3 %collective-permute-start.49 = (bf16[128,2048]{1,0:T(8,128)(2,1)}, bf16[128,2048]{1,0:T(8,128)(2,1)S(1)}, u32[]{:S(2)}, u32[]{:S(2)}) collective-permute-start(bf16[128,2048]{1,0:T(8,128)(2,1)} %get-tuple-element.319), channel_id=1, source_target_pairs={{0,8},{4,12},{8,0},{12,4},{16,24},{20,28},{24,16},{28,20},{1,9},{5... | collective-permute-start | bytes 1572872 | tf_op jit(solution)/shard_map/ppermute | solution.py:1288
  747.8 64.6 %collective-permute-start.54 = (bf16[256,2048]{1,0:T(8,128)(2,1)}, bf16[256,2048]{1,0:T(8,128)(2,1)S(1)}, u32[]{:S(2)}, u32[]{:S(2)}) collective-permute-start(bf16[256,2048]{1,0:T(8,128)(2,1)} %get-tuple-element.327.refs_0_), channel_id=1, source_target_pairs={{0,8},{4,12},{8,0},{12,4},{16,24},{20,28},{24,16},{28,20},{1,9},{5... | collective-permute-start | bytes 3145736 | tf_op jit(solution)/shard_map/ppermute | solution.py:1288
  749.0 63.4 %collective-permute-start.55 = (bf16[256,2048]{1,0:T(8,128)(2,1)}, bf16[256,2048]{1,0:T(8,128)(2,1)}, u32[]{:S(2)}, u32[]{:S(2)}) collective-permute-start(bf16[256,2048]{1,0:T(8,128)(2,1)} %get-tuple-element.328.refs_2_), channel_id=1, source_target_pairs={{0,16},{4,20},{8,24},{12,28},{16,0},{20,4},{24,8},{28,12},{1,17},{... | collective-permute-start | bytes 3145736 | tf_op jit(solution)/shard_map/ppermute | solution.py:1288
  818.0 29.6 %collective-permute-start.50 = (bf16[256,2048]{1,0:T(8,128)(2,1)S(1)}, bf16[256,2048]{1,0:T(8,128)(2,1)S(1)}, u32[]{:S(2)}, u32[]{:S(2)}) collective-permute-start(bf16[256,2048]{1,0:T(8,128)(2,1)S(1)} %copy-done.19), channel_id=1, source_target_pairs={{0,8},{4,12},{8,0},{12,4},{16,24},{20,28},{24,16},{28,20},{1,9},{5... | collective-permute-start | bytes 3145736 | tf_op jit(solution)/shard_map/ppermute | solution.py:1288
  819.0 28.6 %collective-permute-start.52 = (bf16[256,2048]{1,0:T(8,128)(2,1)S(1)}, bf16[256,2048]{1,0:T(8,128)(2,1)}, u32[]{:S(2)}, u32[]{:S(2)}) collective-permute-start(bf16[256,2048]{1,0:T(8,128)(2,1)S(1)} %copy-done.20), channel_id=1, source_target_pairs={{0,16},{4,20},{8,24},{12,28},{16,0},{20,4},{24,8},{28,12},{1,17},{... | collective-permute-start | bytes 3145736 | tf_op jit(solution)/shard_map/ppermute | solution.py:1288
  (96 other events, 937.6 us)
Sparse Core Ops, SparseCore 0:
  10.5 48.2 all-gather.4
  61.2 54.3 all-gather.6
  118.1 89.8 all-gather.8
  209.8 54.3 all-gather.10
